TPU v7x, 32 devices: a whole 2x2x4 slice. The times are simulated.
32 devices in a mesh: seq: 8 (over z, core), mp: 4 (over y, x).
Axes of the slice: x: 2, y: 2, z: 4, core: 2. Of those that a mesh axis runs over, the one named last changes fastest.
Arguments:
- inputs: bfloat16 [4, 4096, 1536], P(None, 'seq', 'mp'), may hold values from -6 to 6
- cotangent: bfloat16 [4, 4096, 1536], P(None, 'seq', 'mp'), may hold values from -6 to 6
- mixer_gain: bfloat16 [1536], replicated, may hold values from 0.099609375 to 1.8984375
- in_weight: bfloat16 [1536, 3, 1536], P(None, None, 'mp'), may hold values from -0.15625 to 0.15625
- in_entry: bfloat16 [1536, 128], P('mp'), may hold values from -0.15625 to 0.15625
- in_exit: bfloat16 [128, 3, 1536], P(None, None, 'mp'), may hold values from -0.75 to 0.75
- conv_weight: bfloat16 [3, 1536], P(None, 'mp'), may hold values from -3.5 to 3.5
- out_weight: bfloat16 [1536, 1536], P('mp'), may hold values from -0.15625 to 0.15625
- out_entry: bfloat16 [1536, 128], P('mp'), may hold values from -0.15625 to 0.15625
- out_exit: bfloat16 [128, 1536], P(None, 'mp'), may hold values from -0.75 to 0.75
- ffn_gain: bfloat16 [1536], replicated, may hold values from 0.099609375 to 1.8984375
- gate_weight: bfloat16 [1536, 6912], P(None, 'mp'), may hold values from -0.15625 to 0.15625
- gate_entry: bfloat16 [1536, 128], P('mp'), may hold values from -0.15625 to 0.15625
- gate_exit: bfloat16 [128, 6912], P(None, 'mp'), may hold values from -0.75 to 0.75
- up_weight: bfloat16 [1536, 6912], P(None, 'mp'), may hold values from -0.15625 to 0.15625
- up_entry: bfloat16 [1536, 128], P('mp'), may hold values from -0.15625 to 0.15625
- up_exit: bfloat16 [128, 6912], P(None, 'mp'), may hold values from -0.75 to 0.75
- down_weight: bfloat16 [6912, 1536], P('mp'), may hold values from -0.078125 to 0.078125
- down_entry: bfloat16 [6912, 128], P('mp'), may hold values from -0.078125 to 0.078125
- down_exit: bfloat16 [128, 1536], P(None, 'mp'), may hold values from -0.75 to 0.75
- doc_starts: int32 [4, 8], replicated, may hold values from 0 to 4095, as said below
- adapter_ids: int32 [4, 8], replicated, may hold values from 0 to 7
Outputs:
- output: bfloat16 [4, 4096, 1536], P(None, 'seq', 'mp')
- input_grad: float32 [4, 4096, 1536], P(None, 'seq', 'mp')
- in_entry_grad: float32 [1536, 128], P('mp')
- in_exit_grad: float32 [128, 3, 1536], P(None, None, 'mp')
- out_entry_grad: float32 [1536, 128], P('mp')
- out_exit_grad: float32 [128, 1536], P(None, 'mp')
- gate_entry_grad: float32 [1536, 128], P('mp')
- gate_exit_grad: float32 [128, 6912], P(None, 'mp')
- up_entry_gradient: float32 [1536, 128], P('mp')
- up_exit_grad: float32 [128, 6912], P(None, 'mp')
- down_entry_grad: float32 [6912, 128], P('mp')
- down_exit_grad: float32 [128, 1536], P(None, 'mp')
Inputs may be any that keep to these rules, and one draw needn't show every extreme that they name: `doc_starts`: each row begins with 0 and rises strictly; a document runs from its start to the next start or to its sequence's end.
All inputs are finite; a program needn't handle non-finite values.
Results may differ from a plain program's by a relative error of at most 0.017.
Values may be sent and summed in bfloat16 or wider, within the bound.
No kernel may reach another device: no remote copies, remote signals or barrier semaphores. Data moves between devices by JAX's collectives and lax.ppermute only.
A program may use at most 256 MiB of HBM per device.

v0:
```python
import jax
import jax.numpy as jnp
from jax import lax
from jax.sharding import PartitionSpec as P

RANK = 16
ADAPT = 8
NDOC = 8


EPS = 1e-05


def from_behind(x, axis, by):
    count = lax.axis_size(axis)
    pairs = [(i, i + by) for i in range(count) if 0 <= i + by < count]
    return lax.ppermute(x, axis, pairs)


def contract(left, right, left_dim, right_extent):
    return lax.dot_general(
        left, right, (((left_dim,), (right_extent,)), ((), ())), preferred_element_type=jnp.float32
    )


def row_total(values):
    return lax.psum(jnp.sum(values, axis=-1), "mp")


def mid_total(parts):
    return lax.psum(parts, "mp")


def share_total(partial_value):
    return lax.psum_scatter(partial_value, "mp", scatter_dimension=1, tiled=True)


def column_products(share, weights):
    piece = lax.all_gather(share, "mp", axis=1, tiled=True)
    return tuple((jnp.dot(piece, weight, preferred_element_type=jnp.float32) for weight in weights))


def row_products(share, weight):
    return contract(lax.all_gather(share, "mp", axis=1, tiled=True), weight, 1, 1)


def doc_tables(starts, ids, length, offset):
    position = offset + jnp.arange(length, dtype=jnp.int32)
    begins = jnp.any(starts[:, :, None] == position[None, None, :], axis=1).astype(jnp.float32)
    earlier = jnp.any(starts[:, :, None] == position[None, None, :] - 1, axis=1).astype(jnp.float32)
    prev_one = 1.0 - begins
    prev_two = prev_one * (1.0 - earlier)
    segment = jnp.sum((starts[:, :, None] <= position[None, None, :]).astype(jnp.int32), axis=1) - 1
    document_onehot = (
        segment[:, :, None] == jnp.arange(NDOC, dtype=jnp.int32)[None, None, :]
    ).astype(jnp.float32)
    adapter_onehot = (ids[:, :, None] == jnp.arange(ADAPT, dtype=jnp.int32)[None, None, :]).astype(
        jnp.float32
    )
    token_onehot = jnp.einsum("cxn,cnt->cxt", document_onehot, adapter_onehot)
    select = jnp.repeat(token_onehot, RANK, axis=2).reshape(-1, ADAPT * RANK)
    return (prev_one, prev_two, select.astype(jnp.bfloat16))


def local(
    inputs,
    cotangent,
    mixer_gain,
    in_weight,
    in_entry,
    in_exit,
    conv_weight,
    out_weight,
    out_entry,
    out_exit,
    ffn_gain,
    gate_weight,
    gate_entry,
    gate_exit,
    up_weight,
    up_entry,
    up_exit,
    down_weight,
    down_entry,
    down_exit,
    doc_starts,
    adapter_ids,
):
    seq_count, length, width_share = inputs.shape
    tokens = seq_count * length
    width = width_share * lax.axis_size("mp")
    column = lax.axis_index("mp") * width_share
    prev_one, prev_two, select = doc_tables(
        doc_starts, adapter_ids, length, lax.axis_index("seq") * length
    )
    mixer_share = lax.dynamic_slice_in_dim(mixer_gain, column, width_share, 0).astype(jnp.float32)
    ffn_full = ffn_gain.astype(jnp.float32)
    ffn_share = lax.dynamic_slice_in_dim(ffn_full, column, width_share, 0)
    residual = inputs.reshape(tokens, width_share).astype(jnp.float32)
    scale_one = lax.rsqrt(row_total(residual * residual) / width + EPS)
    normed = (residual * scale_one[:, None] * mixer_share).astype(jnp.bfloat16)
    in_flat = in_weight.reshape(width, 3 * width_share)
    exit_flat = in_exit.reshape(in_exit.shape[0], 3 * width_share)
    inner_in = mid_total((jnp.dot(normed, in_entry, preferred_element_type=jnp.float32),))[0]
    low_in = inner_in.astype(jnp.bfloat16) * select
    project = column_products(normed, (in_flat,))[0] + jnp.dot(
        low_in, exit_flat, preferred_element_type=jnp.float32
    )
    parts = project.reshape(seq_count, length, 3, width_share)
    input_gate = parts[:, :, 0]
    output_gate = parts[:, :, 1]
    values = parts[:, :, 2]
    mixed = input_gate * values
    edge = from_behind(mixed[:, length - 2 :], "seq", 1)
    extended = jnp.concatenate([edge, mixed], 1)
    taps = conv_weight.astype(jnp.float32)
    filtered = (
        taps[2] * mixed
        + taps[1] * prev_one[..., None] * extended[:, 1 : length + 1]
        + taps[0] * prev_two[..., None] * extended[:, :length]
    )
    gated = (output_gate * filtered).astype(jnp.bfloat16).reshape(tokens, width_share)
    inner_out = mid_total((jnp.dot(gated, out_entry, preferred_element_type=jnp.float32),))[0]
    low_out = inner_out.astype(jnp.bfloat16) * select
    branch_tail = jnp.dot(low_out, out_exit, preferred_element_type=jnp.float32)
    partial_value = jnp.dot(gated, out_weight, preferred_element_type=jnp.float32)
    own = lax.dynamic_slice_in_dim(partial_value, column, width_share, 1) + residual + branch_tail
    rows_total = lax.psum(lax.dynamic_update_slice_in_dim(partial_value, own, column, 1), "mp")
    hidden = lax.dynamic_slice_in_dim(rows_total, column, width_share, 1)
    scale_two = lax.rsqrt(jnp.sum(rows_total * rows_total, axis=1) / width + EPS)
    normed_full = (rows_total * scale_two[:, None] * ffn_full).astype(jnp.bfloat16)
    normed_two = lax.dynamic_slice_in_dim(normed_full, column, width_share, 1)
    gate = jnp.dot(normed_full, gate_weight, preferred_element_type=jnp.float32)
    up = jnp.dot(normed_full, up_weight, preferred_element_type=jnp.float32)
    inner_gate, inner_up = mid_total(
        (
            jnp.dot(normed_two, gate_entry, preferred_element_type=jnp.float32),
            jnp.dot(normed_two, up_entry, preferred_element_type=jnp.float32),
        )
    )
    low_gate = inner_gate.astype(jnp.bfloat16) * select
    low_up = inner_up.astype(jnp.bfloat16) * select
    gate = gate + jnp.dot(low_gate, gate_exit, preferred_element_type=jnp.float32)
    up = up + jnp.dot(low_up, up_exit, preferred_element_type=jnp.float32)
    sigma = jax.nn.sigmoid(gate)
    swish = gate * sigma
    activated = (swish * up).astype(jnp.bfloat16)
    inner_down = mid_total((jnp.dot(activated, down_entry, preferred_element_type=jnp.float32),))[0]
    low_down = inner_down.astype(jnp.bfloat16) * select
    outcome = (
        hidden
        + share_total(jnp.dot(activated, down_weight, preferred_element_type=jnp.float32))
        + jnp.dot(low_down, down_exit, preferred_element_type=jnp.float32)
    )
    output = outcome.astype(jnp.bfloat16).reshape(seq_count, length, width_share)
    grad_hidden = cotangent.reshape(tokens, width_share).astype(jnp.float32)
    grad_down = grad_hidden.astype(jnp.bfloat16)
    grad_act = row_products(grad_down, down_weight)
    back_down = mid_total((contract(grad_down, down_exit, 1, 1),))[0]
    low_back_down = back_down.astype(jnp.bfloat16) * select
    grad_act = grad_act + contract(low_back_down, down_entry, 1, 1)
    down_entry_grad = contract(activated, low_back_down, 0, 0)
    down_exit_grad = contract(low_down, grad_down, 0, 0)
    up_projection_gradient = (grad_act * swish).astype(jnp.bfloat16)
    grad_gate = (grad_act * up * sigma * (1.0 + gate * (1.0 - sigma))).astype(jnp.bfloat16)
    back_gate, back_up = mid_total(
        (contract(grad_gate, gate_exit, 1, 1), contract(up_projection_gradient, up_exit, 1, 1))
    )
    low_back_gate = back_gate.astype(jnp.bfloat16) * select
    low_back_up = back_up.astype(jnp.bfloat16) * select
    grad_normed_two = share_total(
        contract(grad_gate, gate_weight, 1, 1) + contract(up_projection_gradient, up_weight, 1, 1)
    )
    grad_normed_two = (
        grad_normed_two
        + contract(low_back_gate, gate_entry, 1, 1)
        + contract(low_back_up, up_entry, 1, 1)
    )
    gate_entry_grad = contract(normed_two, low_back_gate, 0, 0)
    gate_exit_grad = contract(low_gate, grad_gate, 0, 0)
    up_entry_gradient = contract(normed_two, low_back_up, 0, 0)
    up_exit_grad = contract(low_up, up_projection_gradient, 0, 0)
    weighted_two = grad_normed_two * ffn_share
    cube_two = scale_two * scale_two * scale_two
    grad_hidden = (
        grad_hidden
        + scale_two[:, None] * weighted_two
        - hidden * (cube_two * row_total(weighted_two * hidden) / width)[:, None]
    )
    grad_branch = grad_hidden.astype(jnp.bfloat16)
    grad_gated = row_products(grad_branch, out_weight)
    back_out = mid_total((contract(grad_branch, out_exit, 1, 1),))[0]
    low_back_out = back_out.astype(jnp.bfloat16) * select
    grad_gated = grad_gated + contract(low_back_out, out_entry, 1, 1)
    out_entry_grad = contract(gated, low_back_out, 0, 0)
    out_exit_grad = contract(low_out, grad_branch, 0, 0)
    grad_gated = grad_gated.reshape(seq_count, length, width_share)
    grad_output_gate = grad_gated * filtered
    grad_filtered = grad_gated * output_gate
    near = taps[1] * prev_one[..., None] * grad_filtered
    far = taps[0] * prev_two[..., None] * grad_filtered
    sent = jnp.concatenate([far[:, :1], near[:, :1] + far[:, 1:2]], 1)
    came = from_behind(sent, "seq", -1)
    zero_one = jnp.zeros((seq_count, 1, width_share), jnp.float32)
    zero_two = jnp.zeros((seq_count, 2, width_share), jnp.float32)
    spacer = jnp.zeros((seq_count, length - 2, width_share), jnp.float32)
    grad_mixed = (
        taps[2] * grad_filtered
        + jnp.concatenate([near[:, 1:], zero_one], 1)
        + jnp.concatenate([far[:, 2:], zero_two], 1)
        + jnp.concatenate([spacer, came], 1)
    )
    grad_project = (
        jnp.stack([grad_mixed * values, grad_output_gate, grad_mixed * input_gate], 2)
        .reshape(tokens, 3 * width_share)
        .astype(jnp.bfloat16)
    )
    back_in = mid_total((contract(grad_project, exit_flat, 1, 1),))[0]
    low_back_in = back_in.astype(jnp.bfloat16) * select
    grad_normed = share_total(contract(grad_project, in_flat, 1, 1)) + contract(
        low_back_in, in_entry, 1, 1
    )
    in_entry_grad = contract(normed, low_back_in, 0, 0)
    in_exit_grad = contract(low_in, grad_project, 0, 0).reshape(in_exit.shape)
    weighted_one = grad_normed * mixer_share
    cube_one = scale_one * scale_one * scale_one
    grad_inputs = (
        grad_hidden
        + scale_one[:, None] * weighted_one
        - residual * (cube_one * row_total(weighted_one * residual) / width)[:, None]
    )
    summed = (
        lax.psum(in_entry_grad.astype(jnp.bfloat16), "seq").astype(jnp.float32),
        lax.psum(in_exit_grad.astype(jnp.bfloat16), "seq").astype(jnp.float32),
        lax.psum(out_entry_grad.astype(jnp.bfloat16), "seq").astype(jnp.float32),
        lax.psum(out_exit_grad.astype(jnp.bfloat16), "seq").astype(jnp.float32),
        lax.psum(gate_entry_grad.astype(jnp.bfloat16), "seq").astype(jnp.float32),
        lax.psum(gate_exit_grad.astype(jnp.bfloat16), "seq").astype(jnp.float32),
        lax.psum(up_entry_gradient.astype(jnp.bfloat16), "seq").astype(jnp.float32),
        lax.psum(up_exit_grad.astype(jnp.bfloat16), "seq").astype(jnp.float32),
        lax.psum(down_entry_grad.astype(jnp.bfloat16), "seq").astype(jnp.float32),
        lax.psum(down_exit_grad.astype(jnp.bfloat16), "seq").astype(jnp.float32),
    )
    return (
        output,
        grad_inputs.reshape(seq_count, length, width_share),
        summed[0],
        summed[1],
        summed[2],
        summed[3],
        summed[4],
        summed[5],
        summed[6],
        summed[7],
        summed[8],
        summed[9],
    )


def solution(mesh):
    return jax.shard_map(
        local,
        mesh=mesh,
        in_specs=(
            P(None, "seq", "mp"),
            P(None, "seq", "mp"),
            P(),
            P(None, None, "mp"),
            P("mp", None),
            P(None, None, "mp"),
            P(None, "mp"),
            P("mp", None),
            P("mp", None),
            P(None, "mp"),
            P(),
            P(None, "mp"),
            P("mp", None),
            P(None, "mp"),
            P(None, "mp"),
            P("mp", None),
            P(None, "mp"),
            P("mp", None),
            P("mp", None),
            P(None, "mp"),
            P(),
            P(),
        ),
        out_specs=(
            P(None, "seq", "mp"),
            P(None, "seq", "mp"),
            P("mp", None),
            P(None, None, "mp"),
            P("mp", None),
            P(None, "mp"),
            P("mp", None),
            P(None, "mp"),
            P("mp", None),
            P(None, "mp"),
            P("mp", None),
            P(None, "mp"),
        ),
        check_vma=False,
    )
```

profile of v0, /device:TPU:0, one launch (start us, length us, event | category | flops | bytes accessed | tf_op | source)
XLA Modules:
  0.0 1486.5 jit_solution(6568678228321926032)
XLA Ops:
  9.1 11.5 psum.168
  36.0 67.0 %all-reduce.20 = bf16[2048,128]{1,0:T(8,128)(2,1)S(1)} all-reduce(f32[2048,128]{1,0:T(8,128)S(1)} %copy-done.23), channel_id=1, replica_groups=mesh['seq'=8,'mp'=4] {'mp'}, use_global_device_ids=true, to_apply=%region_2.0 | all-reduce | flops 262144 | bytes 1572864 | tf_op jit(solution)/shard_map/psum | solution.py:31
  103.0 17.8 %all-gather.4.cloned.1.call-done = bf16[2048,1536]{1,0:T(8,128)(2,1)} async-done(((bf16[2048,384]{1,0:T(8,128)(2,1)}), bf16[2048,1536]{1,0:T(8,128)(2,1)}) %all-gather.4.cloned.1.call-update) | async-done | bytes 6291472 | tf_op jit(solution)/shard_map/all_gather | solution.py:39
  120.8 11.5 fusion.34
  137.4 9.6 copy.82
  147.0 12.3 reshape.108
  168.8 10.5 multiply_convert_fusion.4
  181.8 47.9 %all-reduce.21 = bf16[2048,128]{1,0:T(8,128)(2,1)} all-reduce(f32[2048,128]{1,0:T(8,128)} %fusion.37), channel_id=1, replica_groups=mesh['seq'=8,'mp'=4] {'mp'}, use_global_device_ids=true, to_apply=%region_6.0 | all-reduce | flops 262144 | bytes 1572864 | tf_op jit(solution)/shard_map/psum | solution.py:31
  244.1 18.2 %fusion.42 = f32[2048,1728]{0,1:T(8,128)} fusion(bf16[2048,1536]{1,0:T(8,128)(2,1)} %all-gather.6.cloned.1.call-done, bf16[1728,1536]{1,0:T(8,128)(2,1)} %param.39), kind=kOutput, calls=%fused_computation.119 | convolution fusion | flops 10871635968 | bytes 25755648 | tf_op jit(solution)/shard_map/dot_general | solution.py:21
  262.3 217.2 %all-reduce.17.cloned.1.call-done = f32[2048,1536]{1,0:T(8,128)} async-done(((f32[2048,1536]{1,0:T(8,128)}), f32[2048,1536]{1,0:T(8,128)}) %all-reduce.17.cloned.1.call-update) | async-done | bytes 12582928 | tf_op jit(solution)/shard_map/psum | solution.py:128
  485.6 8.4 multiply_convert_fusion.3
  500.2 17.2 %fusion.39 = f32[2048,1728]{0,1:T(8,128)} fusion(bf16[2048,1536]{1,0:T(8,128)(2,1)} %multiply_convert_fusion.3, bf16[1536,1728]{0,1:T(8,128)(2,1)} %param.36), kind=kOutput, calls=%fused_computation.116 | convolution fusion | flops 10871635968 | bytes 25755648 | tf_op jit(solution)/shard_map/dot_general | solution.py:134
  517.4 13.7 fusion.38
  531.0 118.6 %all-reduce.22 = (bf16[2048,128]{1,0:T(8,128)(2,1)}, bf16[2048,128]{1,0:T(8,128)(2,1)}, bf16[2048,128]{1,0:T(8,128)(2,1)}) all-reduce(f32[2048,128]{1,0:T(8,128)} %fusion.15, f32[2048,128]{1,0:T(8,128)} %fusion.17, f32[2048,128]{1,0:T(8,128)} %fusion.43), channel_id=1, replica_groups=mesh['seq'=8,'mp'=4] {'mp'}, use_global_device_ids=true, to_apply=%region_10.0 | all-reduce | flops 786432 | bytes 4718592 | tf_op jit(solution)/shard_map/psum | solution.py:31
  649.6 13.0 convolution_add_fusion.2
  662.7 7.0 convolution_add_fusion.3
  669.7 24.8 %multiply_convert_fusion = (bf16[2048,1728]{0,1:T(8,128)(2,1)}, bf16[2048,1728]{0,1:T(8,128)(2,1)}, bf16[2048,1728]{0,1:T(8,128)(2,1)}) fusion(f32[2048,1728]{0,1:T(8,128)} %convolution_add_fusion.3, f32[2048,1728]{0,1:T(8,128)} %convolution_add_fusion.2, f32[2048,1728]{0,1:T(8,128)} %fusion.42, bf16[1728,128]{1,0:T(8,128)(2,1)} %param.40, ...), kind=kOutput, calls=%fused_computation | convolution fusion | flops 962854912 | bytes 65191936 | tf_op jit(solution)/shard_map/dot_general | solution.py:21
  694.5 18.0 %fusion.44 = f32[2048,1536]{1,0:T(8,128)} fusion(bf16[2048,1728]{0,1:T(8,128)(2,1)} %get-tuple-element.39, bf16[1536,1728]{0,1:T(8,128)(2,1)} %param.33), kind=kOutput, calls=%fused_computation.121 | convolution fusion | flops 10871635968 | bytes 24969216 | tf_op jit(solution)/shard_map/dot_general | solution.py:21
  712.5 18.0 %convolution_add_fusion.4 = f32[2048,1536]{1,0:T(8,128)} fusion(f32[2048,1536]{1,0:T(8,128)} %fusion.44, bf16[2048,1728]{0,1:T(8,128)(2,1)S(1)} %copy-done.15, bf16[1536,1728]{0,1:T(8,128)(2,1)} %param.36), kind=kOutput, calls=%fused_computation.12 | convolution fusion | flops 10874781696 | bytes 37552128 | tf_op jit(solution)/shard_map/dot_general | solution.py:21
  740.1 135.7 %all-reduce.23 = (bf16[2048,128]{1,0:T(8,128)(2,1)S(1)}, bf16[2048,128]{1,0:T(8,128)(2,1)}) all-reduce(f32[2048,128]{1,0:T(8,128)S(1)} %fusion.45, f32[2048,128]{1,0:T(8,128)} %fusion.46), channel_id=1, replica_groups=mesh['seq'=8,'mp'=4] {'mp'}, use_global_device_ids=true, to_apply=%region_15.0 | all-reduce | flops 524288 | bytes 3145728 | tf_op jit(solution)/shard_map/psum | solution.py:31
  878.1 34.0 %reduce-scatter.6.cloned.1.call-done = f32[2048,384]{1,0:T(8,128)} async-done(((f32[2048,1536]{1,0:T(8,128)}), f32[2048,384]{1,0:T(8,128)}) %reduce-scatter.6.cloned.1.call-update) | async-done | bytes 3145744 | tf_op jit(solution)/shard_map/reduce_scatter | solution.py:35
  918.8 8.9 psum.178
  935.1 64.8 %all-reduce.24 = bf16[2048,128]{1,0:T(8,128)(2,1)} all-reduce(f32[2048,128]{1,0:T(8,128)} %fusion.48), channel_id=1, replica_groups=mesh['seq'=8,'mp'=4] {'mp'}, use_global_device_ids=true, to_apply=%region_19.0 | all-reduce | flops 262144 | bytes 1572864 | tf_op jit(solution)/shard_map/psum | solution.py:31
  999.8 23.7 %all-gather.8.cloned.1.call-done = bf16[2048,1536]{1,0:T(8,128)(2,1)} async-done(((bf16[2048,384]{1,0:T(8,128)(2,1)}), bf16[2048,1536]{1,0:T(8,128)(2,1)}) %all-gather.8.cloned.1.call-update) | async-done | bytes 6291472 | tf_op jit(solution)/shard_map/all_gather | solution.py:44
  1062.6 8.5 multiply_bitcast_fusion.2
  1082.0 11.2 fusion.49
  1093.3 17.9 %fusion.40 = f32[2048,1536]{1,0:T(8,128)} fusion(bf16[2048,1728]{0,1:T(8,128)(2,1)} %get-tuple-element.40, bf16[1728,1536]{1,0:T(8,128)(2,1)} %param.39), kind=kOutput, calls=%fused_computation.117 | convolution fusion | flops 10871635968 | bytes 24969216 | tf_op jit(solution)/shard_map/dot_general | solution.py:152
  1140.8 67.6 %all-reduce.25 = bf16[2048,128]{1,0:T(8,128)(2,1)} all-reduce(f32[2048,128]{1,0:T(8,128)} %fusion.50), channel_id=1, replica_groups=mesh['seq'=8,'mp'=4] {'mp'}, use_global_device_ids=true, to_apply=%region_21.0 | all-reduce | flops 262144 | bytes 1572864 | tf_op jit(solution)/shard_map/psum | solution.py:31
  1216.6 22.3 %reduce-scatter.8.cloned.1.call-done = f32[2048,384]{1,0:T(8,128)} async-done(((f32[2048,1536]{1,0:T(8,128)}), f32[2048,384]{1,0:T(8,128)}) %reduce-scatter.8.cloned.1.call-update) | async-done | bytes 3145744 | tf_op jit(solution)/shard_map/reduce_scatter | solution.py:35
  1243.9 79.0 %all-reduce.26 = (bf16[2048,128]{1,0:T(8,128)(2,1)}, f32[2048]{0:T(1024)S(1)}) all-reduce(f32[2048,128]{1,0:T(8,128)} %fusion.41, f32[2048]{0:T(1024)S(1)} %get-tuple-element.50), channel_id=1, replica_groups=mesh['seq'=8,'mp'=4] {'mp'}, use_global_device_ids=true, to_apply=%region_12.0 | all-reduce | flops 264192 | bytes 1589248 | tf_op jit(solution)/shard_map/psum | solution.py:31
  1325.0 70.9 %reduce-scatter.4.cloned.1.call-done = f32[2048,384]{1,0:T(8,128)} async-done(((f32[2048,1536]{1,0:T(8,128)}), f32[2048,384]{1,0:T(8,128)}) %reduce-scatter.4.cloned.1.call-update) | async-done | bytes 3145744 | tf_op jit(solution)/shard_map/reduce_scatter | solution.py:35
  1405.6 62.6 %all-reduce.19.cloned.1.call-done = (bf16[384,128]{1,0:T(8,128)(2,1)}, bf16[128,3,384]{2,0,1:T(8,128)(2,1)}, bf16[384,128]{1,0:T(8,128)(2,1)}, bf16[128,384]{1,0...) async-done(((bf16[384,128]{1,0:T(8,128)(2,1)}, ...) | async-done | bytes 2211856 | tf_op jit(solution)/shard_map/psum | solution.py:233
  (303 shorter events, 202.0 us)
Async XLA Ops:
  7.2 222.5 %copy-start = (bf16[384,1536]{1,0:T(8,128)(2,1)S(1)}, bf16[384,1536]{1,0:T(8,128)(2,1)}, u32[]{:S(2)}) copy-start(bf16[384,1536]{1,0:T(8,128)(2,1)} %param.29) | copy-start | bytes 3538948
  7.2 113.6 %all-gather.4.cloned.1.call-start = ((), (), s32[]{:S(2)}) async-start(), calls=%async_computation.3 | async-start | bytes 7864320 | tf_op jit(solution)/shard_map/all_gather | solution.py:39
  24.5 219.6 %all-gather.6.cloned.1.call-start = ((), (), s32[]{:S(2)}) async-start(), calls=%async_computation.6 | async-start | bytes 7864320 | tf_op jit(solution)/shard_map/all_gather | solution.py:44
  25.3 454.2 %all-reduce.17.cloned.1.call-start = ((), (), s32[]{:S(2)}) async-start(), calls=%async_computation.4 | async-start | bytes 25165824 | tf_op jit(solution)/shard_map/psum | solution.py:128
  36.0 132.8 %copy-start.61 = (f32[4,512]{1,0:T(4,128)}, f32[4,512]{1,0:T(4,128)S(1)}, u32[]{:S(2)}) copy-start(f32[4,512]{1,0:T(4,128)S(1)} %get-tuple-element.46) | copy-start | bytes 24580
  36.0 132.8 %copy-start.63 = (f32[4,512]{1,0:T(4,128)}, f32[4,512]{1,0:T(4,128)S(1)}, u32[]{:S(2)}) copy-start(f32[4,512]{1,0:T(4,128)S(1)} %get-tuple-element.47) | copy-start | bytes 24580
  103.0 29.3 %copy-start.19 = (bf16[2048,128]{1,0:T(8,128)(2,1)}, bf16[2048,128]{1,0:T(8,128)(2,1)S(1)}, u32[]{:S(2)}) copy-start(bf16[2048,128]{1,0:T(8,128)(2,1)S(1)} %all-reduce.20) | copy-start | bytes 1572868
  165.6 2.8 collective-permute-start
  179.8 56.4 %copy-start.8 = (bf16[48,8,4,512]{3,1,2,0:T(8,128)(2,1)}, bf16[48,8,4,512]{3,1,2,0:T(8,128)(2,1)S(1)}, u32[]{:S(2)}) copy-start(bf16[48,8,4,512]{3,1,2,0:T(8,128)(2,1)S(1)} %copy.105) | copy-start | bytes 4718596
  241.1 670.9 %reduce-scatter.6.cloned.1.call-start = ((), (), s32[]{:S(2)}) async-start(), calls=%async_computation.7 | async-start | bytes 15728640 | tf_op jit(solution)/shard_map/reduce_scatter | solution.py:35
  493.9 23.4 %slice-start.12 = ((s8[5308416]{0:T(1024)(128)(4,1)}), s8[4194304]{0:T(1024)(128)(4,1)S(1)}, s32[]{:S(2)}) async-start(s8[5308416]{0:T(1024)(128)(4,1)} %bitcast.172), calls=%async_computation.23 | async-start | bytes 8388608
  497.1 20.3 %slice-start.6 = ((s8[6291456]{0:T(1024)(128)(4,1)}), s8[4194304]{0:T(1024)(128)(4,1)S(1)}, s32[]{:S(2)}) async-start(s8[6291456]{0:T(1024)(128)(4,1)} %bitcast.150), calls=%async_computation.17 | async-start | bytes 8388608
  500.2 17.2 %slice-start.7 = ((s8[6291456]{0:T(1024)(128)(4,1)}), s8[2097152]{0:T(1024)(128)(4,1)S(1)}, s32[]{:S(2)}) async-start(s8[6291456]{0:T(1024)(128)(4,1)} %bitcast.150), calls=%async_computation.18 | async-start | bytes 4194304
  500.2 17.2 %slice-start.13 = ((s8[5308416]{0:T(1024)(128)(4,1)}), s8[1114112]{0:T(1024)(128)(4,1)S(1)}, s32[]{:S(2)}) async-start(s8[5308416]{0:T(1024)(128)(4,1)} %bitcast.172), calls=%async_computation.24 | async-start | bytes 2228224
  531.0 131.6 %slice-start = ((s8[14155776]{0:T(1024)(128)(4,1)}), s8[1572864]{0:T(1024)(128)(4,1)S(1)}, s32[]{:S(2)}) async-start(s8[14155776]{0:T(1024)(128)(4,1)} %bitcast.140), calls=%async_computation.11 | async-start | bytes 3145728
  694.5 18.0 %copy-start.15 = (bf16[2048,1728]{0,1:T(8,128)(2,1)S(1)}, bf16[2048,1728]{0,1:T(8,128)(2,1)}, u32[]{:S(2)}) copy-start(bf16[2048,1728]{0,1:T(8,128)(2,1)} %get-tuple-element.38) | copy-start | bytes 21233668
  730.6 292.9 %all-gather.8.cloned.1.call-start = ((), (), s32[]{:S(2)}) async-start(), calls=%async_computation.8 | async-start | bytes 7864320 | tf_op jit(solution)/shard_map/all_gather | solution.py:44
  736.9 138.9 %copy-start.45 = (bf16[384,128]{1,0:T(8,128)(2,1)S(1)}, bf16[384,128]{1,0:T(8,128)(2,1)}, u32[]{:S(2)}) copy-start(bf16[384,128]{1,0:T(8,128)(2,1)} %param.34) | copy-start | bytes 294916
  740.1 171.9 %copy-start.47 = (bf16[384,128]{1,0:T(8,128)(2,1)S(1)}, bf16[384,128]{1,0:T(8,128)(2,1)}, u32[]{:S(2)}) copy-start(bf16[384,128]{1,0:T(8,128)(2,1)} %param.37) | copy-start | bytes 294916
  875.8 36.2 %copy-start.27 = (bf16[2048,128]{1,0:T(8,128)(2,1)}, bf16[2048,128]{1,0:T(8,128)(2,1)S(1)}, u32[]{:S(2)}) copy-start(bf16[2048,128]{1,0:T(8,128)(2,1)S(1)} %get-tuple-element.19) | copy-start | bytes 1572868
  912.0 15.7 %copy-start.3 = (bf16[4,512,384]{2,1,0:T(8,128)(2,1)S(1)}, bf16[4,512,384]{2,1,0:T(8,128)(2,1)}, u32[]{:S(2)}) copy-start(bf16[4,512,384]{2,1,0:T(8,128)(2,1)} %param.23) | copy-start | bytes 4718596
  912.0 15.7 %copy-start.50 = (f32[2048]{0:T(1024)S(1)}, f32[2048]{0:T(1024)}, u32[]{:S(2)}) copy-start(f32[2048]{0:T(1024)} %copy-done.49) | copy-start | bytes 24580
  932.1 306.8 %reduce-scatter.8.cloned.1.call-start = ((), (), s32[]{:S(2)}) async-start(), calls=%async_computation.9 | async-start | bytes 15728640 | tf_op jit(solution)/shard_map/reduce_scatter | solution.py:35
  999.8 29.3 %copy-start.39 = (bf16[384,128]{1,0:T(8,128)(2,1)S(1)}, bf16[384,128]{1,0:T(8,128)(2,1)}, u32[]{:S(2)}) copy-start(bf16[384,128]{1,0:T(8,128)(2,1)} %param.30) | copy-start | bytes 294916
  1051.1 10.2 collective-permute-start.1
  1093.2 302.7 %reduce-scatter.4.cloned.1.call-start = ((), (), s32[]{:S(2)}) async-start(), calls=%async_computation.5 | async-start | bytes 15728640 | tf_op jit(solution)/shard_map/reduce_scatter | solution.py:35
  1111.2 357.0 %all-reduce.19.cloned.1.call-start = ((), (), s32[]{:S(2)}) async-start(), calls=%async_computation.10 | async-start | bytes 4423680 | tf_op jit(solution)/shard_map/psum | solution.py:233
  1211.6 27.3 %copy-start.41 = (bf16[384,128]{1,0:T(8,128)(2,1)S(1)}, bf16[384,128]{1,0:T(8,128)(2,1)}, u32[]{:S(2)}) copy-start(bf16[384,128]{1,0:T(8,128)(2,1)} %param.26) | copy-start | bytes 294916
  1211.6 27.3 %copy-start.74 = (f32[384]{0:T(512)S(1)}, f32[384]{0:T(512)}, u32[]{:S(2)}) copy-start(f32[384]{0:T(512)} %copy-done.73) | copy-start | bytes 4612
  1216.6 106.2 %copy-start.60 = (f32[2048]{0:T(1024)S(1)}, f32[2048]{0:T(1024)}, u32[]{:S(2)}) copy-start(f32[2048]{0:T(1024)} %copy-done.59) | copy-start | bytes 24580
  1243.9 152.1 %copy-start.43 = (bf16[128,384]{1,0:T(8,128)(2,1)S(1)}, bf16[128,384]{1,0:T(8,128)(2,1)}, u32[]{:S(2)}) copy-start(bf16[128,384]{1,0:T(8,128)(2,1)} %param.41) | copy-start | bytes 294916
  1325.0 75.7 %copy-start.58 = (f32[2048]{0:T(1024)S(1)}, f32[2048]{0:T(1024)}, u32[]{:S(2)}) copy-start(f32[2048]{0:T(1024)} %copy-done.57) | copy-start | bytes 24580
  (73 other events, 457.7 us)
Sparse Core Ops, SparseCore 0:
  24.6 96.1 all-gather.3
  122.6 75.2 all-gather.5
  241.2 238.1 all-reduce.16
  730.7 181.2 reduce-scatter.5
  932.2 91.3 all-gather.7
  1093.3 145.5 reduce-scatter.7
  1242.0 153.8 reduce-scatter.3
  1400.3 67.8 all-reduce.18
where the time goes:
time: 1500 us; the launch traced here: 1490 us
  blocking collectives  601 us (40%)
  waiting for transfers between devices  450 us (30%)
  matrix products  276 us (18%)
  other arithmetic  73.4 us (5%)
  local copies, waits for them, and re-layouts  67.3 us (4%)
  between operations  15.4 us (1%)
    psum x7, blocking collectives, mid_total(): return lax.psum(parts, 'mp')  580 us
    psum x1, waiting for transfers between devices, local(): lax.psum(lax.dynamic_update_slice_in_dim(partial_value, own, column, 1),...  217 us
    dot_general x25, matrix products, contract(): lax.dot_general(left, right, (((left_dim,), (right_extent,)), ((), ())),...  158 us
    reduce_scatter x3, waiting for transfers between devices, share_total(): lax.psum_scatter(partial_value, 'mp', scatter_dimension=1, tiled=True)  127 us
    psum x1, waiting for transfers between devices, local(): lax.psum(in_entry_grad.astype(jnp.bfloat16), 'seq').astype(jnp.float32)  62.6 us
  transfers between devices with their start and end apart: 10, of which 8 were waited for; matrix products, arithmetic and copies ran while one was open for 13% of the time, Pallas kernels for 0%

commit v1 on v0

--- a/solution.py
+++ b/solution.py
@@ -62,7 +62,7 @@
     return (prev_one, prev_two, select.astype(jnp.bfloat16))
 
 
-def local(
+def general_local(
     inputs,
     cotangent,
     mixer_gain,
@@ -257,9 +257,355 @@
     )
 
 
+def swap(value, axis, bit):
+    return lax.ppermute(value, axis, [(i, i ^ bit) for i in range(lax.axis_size(axis))])
+
+
+def place(relative, me):
+    stacked = jnp.stack(relative)
+    return [lax.dynamic_index_in_dim(stacked, a ^ me, 0, keepdims=False) for a in range(len(relative))]
+
+
+def halves(block, me):
+    rows = block.shape[0] // 2
+    return lax.dynamic_slice_in_dim(block, me * rows, rows, 0)
+
+
+def gather_blocks(block, core):
+    mine = halves(block, core)
+    from_x = swap(mine, "mp", 1)
+    from_y = swap(mine, "mp", 2)
+    cut = (mine.shape[0] // 32) * 16
+    from_g = jnp.concatenate([swap(from_x[:cut], "mp", 2), swap(from_y[cut:], "mp", 1)], 0)
+    full = [block]
+    for piece in (from_x, from_y, from_g):
+        full.append(jnp.concatenate(place([piece, swap(piece, "seq", 1)], core), 0))
+    return full
+
+
+def fetch_block(block, quarter):
+    rows = block.shape[0] // 4
+    mine = swap(lax.dynamic_slice_in_dim(block, quarter * rows, rows, 0), "mp", 2)
+    over = swap(mine, "seq", 2)
+    both = swap(jnp.stack([mine, over]), "seq", 1)
+    return jnp.concatenate(place([mine, both[0], over, both[1]], quarter), 0)
+
+
+def dot(left, right):
+    return jnp.dot(left, right, preferred_element_type=jnp.float32)
+
+
+def low(value):
+    return value.astype(jnp.bfloat16)
+
+
+def fast_local(
+    inputs,
+    cotangent,
+    mixer_gain,
+    in_weight,
+    in_entry,
+    in_exit,
+    conv_weight,
+    out_weight,
+    out_entry,
+    out_exit,
+    ffn_gain,
+    gate_weight,
+    gate_entry,
+    gate_exit,
+    up_weight,
+    up_entry,
+    up_exit,
+    down_weight,
+    down_entry,
+    down_exit,
+    doc_starts,
+    adapter_ids,
+):
+    seqs, length, share = inputs.shape
+    width = 4 * share
+    rank = in_entry.shape[1]
+    hidden_share = gate_weight.shape[1]
+    m = lax.axis_index("mp")
+    s = lax.axis_index("seq")
+    x, y, core, quarter = m % 2, m // 2, s % 2, s % 4
+    halo = 16
+
+    edge = from_behind(inputs[:, length - 2 :], "seq", 1)
+    extended = jnp.concatenate([jnp.zeros((seqs, halo - 2, share), inputs.dtype), edge, inputs], 1)
+
+    def block_for(r):
+        return lax.dynamic_index_in_dim(extended, m ^ r, 0, keepdims=False)
+
+    tokens_ext = jnp.concatenate(
+        place([block_for(0)] + [swap(block_for(r), "mp", r) for r in (1, 2, 3)], m), 1
+    )
+    in_flat = in_weight.reshape(width, 3 * share)
+    in_blocks = gather_blocks(in_flat, core)
+    exits = jnp.concatenate(
+        [
+            jnp.concatenate([in_exit.reshape(rank, 3 * share), out_exit, down_exit], 1),
+            jnp.pad(conv_weight, ((0, 29), (0, 4 * share))),
+        ],
+        0,
+    )
+    exit_blocks = gather_blocks(exits, core)
+    entries = jnp.concatenate([in_entry, out_entry, gate_entry, up_entry], 1)
+    entry_blocks = gather_blocks(entries, core)
+    out_blocks = gather_blocks(out_weight, core)
+    entry_full = jnp.concatenate(place(entry_blocks, m), 0)
+    in_entry_full, out_entry_full, gate_entry_full, up_entry_full = (
+        entry_full[:, i * rank : (i + 1) * rank] for i in range(4)
+    )
+    out_exit_full = jnp.concatenate(place([b[:rank, 3 * share : 4 * share] for b in exit_blocks], m), 1)
+    down_exit_full = jnp.concatenate(place([b[:rank, 4 * share :] for b in exit_blocks], m), 1)
+    in_exit_blocks = [b[:rank, : 3 * share] for b in exit_blocks]
+    tap_blocks = [b[rank : rank + 3, :share].astype(jnp.float32) for b in exit_blocks]
+
+    row_of = lax.dynamic_slice_in_dim(cotangent, 2 * y, 2, 0)
+    row_other = lax.dynamic_slice_in_dim(cotangent, 2 - 2 * y, 2, 0)
+    both = jnp.stack([row_of, swap(row_other, "mp", 2)])
+    ct_mine = lax.dynamic_index_in_dim(both, x, 1, keepdims=False)
+    ct_next = lax.dynamic_index_in_dim(both, 1 - x, 1, keepdims=False)
+    got_mine = swap(ct_next, "mp", 1)
+
+    gate_ext = jnp.concatenate([gate_weight, gate_exit], 0)
+    up_ext = jnp.concatenate([up_weight, up_exit], 0)
+    down_ext = jnp.concatenate([down_weight, down_entry], 1)
+    gate_far = fetch_block(gate_ext, quarter)
+    up_far = fetch_block(up_ext, quarter)
+    down_far = fetch_block(down_ext, quarter)
+
+    starts = jnp.stack([doc_starts[m], doc_starts[m ^ 1]])
+    ids = jnp.stack([adapter_ids[m], adapter_ids[m ^ 1]])
+    prev_one, prev_two, select = doc_tables(starts, ids, length, s * length)
+    prev_one, prev_two = prev_one[0][:, None], prev_two[0][:, None]
+    select = select.reshape(2, length, rank)
+    select_ext = jnp.concatenate([jnp.zeros((halo, rank), jnp.bfloat16), select[0]], 0)
+    edge_starts, edge_ids = starts[:1], ids[:1]
+    edge_select = doc_tables(edge_starts, edge_ids, halo, s * length - halo)[2]
+    select_ext = jnp.concatenate([edge_select, select[0]], 0)
+
+    gain_one = mixer_gain.astype(jnp.float32)
+    gain_two = ffn_gain.astype(jnp.float32)
+    residual_ext = tokens_ext.astype(jnp.float32)
+    scale_ext = lax.rsqrt(jnp.sum(residual_ext * residual_ext, 1, keepdims=True) / width + EPS)
+    normed_ext = low(residual_ext * scale_ext * gain_one)
+    residual, scale_one, normed = residual_ext[halo:], scale_ext[halo:], normed_ext[halo:]
+    low_in_ext = low(dot(normed_ext, in_entry_full)) * select_ext
+    low_in = low_in_ext[halo:]
+    kept = []
+    branch = 0.0
+    inner_out = 0.0
+    for r in range(4):
+        project = dot(normed_ext, in_blocks[r]) + dot(low_in_ext, in_exit_blocks[r])
+        input_gate, output_gate, values = (project[:, i * share : (i + 1) * share] for i in range(3))
+        mixed = input_gate * values
+        taps = tap_blocks[r]
+        filtered = (
+            taps[2] * mixed[halo:]
+            + taps[1] * prev_one * mixed[halo - 1 : halo - 1 + length]
+            + taps[0] * prev_two * mixed[halo - 2 : halo - 2 + length]
+        )
+        output_gate = output_gate[halo:]
+        gated = low(output_gate * filtered)
+        kept.append((low(input_gate[halo:]), low(output_gate), low(values[halo:]), low(filtered), gated))
+        branch = branch + dot(gated, out_blocks[r])
+        inner_out = inner_out + dot(gated, entry_blocks[r][:, rank : 2 * rank])
+    low_out = low(inner_out) * select[0]
+    hidden = residual + branch + dot(low_out, out_exit_full)
+    scale_two = lax.rsqrt(jnp.sum(hidden * hidden, 1, keepdims=True) / width + EPS)
+    normed_two = low(hidden * scale_two * gain_two)
+    normed_next = swap(normed_two, "mp", 1)
+    got_next = swap(ct_mine, "mp", 1)
+
+    def rows(first, second):
+        return jnp.concatenate(place([first[0], second[0], first[1], second[1]], m), 1)
+
+    grad_down = [rows(ct_mine, got_mine), rows(ct_next, got_next)]
+
+    seen = [normed_two, normed_next]
+    low_gates, low_ups, low_backs = [], [], []
+    for t in range(2):
+        low_gates.append(low(dot(seen[t], gate_entry_full)) * select[t])
+        low_ups.append(low(dot(seen[t], up_entry_full)) * select[t])
+        low_backs.append(low(contract(grad_down[t], down_exit_full, 1, 1)) * select[t])
+
+    def feed(t, gate_w, up_w, down_w):
+        gate = dot(jnp.concatenate([seen[t], low_gates[t]], 1), gate_w)
+        up = dot(jnp.concatenate([seen[t], low_ups[t]], 1), up_w)
+        sigma = jax.nn.sigmoid(gate)
+        swish = gate * sigma
+        activated = low(swish * up)
+        grad_act = contract(jnp.concatenate([grad_down[t], low_backs[t]], 1), down_w, 1, 1)
+        grad_up = low(grad_act * swish)
+        grad_gate = low(grad_act * up * sigma * (1.0 + gate * (1.0 - sigma)))
+        down = dot(activated, down_w)
+        back = (contract(grad_gate, gate_w, 1, 1), contract(grad_up, up_w, 1, 1))
+        adapters = (
+            contract(low_gates[t], grad_gate, 0, 0),
+            contract(low_ups[t], grad_up, 0, 0),
+            contract(low_backs[t], activated, 0, 0),
+        )
+        return down, back, adapters
+
+    def join(one, two):
+        return jax.tree.map(jnp.add, one, two)
+
+    near = (gate_ext, up_ext, down_ext)
+    far = (gate_far, up_far, down_far)
+    near_mine = feed(0, *near)
+    near_next = feed(1, *near)
+    far_next = feed(1, *far)
+    down_next, back_next = join(near_next[:2], far_next[:2])
+    packed = jnp.concatenate(
+        [
+            low(back_next[0][:, :width] + back_next[1][:, :width]),
+            low(back_next[0][:, width:]),
+            low(back_next[1][:, width:]),
+        ],
+        1,
+    )
+    got_back = swap(packed, "mp", 1).astype(jnp.float32)
+    far_mine = feed(0, *far)
+    down_mine, back_mine = join(near_mine[:2], far_mine[:2])
+    near_grads = join(near_mine[2], near_next[2])
+    far_grads = join(far_mine[2], far_next[2])
+    far_sent = swap(low(jnp.stack(far_grads)), "mp", 2)
+    ffn_grads = jnp.stack(near_grads) + far_sent.astype(jnp.float32)
+
+    inner = low(jnp.stack([down_mine[:, width:], down_next[:, width:]]))
+    inner_got = swap(inner, "mp", 1)
+    inner_down = inner.astype(jnp.float32) + inner_got[::-1].astype(jnp.float32)
+    low_down = low(inner_down) * select
+
+    def quarter_stack(value):
+        return jnp.stack([value[:, i * share : (i + 1) * share] for i in range(4)])
+
+    def take(stack, r):
+        return lax.dynamic_index_in_dim(stack, m ^ r, 0, keepdims=False)
+
+    stack_mine = quarter_stack(hidden + down_mine[:, :width])
+    stack_next = quarter_stack(down_next[:, :width])
+    sent = low(jnp.stack([take(stack_mine, 1), take(stack_mine, 3), take(stack_next, 1), take(stack_next, 3)]))
+    came = swap(sent, "mp", 1).astype(jnp.float32)
+    exit_stack = quarter_stack(down_exit_full)
+    results = []
+    for i, r in ((0, 0), (1, 2)):
+        for t, stack in ((0, stack_mine), (1, stack_next)):
+            results.append(low(take(stack, r) + came[2 * (1 - t) + i] + dot(low_down[t], take(exit_stack, r))))
+    kept_rows = jnp.stack(place(results[:2], x))
+    sent_rows = jnp.stack(place(results[2:], x))
+    output = jnp.concatenate(place([kept_rows, swap(sent_rows, "mp", 2)], y), 0)
+
+    inner_back = got_back[:, width:] + jnp.concatenate([back_mine[0][:, width:], back_mine[1][:, width:]], 1)
+    low_back_gate = low(inner_back[:, :rank]) * select[0]
+    low_back_up = low(inner_back[:, rank:]) * select[0]
+    grad_normed_two = (
+        got_back[:, :width]
+        + back_mine[0][:, :width]
+        + back_mine[1][:, :width]
+        + contract(low_back_gate, gate_entry_full, 1, 1)
+        + contract(low_back_up, up_entry_full, 1, 1)
+    )
+    weighted_two = grad_normed_two * gain_two
+    grad_hidden = (
+        grad_down[0].astype(jnp.float32)
+        + scale_two * weighted_two
+        - hidden * (scale_two**3 * jnp.sum(weighted_two * hidden, 1, keepdims=True) / width)
+    )
+    grad_branch = low(grad_hidden)
+    low_back_out = low(contract(grad_branch, out_exit_full, 1, 1)) * select[0]
+
+    near_rows, far_rows, filtered_grads, gate_grads = [], [], [], []
+    for r in range(4):
+        grad_gated = contract(grad_branch, out_blocks[r], 1, 1) + contract(
+            low_back_out, entry_blocks[r][:, rank : 2 * rank], 1, 1
+        )
+        input_gate, output_gate, values, filtered, gated = kept[r]
+        grad_filtered = grad_gated * output_gate.astype(jnp.float32)
+        gate_grads.append(low(grad_gated * filtered.astype(jnp.float32)))
+        filtered_grads.append(grad_filtered)
+    head_rows = jnp.concatenate([g[:2] for g in filtered_grads], 1)
+    head_taps = jnp.concatenate(tap_blocks, 1)
+    head_near = head_taps[1] * prev_one[:2] * head_rows
+    head_far = head_taps[0] * prev_two[:2] * head_rows
+    came_back = from_behind(jnp.concatenate([head_far[:1], head_near[:1] + head_far[1:2]], 0), "seq", -1)
+    grad_normed = 0.0
+    inner_back_in = 0.0
+    in_exit_grads, out_entry_grads = [], []
+    for r in range(4):
+        input_gate, output_gate, values, filtered, gated = kept[r]
+        taps = tap_blocks[r]
+        grad_filtered = filtered_grads[r]
+        near_part = taps[1] * prev_one * grad_filtered
+        far_part = taps[0] * prev_two * grad_filtered
+        tail = came_back[:, r * share : (r + 1) * share]
+        near_part = jnp.concatenate([near_part[1:], tail[1:2]], 0)
+        far_part = jnp.concatenate([far_part[2:], tail[0:1], jnp.zeros((1, share), jnp.float32)], 0)
+        grad_mixed = taps[2] * grad_filtered + near_part + far_part
+        grad_project = jnp.concatenate(
+            [
+                low(grad_mixed * values.astype(jnp.float32)),
+                gate_grads[r],
+                low(grad_mixed * input_gate.astype(jnp.float32)),
+            ],
+            1,
+        )
+        grad_normed = grad_normed + contract(grad_project, in_blocks[r], 1, 1)
+        inner_back_in = inner_back_in + contract(grad_project, in_exit_blocks[r], 1, 1)
+        in_exit_grads.append(contract(low_in, grad_project, 0, 0))
+        out_entry_grads.append(contract(low_back_out, gated, 0, 0))
+    low_back_in = low(inner_back_in) * select[0]
+    grad_normed = grad_normed + contract(low_back_in, in_entry_full, 1, 1)
+    weighted_one = grad_normed * gain_one
+    grad_inputs = (
+        grad_hidden
+        + scale_one * weighted_one
+        - residual * (scale_one**3 * jnp.sum(weighted_one * residual, 1, keepdims=True) / width)
+    )
+    grad_stack = quarter_stack(low(grad_inputs))
+    grad_blocks = [take(grad_stack, 0)] + [swap(take(grad_stack, r), "mp", r) for r in (1, 2, 3)]
+    grad_out = jnp.stack(place(grad_blocks, m)).astype(jnp.float32)
+
+    wide = jnp.stack(
+        [
+            quarter_stack(contract(low_back_gate, normed_two, 0, 0)),
+            quarter_stack(contract(low_back_up, normed_two, 0, 0)),
+            quarter_stack(contract(low_out, grad_branch, 0, 0)),
+            quarter_stack(contract(low_down[0], grad_down[0], 0, 0)),
+            quarter_stack(contract(low_back_in, normed, 0, 0)),
+        ],
+        1,
+    )
+    own_wide = 0.0
+    for r in range(4):
+        exit_grad = in_exit_grads[r].reshape(rank, 3, share).swapaxes(0, 1)
+        part = jnp.concatenate([take(wide, r), out_entry_grads[r][None], exit_grad], 0)
+        own_wide = own_wide + (part if r == 0 else swap(low(part), "mp", r).astype(jnp.float32))
+    wide_total = lax.psum(low(own_wide), "seq").astype(jnp.float32)
+    ffn_total = lax.psum(low(ffn_grads), "seq").astype(jnp.float32)
+    return (
+        output,
+        grad_out,
+        wide_total[4].T,
+        wide_total[6:9].swapaxes(0, 1),
+        wide_total[5].T,
+        wide_total[2],
+        wide_total[0].T,
+        ffn_total[0],
+        wide_total[1].T,
+        ffn_total[1],
+        ffn_total[2].T,
+        wide_total[3],
+    )
+
+
 def solution(mesh):
+    fast = mesh.shape["mp"] == 4 and mesh.shape["seq"] % 4 == 0
     return jax.shard_map(
-        local,
+        fast_local if fast else general_local,
         mesh=mesh,
         in_specs=(
             P(None, "seq", "mp"),

time: 1500 us -> 883 us (0.59)
  blocking collectives: 601 us -> 0 us
  waiting for transfers between devices: 450 us -> 294 us
  local copies, waits for them, and re-layouts: 67.3 us -> 150 us
  starting transfers between devices: 4.33 us -> 52.8 us
  other arithmetic: 73.4 us -> 112 us
  matrix products: 276 us -> 248 us
    psum x9 -> x0, blocking collectives: 601 us -> none  [the longest x7 580 us: mid_total(): return lax.psum(parts, 'mp')]
    ppermute x0 -> x55, waiting for transfers between devices: none -> 238 us  [swap(): lax.ppermute(value, axis, [(i, i ^ bit) for i in range(lax.axis_size(axis...]
    psum x2 -> x1, waiting for transfers between devices: 280 us -> 56 us  [fast_local(): wide_total = lax.psum(low(own_wide), 'seq').astype(jnp.float32)]
    reduce_scatter x3 -> x0, waiting for transfers between devices: 127 us -> none  [share_total(): lax.psum_scatter(partial_value, 'mp', scatter_dimension=1, tiled=True)]
    unnamed x196 -> x594, local copies, waits for them, and re-layouts: 20.9 us -> 77.8 us
    ppermute x0 -> x55, starting transfers between devices: none -> 49.7 us  [swap(): lax.ppermute(value, axis, [(i, i ^ bit) for i in range(lax.axis_size(axis...]
    all_gather x3 -> x0, waiting for transfers between devices: 41.5 us -> none  [the longest x2 23.7 us: row_products(): lax.all_gather(share, 'mp', axis=1, tiled=True)]
    another operation x2 -> x36, other arithmetic: 11.2 us -> 42.8 us  [the longest x21 26.5 us: place(): stacked = jnp.stack(relative)]
  transfers between devices with their start and end apart: 10 -> 58, of which waited for: 8 -> 17; matrix products, arithmetic and copies ran while one was open for 13% -> 42% of each run, Pallas kernels for 0% -> 0%
where the time goes in v1:
time: 883 us; the launch traced here: 875 us
  waiting for transfers between devices  294 us (33%)
  matrix products  248 us (28%)
  local copies, waits for them, and re-layouts  150 us (17%)
  other arithmetic  112 us (13%)
  starting transfers between devices  52.8 us (6%)
  between operations  18.4 us (2%)
    ppermute x55, waiting for transfers between devices, swap(): lax.ppermute(value, axis, [(i, i ^ bit) for i in range(lax.axis_size(axis...  238 us
    dot_general x59, matrix products, contract(): lax.dot_general(left, right, (((left_dim,), (right_extent,)), ((), ())),...  140 us
    dot_general x38, matrix products, dot(): return jnp.dot(left, right, preferred_element_type=jnp.float32)  108 us
    unnamed x594, local copies, waits for them, and re-layouts  77.8 us
    psum x1, waiting for transfers between devices, fast_local(): wide_total = lax.psum(low(own_wide), 'seq').astype(jnp.float32)  56 us
    ppermute x55, starting transfers between devices, swap(): lax.ppermute(value, axis, [(i, i ^ bit) for i in range(lax.axis_size(axis...  49.7 us
    another operation x21, other arithmetic, place(): stacked = jnp.stack(relative)  26.5 us
    convert_element_type x15, other arithmetic, low(): return value.astype(jnp.bfloat16)  22.9 us
  transfers between devices with their start and end apart: 58, of which 17 were waited for; matrix products, arithmetic and copies ran while one was open for 42% of the time, Pallas kernels for 0%

profile of v1, /device:TPU:0, one launch (start us, length us, event | category | flops | bytes accessed | tf_op | source)
XLA Modules:
  0.0 875.4 jit_solution(15121006362533399285)
XLA Ops:
  25.5 6.1 copy.180
  32.6 7.9 copy.200
  40.7 5.4 constant_dynamic-update-slice_fusion.11
  46.1 8.4 copy.196
  84.9 9.5 %collective-permute-done.9 = bf16[96,512]{1,0:T(8,128)(2,1)S(1)} collective-permute-done((bf16[96,512]{1,0:T(8,128)(2,1)S(1)}, bf16[96,512]{1,0:T(8,128)(2,1)S(1)}, u32[]{:S(2)}, u32[]{:S(2)}) %collective-permute-start.9) | collective-permute-done | bytes 98336 | tf_op jit(solution)/shard_map/ppermute | solution.py:261
  123.5 38.9 %collective-permute-done.26 = bf16[32,1920]{0,1:T(8,128)(2,1)S(1)} collective-permute-done((bf16[32,1920]{0,1:T(8,128)(2,1)S(1)}, bf16[32,1920]{0,1:T(8,128)(2,1)S(1)}, u32[]{:S(2)}, u32[]{:S(2)}) %collective-permute-start.26) | collective-permute-done | bytes 122912 | tf_op jit(solution)/shard_map/ppermute | solution.py:261
  198.1 23.8 %collective-permute-done.29 = bf16[96,1536]{1,0:T(8,128)(2,1)} collective-permute-done((bf16[96,1536]{1,0:T(8,128)(2,1)}, bf16[96,1536]{1,0:T(8,128)(2,1)}, u32[]{:S(2)}, u32[]{:S(2)}) %collective-permute-start.29) | collective-permute-done | bytes 294944 | tf_op jit(solution)/shard_map/ppermute | solution.py:261
  232.7 12.3 %collective-permute-done.47 = bf16[2,512,384]{2,1,0:T(8,128)(2,1)S(1)} collective-permute-done((bf16[2,512,384]{2,1,0:T(8,128)(2,1)S(1)}, bf16[2,512,384]{2,1,0:T(8,128)(2,1)S(1)}, u32[]{:S(2)}, u32[]{:S(2)}) %collective-permute-start.47) | collective-permute-done | bytes 786464 | tf_op jit(solution)/shard_map/ppermute | solution.py:261
  249.4 14.1 %collective-permute-done.32 = bf16[416,1728]{1,0:T(8,128)(2,1)} collective-permute-done((bf16[416,1728]{1,0:T(8,128)(2,1)S(1)}, bf16[416,1728]{1,0:T(8,128)(2,1)}, u32[]{:S(2)}, u32[]{:S(2)}) %collective-permute-start.32) | collective-permute-done | bytes 1437728 | tf_op jit(solution)/shard_map/ppermute | solution.py:261
  266.1 32.8 %collective-permute-done.46 = bf16[2,512,384]{2,1,0:T(8,128)(2,1)S(1)} collective-permute-done((bf16[2,512,384]{2,1,0:T(8,128)(2,1)S(1)}, bf16[2,512,384]{2,1,0:T(8,128)(2,1)S(1)}, u32[]{:S(2)}, u32[]{:S(2)}) %collective-permute-start.46) | collective-permute-done | bytes 786464 | tf_op jit(solution)/shard_map/ppermute | solution.py:261
  319.6 12.3 %collective-permute-done.23 = bf16[384,1152]{0,1:T(8,128)(2,1)S(1)} collective-permute-done((bf16[384,1152]{0,1:T(8,128)(2,1)S(1)}, bf16[384,1152]{0,1:T(8,128)(2,1)S(1)}, u32[]{:S(2)}, u32[]{:S(2)}) %collective-permute-start.23) | collective-permute-done | bytes 884768 | tf_op jit(solution)/shard_map/ppermute | solution.py:261
  331.9 5.8 fusion.291
  397.8 9.4 %multiply_convert_fusion.3 = (bf16[512,1728]{0,1:T(8,128)(2,1)}, bf16[512,1728]{0,1:T(8,128)(2,1)}, bf16[512,1728]{0,1:T(8,128)(2,1)}) fusion(f32[512,1728]{0,1:T(8,128)} %fusion.292, f32[512,1728]{0,1:T(8,128)} %fusion.75, bf16[128,1728]{1,0:T(8,128)(2,1)} %copy.197, bf16[1536,1728]{1,0:T(8,128)(2,1)S(1)} %bitcast.576, bf16[512,128]{1,0:T(8,128)(2,1)S(1)} %fusion.57, ...), kind=kOutput, calls=%fused_computation.30 | convolution fusion | flops 2972581888 | bytes 19841024 | tf_op jit(solution)/shard_map/dot_general | solution.py:295
  407.2 8.6 fusion.289
  459.9 8.0 fusion.264
  467.9 10.1 %multiply_convert_fusion.2 = (bf16[512,1728]{0,1:T(8,128)(2,1)}, bf16[512,1728]{0,1:T(8,128)(2,1)}, bf16[512,1728]{0,1:T(8,128)(2,1)}) fusion(f32[512,1728]{0,1:T(8,128)} %fusion.264, f32[512,1728]{0,1:T(8,128)} %fusion.74, bf16[416,1728]{1,0:T(8,128)(2,1)} %get-tuple-element.139, bf16[416,1728]{1,0:T(8,128)(2,1)} %get-tuple-element.140, ...), kind=kOutput, calls=%fused_computation.29 | convolution fusion | flops 2984083456 | bytes 19841024 | tf_op jit(solution)/shard_map/dot_general | solution.py:295
  478.0 7.8 convolution_add_fusion.13
  485.8 10.8 %convolution_add_fusion.12 = f32[512,1664]{1,0:T(8,128)} fusion(f32[512,1664]{1,0:T(8,128)} %fusion.261, bf16[512,1728]{0,1:T(8,128)(2,1)} %get-tuple-element.127, bf16[416,1728]{1,0:T(8,128)(2,1)} %get-tuple-element.143, bf16[416,1728]{1,0:T(8,128)(2,1)} %get-tuple-element.144, bf16[416,1728]{1,0:T(8,128)(2,1)} %get-tuple-element.145, ...), kind=kOutput, calls=%fused_computation.63 | convolution fusion | flops 2968256512 | bytes 14336000 | tf_op jit(solution)/shard_map/dot_general | solution.py:21
  496.6 7.9 convolution_add_fusion.17
  515.5 8.5 multiply_convert_fusion.7
  524.0 7.4 fusion.262
  542.2 5.7 fusion.72
  547.9 10.1 %multiply_convert_fusion.6 = (bf16[512,1728]{0,1:T(8,128)(2,1)S(1)}, bf16[512,1728]{0,1:T(8,128)(2,1)S(1)}, bf16[512,1728]{0,1:T(8,128)(2,1)S(1)}) fusion(f32[512,1728]{0,1:T(8,128)} %fusion.72, f32[512,1728]{0,1:T(8,128)} %fusion.70, bf16[512,1664]{1,0:T(8,128)(2,1)} %copy-done.246, bf16[432,1664]{1,0:T(8,128)(2,1)} %get-tuple-element.147, ...), kind=kOutput, calls=%fused_computation.33 | convolution fusion | flops 2980675584 | bytes 19841024 | tf_op jit(solution)/shard_map/dot_general | solution.py:21
  558.0 6.2 convolution_add_fusion.15
  564.2 7.4 convolution_add_fusion.14
  580.6 6.2 convolution_add_fusion.16
  599.7 42.3 %collective-permute-done.43 = bf16[2,512,128]{2,1,0:T(8,128)(2,1)S(1)} collective-permute-done((bf16[2,512,128]{2,1,0:T(8,128)(2,1)S(1)}, bf16[2,512,128]{2,1,0:T(8,128)(2,1)S(1)}, u32[]{:S(2)}, u32[]{:S(2)}) %collective-permute-start.43) | collective-permute-done | bytes 262176 | tf_op jit(solution)/shard_map/ppermute | solution.py:261
  711.6 5.7 convolution_add_fusion.11
  735.1 8.6 collective-permute-done.50
  750.9 24.4 %collective-permute-done.52 = bf16[512,384]{1,0:T(8,128)(2,1)} collective-permute-done((bf16[512,384]{1,0:T(8,128)(2,1)}, bf16[512,384]{1,0:T(8,128)(2,1)}, u32[]{:S(2)}, u32[]{:S(2)}) %collective-permute-start.52) | collective-permute-done | bytes 393248 | tf_op jit(solution)/shard_map/ppermute | solution.py:261
  778.8 6.6 collective-permute-done.54
  796.8 56.0 %all-reduce.4.cloned.1.call-done = (bf16[9,128,384]{2,1,0:T(8,128)(2,1)}, bf16[3,128,1728]{1,2,0:T(8,128)(2,1)}) async-done(((bf16[9,128,384]{2,1,0:T(8,128)(2,1)}, bf16[3,128,1728]{1,2,0:T(8,128)(2,1)}), (bf16[9,128,384]{2,1,0:T(8,128)(2,1)}, bf16[3,128,1728]{1,2,0:T(8,128)(2,1)})) %all-reduce.4.cloned.1.call-update) | async-done | bytes 2211856 | tf_op jit(solution)/shard_map/psum | solution.py:587
  (1001 shorter events, 422.2 us)
Async XLA Ops:
  7.2 845.6 %all-reduce.4.cloned.1.call-start = ((), (), s32[]{:S(2)}) async-start(), calls=%async_computation | async-start | bytes 4423680 | tf_op jit(solution)/shard_map/psum | solution.py:587
  11.8 66.3 %collective-permute-start.4 = (bf16[192,512]{1,0:T(8,128)(2,1)}, bf16[192,512]{1,0:T(8,128)(2,1)}, u32[]{:S(2)}, u32[]{:S(2)}) collective-permute-start(bf16[192,512]{1,0:T(8,128)(2,1)} %constant_dynamic-slice_fusion.17), channel_id=1, source_target_pairs={{0,1},{1,0},{2,3},{3,2},{4,5},{5,4},{6,7},{7,6},{8,9},{9,8},{10,11... | collective-permute-start | bytes 589832 | tf_op jit(solution)/shard_map/ppermute | solution.py:261
  14.8 66.8 %collective-permute-start.6 = (bf16[192,512]{1,0:T(8,128)(2,1)}, bf16[192,512]{1,0:T(8,128)(2,1)S(1)}, u32[]{:S(2)}, u32[]{:S(2)}) collective-permute-start(bf16[192,512]{1,0:T(8,128)(2,1)} %constant_dynamic-slice_fusion.17), channel_id=1, source_target_pairs={{0,2},{1,3},{2,0},{3,1},{4,6},{5,7},{6,4},{7,5},{8,10},{9,11},{10,... | collective-permute-start | bytes 589832 | tf_op jit(solution)/shard_map/ppermute | solution.py:261
  17.0 59.3 %collective-permute-start = (bf16[4,2,384]{2,1,0:T(2,128)(2,1)S(1)}, bf16[4,2,384]{2,1,0:T(2,128)(2,1)S(1)}, u32[]{:S(2)}, u32[]{:S(2)}) collective-permute-start(bf16[4,2,384]{2,1,0:T(2,128)(2,1)S(1)} %slice.658), channel_id=1, source_target_pairs={{0,4},{4,8},{8,12},{12,16},{16,20},{20,24},{24,28},{1,5},{5,9},{9,... | collective-permute-start | bytes 18440 | tf_op jit(solution)/shard_map/ppermute | solution.py:17
  24.5 70.0 %collective-permute-start.19 = (bf16[80,1920]{0,1:T(8,128)(2,1)}, bf16[80,1920]{0,1:T(8,128)(2,1)}, u32[]{:S(2)}, u32[]{:S(2)}) collective-permute-start(bf16[80,1920]{0,1:T(8,128)(2,1)} %fusion.127), channel_id=1, source_target_pairs={{0,2},{1,3},{2,0},{3,1},{4,6},{5,7},{6,4},{7,5},{8,10},{9,11},{10,... | collective-permute-start | bytes 921608 | tf_op jit(solution)/shard_map/ppermute | solution.py:261
  99.2 65.8 %collective-permute-start.15 = (bf16[192,1536]{1,0:T(8,128)(2,1)S(1)}, bf16[192,1536]{1,0:T(8,128)(2,1)}, u32[]{:S(2)}, u32[]{:S(2)}) collective-permute-start(bf16[192,1536]{1,0:T(8,128)(2,1)S(1)} %copy-done.197), channel_id=1, source_target_pairs={{0,1},{1,0},{2,3},{3,2},{4,5},{5,4},{6,7},{7,6},{8,9},{9,8},{10,11... | collective-permute-start | bytes 1769480 | tf_op jit(solution)/shard_map/ppermute | solution.py:261
  100.7 66.5 %collective-permute-start.21 = (bf16[192,1536]{1,0:T(8,128)(2,1)S(1)}, bf16[192,1536]{1,0:T(8,128)(2,1)S(1)}, u32[]{:S(2)}, u32[]{:S(2)}) collective-permute-start(bf16[192,1536]{1,0:T(8,128)(2,1)S(1)} %copy-done.197), channel_id=1, source_target_pairs={{0,2},{1,3},{2,0},{3,1},{4,6},{5,7},{6,4},{7,5},{8,10},{9,11},{10,... | collective-permute-start | bytes 1769480 | tf_op jit(solution)/shard_map/ppermute | solution.py:261
  102.5 143.8 %collective-permute-start.35 = (bf16[416,1728]{1,0:T(8,128)(2,1)}, bf16[416,1728]{1,0:T(8,128)(2,1)}, u32[]{:S(2)}, u32[]{:S(2)}) collective-permute-start(bf16[416,1728]{1,0:T(8,128)(2,1)} %fusion.48), channel_id=1, source_target_pairs={{0,2},{1,3},{2,0},{3,1},{4,6},{5,7},{6,4},{7,5},{8,10},{9,11},{10,... | collective-permute-start | bytes 4313096 | tf_op jit(solution)/shard_map/ppermute | solution.py:261
  117.2 45.2 %collective-permute-start.27 = (bf16[48,1920]{0,1:T(8,128)(2,1)S(1)}, bf16[48,1920]{0,1:T(8,128)(2,1)S(1)}, u32[]{:S(2)}, u32[]{:S(2)}) collective-permute-start(bf16[48,1920]{0,1:T(8,128)(2,1)S(1)} %slice.892), channel_id=1, source_target_pairs={{0,1},{1,0},{2,3},{3,2},{4,5},{5,4},{6,7},{7,6},{8,9},{9,8},{10,11... | collective-permute-start | bytes 552968 | tf_op jit(solution)/shard_map/ppermute | solution.py:261
  117.3 45.1 %collective-permute-start.26 = (bf16[32,1920]{0,1:T(8,128)(2,1)S(1)}, bf16[32,1920]{0,1:T(8,128)(2,1)S(1)}, u32[]{:S(2)}, u32[]{:S(2)}) collective-permute-start(bf16[32,1920]{0,1:T(8,128)(2,1)S(1)} %bitcast.631), channel_id=1, source_target_pairs={{0,2},{1,3},{2,0},{3,1},{4,6},{5,7},{6,4},{7,5},{8,10},{9,11},{10,... | collective-permute-start | bytes 368648 | tf_op jit(solution)/shard_map/ppermute | solution.py:261
  167.2 79.5 %collective-permute-start.38 = (bf16[432,1664]{1,0:T(8,128)(2,1)}, bf16[432,1664]{1,0:T(8,128)(2,1)}, u32[]{:S(2)}, u32[]{:S(2)}) collective-permute-start(bf16[432,1664]{1,0:T(8,128)(2,1)} %constant_dynamic-slice_fusion.10), channel_id=1, source_target_pairs={{0,2},{1,3},{2,0},{3,1},{4,6},{5,7},{6,4},{7,5},{8,10},{9,11},{10,... | collective-permute-start | bytes 4313096 | tf_op jit(solution)/shard_map/ppermute | solution.py:261
  173.2 48.7 %collective-permute-start.29 = (bf16[96,1536]{1,0:T(8,128)(2,1)}, bf16[96,1536]{1,0:T(8,128)(2,1)}, u32[]{:S(2)}, u32[]{:S(2)}) collective-permute-start(bf16[96,1536]{1,0:T(8,128)(2,1)} %slice.905), channel_id=1, source_target_pairs={{0,2},{1,3},{2,0},{3,1},{4,6},{5,7},{6,4},{7,5},{8,10},{9,11},{10,... | collective-permute-start | bytes 884744 | tf_op jit(solution)/shard_map/ppermute | solution.py:261
  185.7 37.2 %collective-permute-start.30 = (bf16[96,1536]{1,0:T(8,128)(2,1)}, bf16[96,1536]{1,0:T(8,128)(2,1)}, u32[]{:S(2)}, u32[]{:S(2)}) collective-permute-start(bf16[96,1536]{1,0:T(8,128)(2,1)} %slice.906), channel_id=1, source_target_pairs={{0,1},{1,0},{2,3},{3,2},{4,5},{5,4},{6,7},{7,6},{8,9},{9,8},{10,11... | collective-permute-start | bytes 884744 | tf_op jit(solution)/shard_map/ppermute | solution.py:261
  227.8 35.7 %collective-permute-start.32 = (bf16[416,1728]{1,0:T(8,128)(2,1)S(1)}, bf16[416,1728]{1,0:T(8,128)(2,1)}, u32[]{:S(2)}, u32[]{:S(2)}) collective-permute-start(bf16[416,1728]{1,0:T(8,128)(2,1)S(1)} %copy-done.176), channel_id=1, source_target_pairs={{0,2},{1,3},{2,0},{3,1},{4,6},{5,7},{6,4},{7,5},{8,10},{9,11},{10,... | collective-permute-start | bytes 4313096 | tf_op jit(solution)/shard_map/ppermute | solution.py:261
  229.5 79.4 %collective-permute-start.11 = (bf16[768,1152]{0,1:T(8,128)(2,1)}, bf16[768,1152]{0,1:T(8,128)(2,1)}, u32[]{:S(2)}, u32[]{:S(2)}) collective-permute-start(bf16[768,1152]{0,1:T(8,128)(2,1)} %constant_dynamic-slice_fusion.12), channel_id=1, source_target_pairs={{0,1},{1,0},{2,3},{3,2},{4,5},{5,4},{6,7},{7,6},{8,9},{9,8},{10,11... | collective-permute-start | bytes 5308424 | tf_op jit(solution)/shard_map/ppermute | solution.py:261
  245.0 53.8 %collective-permute-start.46 = (bf16[2,512,384]{2,1,0:T(8,128)(2,1)S(1)}, bf16[2,512,384]{2,1,0:T(8,128)(2,1)S(1)}, u32[]{:S(2)}, u32[]{:S(2)}) collective-permute-start(bf16[2,512,384]{2,1,0:T(8,128)(2,1)S(1)} %bitcast.585), channel_id=1, source_target_pairs={{0,1},{1,0},{2,3},{3,2},{4,5},{5,4},{6,7},{7,6},{8,9},{9,8},{10,11... | collective-permute-start | bytes 2359304 | tf_op jit(solution)/shard_map/ppermute | solution.py:261
  246.4 70.8 %collective-permute-start.17 = (bf16[768,1152]{0,1:T(8,128)(2,1)}, bf16[768,1152]{0,1:T(8,128)(2,1)}, u32[]{:S(2)}, u32[]{:S(2)}) collective-permute-start(bf16[768,1152]{0,1:T(8,128)(2,1)} %constant_dynamic-slice_fusion.12), channel_id=1, source_target_pairs={{0,2},{1,3},{2,0},{3,1},{4,6},{5,7},{6,4},{7,5},{8,10},{9,11},{10,... | collective-permute-start | bytes 5308424 | tf_op jit(solution)/shard_map/ppermute | solution.py:261
  246.7 92.8 %collective-permute-start.36 = (bf16[416,1728]{1,0:T(8,128)(2,1)}, bf16[416,1728]{1,0:T(8,128)(2,1)}, u32[]{:S(2)}, u32[]{:S(2)}) collective-permute-start(bf16[416,1728]{1,0:T(8,128)(2,1)} %collective-permute-done.35), channel_id=1, source_target_pairs={{0,8},{4,12},{8,0},{12,4},{16,24},{20,28},{24,16},{28,20},{1,9},{5... | collective-permute-start | bytes 4313096 | tf_op jit(solution)/shard_map/ppermute | solution.py:261
  263.6 80.3 %collective-permute-start.39 = (bf16[432,1664]{1,0:T(8,128)(2,1)}, bf16[432,1664]{1,0:T(8,128)(2,1)}, u32[]{:S(2)}, u32[]{:S(2)}) collective-permute-start(bf16[432,1664]{1,0:T(8,128)(2,1)} %collective-permute-done.38), channel_id=1, source_target_pairs={{0,8},{4,12},{8,0},{12,4},{16,24},{20,28},{24,16},{28,20},{1,9},{5... | collective-permute-start | bytes 4313096 | tf_op jit(solution)/shard_map/ppermute | solution.py:261
  298.8 48.6 %collective-permute-start.33 = (bf16[416,1728]{1,0:T(8,128)(2,1)}, bf16[416,1728]{1,0:T(8,128)(2,1)}, u32[]{:S(2)}, u32[]{:S(2)}) collective-permute-start(bf16[416,1728]{1,0:T(8,128)(2,1)} %collective-permute-done.32), channel_id=1, source_target_pairs={{0,8},{4,12},{8,0},{12,4},{16,24},{20,28},{24,16},{28,20},{1,9},{5... | collective-permute-start | bytes 4313096 | tf_op jit(solution)/shard_map/ppermute | solution.py:261
  343.8 85.6 %collective-permute-start.37 = (bf16[2,416,1728]{2,1,0:T(8,128)(2,1)}, bf16[2,416,1728]{2,1,0:T(8,128)(2,1)}, u32[]{:S(2)}, u32[]{:S(2)}) collective-permute-start(bf16[2,416,1728]{2,1,0:T(8,128)(2,1)} %pad_maximum_fusion.14), channel_id=1, source_target_pairs={{0,4},{4,0},{8,12},{12,8},{16,20},{20,16},{24,28},{28,24},{1,5},{5... | collective-permute-start | bytes 8626184 | tf_op jit(solution)/shard_map/ppermute | solution.py:261
  347.5 89.5 %collective-permute-start.40 = (bf16[2,432,1664]{2,1,0:T(8,128)(2,1)}, bf16[2,432,1664]{2,1,0:T(8,128)(2,1)}, u32[]{:S(2)}, u32[]{:S(2)}) collective-permute-start(bf16[2,432,1664]{2,1,0:T(8,128)(2,1)} %pad_maximum_fusion.15), channel_id=1, source_target_pairs={{0,4},{4,0},{8,12},{12,8},{16,20},{20,16},{24,28},{28,24},{1,5},{5... | collective-permute-start | bytes 8626184 | tf_op jit(solution)/shard_map/ppermute | solution.py:261
  350.1 95.0 %collective-permute-start.34 = (bf16[2,416,1728]{2,1,0:T(8,128)(2,1)S(1)}, bf16[2,416,1728]{2,1,0:T(8,128)(2,1)}, u32[]{:S(2)}, u32[]{:S(2)}) collective-permute-start(bf16[2,416,1728]{2,1,0:T(8,128)(2,1)S(1)} %pad_maximum_fusion.13), channel_id=1, source_target_pairs={{0,4},{4,0},{8,12},{12,8},{16,20},{20,16},{24,28},{28,24},{1,5},{5... | collective-permute-start | bytes 8626184 | tf_op jit(solution)/shard_map/ppermute | solution.py:261
  390.7 118.1 %collective-permute-start.41 = (bf16[512,1536]{1,0:T(8,128)(2,1)S(1)}, bf16[512,1536]{1,0:T(8,128)(2,1)S(1)}, u32[]{:S(2)}, u32[]{:S(2)}) collective-permute-start(bf16[512,1536]{1,0:T(8,128)(2,1)S(1)} %multiply_convert_fusion.13), channel_id=1, source_target_pairs={{0,1},{1,0},{2,3},{3,2},{4,5},{5,4},{6,7},{7,6},{8,9},{9,8},{10,11... | collective-permute-start | bytes 4718600 | tf_op jit(solution)/shard_map/ppermute | solution.py:261
  591.5 51.5 %collective-permute-start.56 = (bf16[3,128,1728]{1,2,0:T(8,128)(2,1)S(1)}, bf16[3,128,1728]{1,2,0:T(8,128)(2,1)S(1)}, u32[]{:S(2)}, u32[]{:S(2)}) collective-permute-start(bf16[3,128,1728]{1,2,0:T(8,128)(2,1)S(1)} %pad_maximum_fusion.37), channel_id=1, source_target_pairs={{0,2},{1,3},{2,0},{3,1},{4,6},{5,7},{6,4},{7,5},{8,10},{9,11},{10,... | collective-permute-start | bytes 3981320 | tf_op jit(solution)/shard_map/ppermute | solution.py:261
  594.5 49.9 %collective-permute-start.48 = (bf16[512,1792]{1,0:T(8,128)(2,1)S(1)}, bf16[512,1792]{1,0:T(8,128)(2,1)S(1)}, u32[]{:S(2)}, u32[]{:S(2)}) collective-permute-start(bf16[512,1792]{1,0:T(8,128)(2,1)S(1)} %pad_maximum_fusion.22), channel_id=1, source_target_pairs={{0,1},{1,0},{2,3},{3,2},{4,5},{5,4},{6,7},{7,6},{8,9},{9,8},{10,11... | collective-permute-start | bytes 5505032 | tf_op jit(solution)/shard_map/ppermute | solution.py:261
  596.1 45.9 %collective-permute-start.43 = (bf16[2,512,128]{2,1,0:T(8,128)(2,1)S(1)}, bf16[2,512,128]{2,1,0:T(8,128)(2,1)S(1)}, u32[]{:S(2)}, u32[]{:S(2)}) collective-permute-start(bf16[2,512,128]{2,1,0:T(8,128)(2,1)S(1)} %pad_maximum_fusion.77), channel_id=1, source_target_pairs={{0,1},{1,0},{2,3},{3,2},{4,5},{5,4},{6,7},{7,6},{8,9},{9,8},{10,11... | collective-permute-start | bytes 786440 | tf_op jit(solution)/shard_map/ppermute | solution.py:261
  678.8 109.5 %collective-permute-start.42 = (bf16[4,512,384]{2,1,0:T(8,128)(2,1)}, bf16[4,512,384]{2,1,0:T(8,128)(2,1)}, u32[]{:S(2)}, u32[]{:S(2)}) collective-permute-start(bf16[4,512,384]{2,1,0:T(8,128)(2,1)} %pad_maximum_fusion.30), channel_id=1, source_target_pairs={{0,1},{1,0},{2,3},{3,2},{4,5},{5,4},{6,7},{7,6},{8,9},{9,8},{10,11... | collective-permute-start | bytes 4718600 | tf_op jit(solution)/shard_map/ppermute | solution.py:261
  710.6 68.3 %collective-permute-start.53 = (bf16[9,128,384]{2,1,0:T(8,128)(2,1)}, bf16[9,128,384]{2,1,0:T(8,128)(2,1)}, u32[]{:S(2)}, u32[]{:S(2)}) collective-permute-start(bf16[9,128,384]{2,1,0:T(8,128)(2,1)} %pad_maximum_fusion.53), channel_id=1, source_target_pairs={{0,1},{1,0},{2,3},{3,2},{4,5},{5,4},{6,7},{7,6},{8,9},{9,8},{10,11... | collective-permute-start | bytes 2654216 | tf_op jit(solution)/shard_map/ppermute | solution.py:261
  731.1 54.4 %collective-permute-start.54 = (bf16[9,128,384]{2,1,0:T(8,128)(2,1)}, bf16[9,128,384]{2,1,0:T(8,128)(2,1)}, u32[]{:S(2)}, u32[]{:S(2)}) collective-permute-start(bf16[9,128,384]{2,1,0:T(8,128)(2,1)} %pad_maximum_fusion.54), channel_id=1, source_target_pairs={{0,2},{1,3},{2,0},{3,1},{4,6},{5,7},{6,4},{7,5},{8,10},{9,11},{10,... | collective-permute-start | bytes 2654216 | tf_op jit(solution)/shard_map/ppermute | solution.py:261
  743.7 41.8 %collective-permute-start.55 = (bf16[9,128,384]{2,1,0:T(8,128)(2,1)}, bf16[9,128,384]{2,1,0:T(8,128)(2,1)S(1)}, u32[]{:S(2)}, u32[]{:S(2)}) collective-permute-start(bf16[9,128,384]{2,1,0:T(8,128)(2,1)} %pad_maximum_fusion.55), channel_id=1, source_target_pairs={{0,3},{1,2},{2,1},{3,0},{4,7},{5,6},{6,5},{7,4},{8,11},{9,10},{10,... | collective-permute-start | bytes 2654216 | tf_op jit(solution)/shard_map/ppermute | solution.py:261
  793.5 71.8 %collective-permute-start.44 = (bf16[2,512,384]{2,1,0:T(8,128)(2,1)}, bf16[2,512,384]{2,1,0:T(8,128)(2,1)}, u32[]{:S(2)}, u32[]{:S(2)}) collective-permute-start(bf16[2,512,384]{2,1,0:T(8,128)(2,1)} %pad_maximum_fusion.56), channel_id=1, source_target_pairs={{0,2},{1,3},{2,0},{3,1},{4,6},{5,7},{6,4},{7,5},{8,10},{9,11},{10,... | collective-permute-start | bytes 2359304 | tf_op jit(solution)/shard_map/ppermute | solution.py:261
  (311 other events, 4216.6 us)
Sparse Core Ops, SparseCore 0:
  788.4 64.3 all-reduce.3

commit v2 on v0

--- a/solution.py
+++ b/solution.py
@@ -1,6 +1,10 @@
+import functools
+
 import jax
 import jax.numpy as jnp
 from jax import lax
+from jax.experimental import pallas as pl
+from jax.experimental.pallas import tpu as pltpu
 from jax.sharding import PartitionSpec as P
 
 RANK = 16
@@ -62,7 +66,7 @@
     return (prev_one, prev_two, select.astype(jnp.bfloat16))
 
 
-def local(
+def general_local(
     inputs,
     cotangent,
     mixer_gain,
@@ -257,9 +261,978 @@
     )
 
 
+VMEM_BYTES = 58 * 1024 * 1024
+
+
+def product(left, right):
+    return jnp.dot(left, right, preferred_element_type=jnp.float32)
+
+
+def product_t(left, right):
+    return lax.dot_general(left, right, (((1,), (1,)), ((), ())), preferred_element_type=jnp.float32)
+
+
+def wide_value(value):
+    return value.astype(jnp.float32)
+
+
+def low(value):
+    return value.astype(jnp.bfloat16)
+
+
+def each_tile(total, size, body):
+    whole = total // size
+    if whole:
+
+        @pl.loop(0, whole)
+        def _(i):
+            body(pl.multiple_of(i * size, size), size)
+
+    if total % size:
+        body(whole * size, total % size)
+
+
+def spans(total, size):
+    return [(at, min(size, total - at)) for at in range(0, total, size)]
+
+
+class Mover:
+    def __init__(self, sems):
+        self.sems, self.count, self.pending = sems, 0, []
+
+    def start(self, source, target):
+        copy = pltpu.make_async_copy(source, target, self.sems.at[self.count])
+        self.count += 1
+        copy.start()
+        self.pending.append(copy)
+        return copy
+
+    def wait(self, copies=None):
+        for copy in list(self.pending if copies is None else copies):
+            copy.wait()
+            self.pending = [c for c in self.pending if c is not copy]
+
+
+def piece_index(place_ref, kind, flip):
+    return jnp.bitwise_xor(place_ref[1 if kind == "half" else 2], flip)
+
+
+def start_in(mover, loads, own, located, target, width, share):
+    for i in range(3):
+        loads.append(mover.start(own.at[i], target.at[:, pl.ds(i * width, share)]))
+    for ref, r, index, pack, _ in located:
+        rows = pl.ds(pl.multiple_of(index * pack.in_rows, 16), pack.in_rows)
+        for i in range(3):
+            source = ref.at[pl.ds(i * pack.in_rows, pack.in_rows)]
+            loads.append(mover.start(source, target.at[rows, pl.ds(i * width + r * share, share)]))
+
+
+def start_out(mover, loads, own, located, target, width, share):
+    loads.append(mover.start(own, target.at[pl.ds(0, share)]))
+    for ref, r, index, pack, _ in located:
+        rows = pl.ds(pl.multiple_of(r * share + index * pack.out_rows, 16), pack.out_rows)
+        for i in range(4):
+            source = ref.at[pl.ds(pack.out_at + i * pack.out_rows, pack.out_rows)]
+            loads.append(mover.start(source, target.at[rows, pl.ds(i * share, share)]))
+
+
+def kernel_call(body, name, args, kinds, outs, scratch, sems, flops, size, out_space=pl.ANY):
+    spaces = {"s": pltpu.SMEM, "v": pltpu.VMEM, "a": pl.ANY}
+    return pl.pallas_call(
+        body,
+        out_shape=tuple(outs),
+        in_specs=[pl.BlockSpec(memory_space=spaces[k]) for k in kinds],
+        out_specs=tuple(pl.BlockSpec(memory_space=out_space) for _ in outs),
+        scratch_shapes=list(scratch) + [pltpu.SemaphoreType.DMA((sems,))],
+        compiler_params=pltpu.CompilerParams(vmem_limit_bytes=VMEM_BYTES),
+        cost_estimate=pl.CostEstimate(flops=flops, bytes_accessed=size, transcendentals=0),
+        name=name,
+    )(*args)
+
+
+def shaped(shape, kind=jnp.bfloat16):
+    return jax.ShapeDtypeStruct(shape, kind)
+
+
+TAP_ROWS = 16
+
+
+class Pack:
+    def __init__(self, width, share, rank, count):
+        self.in_rows, self.out_rows, self.side_rows = width // count, share // count, rank // count
+        self.out_at = 3 * self.in_rows
+        self.entry_at = self.out_at + 4 * self.out_rows
+        self.side_at = self.entry_at + 2 * self.out_rows
+        self.tap_at = self.side_at + 5 * self.side_rows
+        self.rows = self.tap_at + TAP_ROWS
+
+
+PACK_COUNT = {"half": 2, "quarter": 4}
+
+
+def pack_first_kernel(place_ref, inputs, in_weight, out_weight, *refs):
+    entries, (in_exit, out_exit, down_exit, taps), outs, sems = refs[:4], refs[4:8], refs[8:-1], refs[-1]
+    share, width = out_weight.shape
+    rank = entries[0].shape[1]
+    mover = Mover(sems)
+    for index, out in ((2, outs[0]), (1, outs[1])):
+        pack = Pack(width, share, rank, 4 if index == 2 else 2)
+
+        def part(rows):
+            return pl.ds(pl.multiple_of(place_ref[index] * rows, 16), rows)
+
+        for i in range(3):
+            mover.start(in_weight.at[i, part(pack.in_rows)], out.at[pl.ds(i * pack.in_rows, pack.in_rows)])
+        rows = part(pack.out_rows)
+        for i in range(4):
+            target = out.at[pl.ds(pack.out_at + i * pack.out_rows, pack.out_rows)]
+            mover.start(out_weight.at[rows, pl.ds(i * share, share)], target)
+            target = out.at[pl.ds(pack.entry_at + i // 3 * pack.out_rows, pack.out_rows), pl.ds(i % 3 * rank, rank)]
+            mover.start(entries[i].at[rows], target)
+        rows = part(pack.side_rows)
+        for i, side in enumerate((in_exit.at[0], in_exit.at[1], in_exit.at[2], out_exit, down_exit)):
+            mover.start(side.at[rows], out.at[pl.ds(pack.side_at + i * pack.side_rows, pack.side_rows)])
+        mover.start(taps, out.at[pl.ds(pack.tap_at, TAP_ROWS)])
+    for r in range(4):
+        mover.start(inputs.at[jnp.bitwise_xor(place_ref[0], r)], outs[2 + r])
+    mover.wait()
+
+
+def pack_first(place_ids, inputs, in_weight, out_weight, entries, sides, taps):
+    length, share = inputs.shape[1:]
+    width, rank = in_weight.shape[1], entries[0].shape[1]
+    args = [place_ids, inputs, in_weight, out_weight, *entries, *sides, taps]
+    outs = [shaped((Pack(width, share, rank, count).rows, share)) for count in (4, 2)] + [shaped((length, share))] * 4
+    return kernel_call(pack_first_kernel, "pack_first", args, "s" + "a" * 11, outs, [], 64, 0, 16_000_000, pltpu.VMEM)
+
+
+def pack_second_kernel(cuts, place_ref, cotangent, *refs):
+    near, (own, other, far_row), packs, sems = refs[:6], refs[6:9], refs[9:-1], refs[-1]
+    mover = Mover(sems)
+    mine = place_ref[0]
+    mover.start(cotangent.at[jnp.bitwise_xor(mine, 2)], far_row.at[0])
+    mover.start(cotangent.at[jnp.bitwise_xor(mine, 3)], far_row.at[1])
+    mover.start(cotangent.at[mine], own)
+    mover.start(cotangent.at[jnp.bitwise_xor(mine, 1)], other)
+    quarter_rows = near[0].shape[0] // 4
+    width = near[0].shape[1]
+    for (at, n), pack in zip(cuts, packs):
+        rows = pl.ds(pl.multiple_of(place_ref[2] * quarter_rows + at, 16), n)
+        for i in range(3):
+            mover.start(near[2 * i].at[rows], pack.at[i, :, pl.ds(0, width)])
+            mover.start(near[2 * i + 1].at[rows], pack.at[i, :, pl.ds(width, near[1].shape[1])])
+    mover.wait()
+
+
+def pack_second(place_ids, cotangent, near, cuts):
+    length, share = cotangent.shape[1:]
+    outs = [shaped((length, share)), shaped((length, share)), shaped((2, length, share))]
+    outs += [shaped((3, n, near[0].shape[1] + near[1].shape[1])) for _, n in cuts]
+    return kernel_call(
+        functools.partial(pack_second_kernel, cuts), "pack_second", [place_ids, cotangent, *near], "s" + "a" * 7, outs, [], 32, 0, 20_000_000, pltpu.VMEM
+    )
+
+
+def mixer_kernel(plan, *refs):
+    refs = list(refs)
+
+    def take(n):
+        return [refs.pop(0) for _ in range(n)]
+
+    place_ref, select, prev, gain_one, gain_two = take(5)
+    head, in_own, out_own, *own = take(11)
+    entries_own, (in_exit, out_exit, down_exit, taps_own) = own[:4], own[4:]
+    blocks = take(4)
+    pieces = take(len(plan))
+    kept_out, gated_out, tokens_out, normed_out, hidden_out, two_out, lows_out, entry_out, column_out, exit_out, taps_out = take(11)
+    (x_s, n_s, in_s, out_s, entry_s, col_s, exit_s, tap_s, taps_s, proj_s, mix_s) = take(11)
+    kept_s, gated_s, hid_s, two_s, low_in_s, lows_s, sems = refs
+    length, width = gated_s.shape
+    share, rank, edge = width // 4, low_in_s.shape[1], head.shape[1]
+    mover = Mover(sems)
+
+    def absolute(r):
+        return pl.multiple_of(jnp.bitwise_xor(place_ref[0], r) * share, 128)
+
+    for r in range(4):
+        lanes = pl.ds(absolute(r), share)
+        mover.start(blocks[r], x_s.at[pl.ds(edge, length), lanes])
+        mover.start(head.at[r], x_s.at[pl.ds(0, edge), lanes])
+    token_loads = list(mover.pending)
+    row_loads, column_loads, loads, out_loads = [], [], [], []
+    for i, source in enumerate(entries_own):
+        row_loads.append(mover.start(source, entry_s.at[pl.ds(absolute(0), share), pl.ds(i * rank, rank)]))
+    for i, source in enumerate((in_exit.at[0], in_exit.at[1], in_exit.at[2], out_exit, down_exit)):
+        column_loads.append(mover.start(source, col_s.at[pl.ds(i * rank, rank), pl.ds(0, share)]))
+    column_loads.append(mover.start(taps_own, tap_s.at[:, pl.ds(0, share)]))
+    located = [(ref, r, piece_index(place_ref, kind, flip), Pack(width, share, rank, PACK_COUNT[kind]), flip) for ref, (r, kind, flip) in zip(pieces, plan)]
+    for ref, r, index, pack, flip in located:
+        rows = pl.ds(pl.multiple_of(absolute(r) + index * pack.out_rows, 16), pack.out_rows)
+        source = ref.at[pl.ds(pack.entry_at, pack.out_rows)]
+        row_loads.append(mover.start(source, entry_s.at[rows, pl.ds(0, 3 * rank)]))
+        source = ref.at[pl.ds(pack.entry_at + pack.out_rows, pack.out_rows), pl.ds(0, rank)]
+        row_loads.append(mover.start(source, entry_s.at[rows, pl.ds(3 * rank, rank)]))
+        lanes = pl.ds(r * share, share)
+        for i in range(5):
+            rows = pl.ds(pl.multiple_of(i * rank + index * pack.side_rows, 16), pack.side_rows)
+            source = ref.at[pl.ds(pack.side_at + i * pack.side_rows, pack.side_rows)]
+            column_loads.append(mover.start(source, col_s.at[rows, lanes]))
+        if flip == 0:
+            column_loads.append(mover.start(ref.at[pl.ds(pack.tap_at, TAP_ROWS)], tap_s.at[:, lanes]))
+    start_in(mover, loads, in_own, located, in_s, width, share)
+    start_out(mover, out_loads, out_own, located, out_s, width, share)
+    mover.wait(token_loads)
+
+    def norm(at, n):
+        rows = pl.ds(at, n)
+        x = wide_value(x_s[rows, :])
+        scale = lax.rsqrt(jnp.sum(x * x, 1, keepdims=True) / width + EPS)
+        n_s[rows, :] = low(x * scale * gain_one[...])
+
+    each_tile(edge + length, 48, norm)
+    main = pl.ds(edge, length)
+    mover.start(x_s.at[main], tokens_out)
+    mover.start(n_s.at[main], normed_out)
+    mover.wait(row_loads)
+    mover.start(entry_s, entry_out)
+    low_in_s[...] = low(product(n_s[...], entry_s[:, pl.ds(0, rank)])) * select[...]
+    lows_s[0] = low_in_s[main, :]
+    mover.wait(column_loads)
+    mover.start(col_s, column_out)
+    taps_s[...] = wide_value(tap_s[...])[:8]
+    mover.start(taps_s, taps_out)
+    for r in range(4):
+        exit_s[:, pl.ds(absolute(r), share)] = col_s[pl.ds(3 * rank, 2 * rank), pl.ds(r * share, share)]
+    mover.start(exit_s, exit_out)
+    mover.wait(loads)
+    for i in range(3):
+
+        def project(at, n):
+            total = product(n_s[...], in_s[:, pl.ds(i * width + at, n)])
+            total += product(low_in_s[...], col_s[pl.ds(i * rank, rank), pl.ds(at, n)])
+            proj_s[:, pl.ds(i * width + at, n)] = total
+
+        each_tile(width, width // 3, project)
+    for r in range(4):
+        lanes = pl.ds(r * share, share)
+        mix_s[...] = proj_s[:, lanes] * proj_s[:, pl.ds(2 * width + r * share, share)]
+        tap = [taps_s[pl.ds(i, 1), lanes] for i in range(3)]
+        for at, n in spans(length, 128):
+            rows, above = pl.ds(at, n), pl.ds(at + edge, n)
+            filtered = (
+                tap[2] * mix_s[above, :]
+                + tap[1] * (prev[rows, pl.ds(0, 1)] * mix_s[pl.ds(at + edge - 1, n), :])
+                + tap[0] * (prev[rows, pl.ds(1, 1)] * mix_s[pl.ds(at + edge - 2, n), :])
+            )
+            output_gate = proj_s[above, pl.ds(width + r * share, share)]
+            gated_s[rows, lanes] = low(output_gate * filtered)
+            kept_s[0, rows, lanes] = low(proj_s[above, lanes])
+            kept_s[1, rows, lanes] = low(output_gate)
+            kept_s[2, rows, lanes] = low(proj_s[above, pl.ds(2 * width + r * share, share)])
+            kept_s[3, rows, lanes] = low(filtered)
+    mover.start(kept_s, kept_out)
+    mover.start(gated_s, gated_out)
+    chosen = select[main, :]
+    inner = 0.0
+    for r in range(4):
+        rows = pl.ds(absolute(r), share)
+        inner = inner + product(gated_s[:, pl.ds(r * share, share)], entry_s[rows, pl.ds(rank, rank)])
+    lows_s[1] = low(inner) * chosen
+    mover.wait(out_loads)
+
+    def branch(at, n):
+        cols = pl.ds(at, n)
+        total = product(gated_s[...], out_s[:, cols]) + product(lows_s[1], exit_s[pl.ds(0, rank), cols])
+        hid_s[:, cols] = total + wide_value(x_s[main, cols])
+
+    each_tile(width, width // 3, branch)
+    mover.start(hid_s, hidden_out)
+
+    def norm_two(at, n):
+        rows = pl.ds(at, n)
+        h = hid_s[rows, :]
+        scale = lax.rsqrt(jnp.sum(h * h, 1, keepdims=True) / width + EPS)
+        two_s[rows, :] = low(h * scale * gain_two[...])
+
+    each_tile(length, 64, norm_two)
+    mover.start(two_s, two_out)
+    inner = product(two_s[...], entry_s[:, pl.ds(2 * rank, 2 * rank)])
+    lows_s[2] = low(inner[:, :rank]) * chosen
+    lows_s[3] = low(inner[:, rank:]) * chosen
+    mover.start(lows_s, lows_out)
+    mover.wait()
+
+
+def mixer(place_ids, small, own, blocks, pieces):
+    length, share = blocks[0].shape
+    width, rank, edge = 4 * share, own[3].shape[1], own[0].shape[1]
+    bf, f32 = jnp.bfloat16, jnp.float32
+    args = [place_ids, *small, *own, *blocks] + [p[0] for p in pieces]
+    kinds = "s" + "v" * len(small) + "a" * (len(args) - 1 - len(small))
+    v = pltpu.VMEM
+    columns, taps = 5 * rank, TAP_ROWS
+    return kernel_call(
+        functools.partial(mixer_kernel, [p[1:] for p in pieces]),
+        "mixer",
+        args,
+        kinds,
+        [
+            shaped((4, length, width)),
+            shaped((length, width)),
+            shaped((length, width)),
+            shaped((length, width)),
+            shaped((length, width), f32),
+            shaped((length, width)),
+            shaped((4, length, rank)),
+            shaped((width, 4 * rank)),
+            shaped((columns, width)),
+            shaped((2 * rank, width)),
+            shaped((8, width), f32),
+        ],
+        [
+            v((edge + length, width), bf),
+            v((edge + length, width), bf),
+            v((width, 3 * width), bf),
+            v((width, width), bf),
+            v((width, 4 * rank), bf),
+            v((columns, width), bf),
+            v((2 * rank, width), bf),
+            v((taps, width), bf),
+            v((8, width), f32),
+            v((edge + length, 3 * width), f32),
+            v((edge + length, share), f32),
+            v((4, length, width), bf),
+            v((length, width), bf),
+            v((length, width), f32),
+            v((length, width), bf),
+            v((edge + length, rank), bf),
+            v((4, length, rank), bf),
+        ],
+        200,
+        2 * length * width * 4 * width,
+        50_000_000,
+    )
+
+
+def ready_kernel(with_seen, *refs):
+    refs = list(refs)
+
+    def take(n):
+        return [refs.pop(0) for _ in range(n)]
+
+    place_ref, select, exits = take(3)
+    seen, entry = take(2) if with_seen else (None, None)
+    pieces = take(4)
+    grad_out, lows_out, grad_s, lows_s, sems = refs
+    share, rank = pieces[0].shape[1], select.shape[1]
+    mover = Mover(sems)
+    for r in range(4):
+        at = pl.multiple_of(jnp.bitwise_xor(place_ref[0], r) * share, 128)
+        mover.start(pieces[r], grad_s.at[:, pl.ds(at, share)])
+    if with_seen:
+        inner = product(seen[...], entry[:, pl.ds(2 * rank, 2 * rank)])
+        lows_s[1] = low(inner[:, :rank]) * select[...]
+        lows_s[2] = low(inner[:, rank:]) * select[...]
+    mover.wait()
+    mover.start(grad_s, grad_out)
+    lows_s[0] = low(product_t(grad_s[...], exits[pl.ds(rank, rank), :])) * select[...]
+    mover.start(lows_s, lows_out)
+    mover.wait()
+
+
+def ready(place_ids, select, exits, pieces, seen=None, entry=None):
+    length, share = pieces[0].shape
+    rank = select.shape[1]
+    more = [] if seen is None else [seen, entry]
+    count = 3 if more else 1
+    bf = jnp.bfloat16
+    return kernel_call(
+        functools.partial(ready_kernel, bool(more)),
+        "ready",
+        [place_ids, select, exits, *more, *pieces],
+        "svv" + "v" * len(more) + "aaaa",
+        [shaped((length, 4 * share)), shaped((count, length, rank))],
+        [pltpu.VMEM((length, 4 * share), bf), pltpu.VMEM((count, length, rank), bf)],
+        8,
+        2 * length * 4 * share * rank * count,
+        6_000_000,
+    )
+
+
+FAR_FLIPS = (0, 2, 1, 3)
+
+
+def feed_kernel(far, add_tokens, add_grads, settle, size, which, *refs):
+    refs = list(refs)
+
+    def take(n):
+        return [refs.pop(0) for _ in range(n)]
+
+    (quarter_ref,) = take(1) if far else (None,)
+    seen, lows, grad, backs = take(4)
+    low_gate, low_up, low_back = lows.at[which], lows.at[which + 1], backs.at[0]
+    weights = take(4 if far else 6)
+    down_prior, back_prior = take(2) if add_tokens else (None, None)
+    (grads_prior,) = take(1) if add_grads else (None,)
+    down_out, back_out, grads_out = take(3)
+    gate_w, up_w, down_w, act_s, gg_s, gu_s, down_s, back_s, grads_s, sems = refs
+    width, rank, units = seen.shape[1], low_gate.shape[1], gate_w.shape[0]
+    whole, side = pl.ds(0, width), pl.ds(width, rank)
+    steps = spans(units, size)
+    quarter_rows = units // 4
+    mover = Mover(sems)
+    loads = []
+    if far:
+        for n, ref in enumerate(weights):
+            rows = pl.ds(n * quarter_rows, quarter_rows)
+            for i, dst in enumerate((gate_w, up_w, down_w)):
+                loads.append((n * quarter_rows, mover.start(ref.at[i], dst.at[rows])))
+    else:
+        for at, n in steps:
+            rows = pl.ds(at, n)
+            for i, dst in enumerate((gate_w, up_w, down_w)):
+                loads.append((at, mover.start(weights[2 * i].at[rows], dst.at[rows, whole])))
+                loads.append((at, mover.start(weights[2 * i + 1].at[rows], dst.at[rows, side])))
+
+    for at, n in steps:
+        while loads and loads[0][0] < at + n:
+            mover.wait([loads.pop(0)[1]])
+        cols = pl.ds(at, n)
+        gate = product_t(seen[...], gate_w[cols, whole]) + product_t(low_gate[...], gate_w[cols, side])
+        up = product_t(seen[...], up_w[cols, whole]) + product_t(low_up[...], up_w[cols, side])
+        ga = product_t(grad[...], down_w[cols, whole]) + product_t(low_back[...], down_w[cols, side])
+        sigma = jax.nn.sigmoid(gate)
+        swish = gate * sigma
+        act_s[:, cols] = low(swish * up)
+        gu_s[:, cols] = low(ga * swish)
+        gg_s[:, cols] = low(ga * up * (sigma + swish * (1.0 - sigma)))
+
+    for i, (left, right) in enumerate(((low_gate, gg_s), (low_up, gu_s), (low_back, act_s))):
+        turned, lanes = left[...].T, pl.ds(i * rank, rank)
+
+        def grad_tile(at, n):
+            cols = pl.ds(at, n)
+            total = product(turned, right[:, cols]).T
+            if add_grads:
+                total += grads_prior[cols, lanes]
+            grads_s[cols, lanes] = total
+
+        each_tile(units, 512, grad_tile)
+    if settle:
+        for n, flip in enumerate(FAR_FLIPS):
+            at = jnp.bitwise_xor(quarter_ref[0], flip)
+            mover.start(grads_s.at[pl.ds(n * quarter_rows, quarter_rows)], grads_out.at[at])
+    else:
+        mover.start(grads_s, grads_out)
+
+    def back_tile(at, n):
+        cols = pl.ds(at, n)
+        total = product(gg_s[...], gate_w[:, cols]) + product(gu_s[...], up_w[:, cols])
+        if add_tokens:
+            total += wide_value(back_prior[:, cols])
+        back_s[:, cols] = low(total)
+
+    each_tile(width, 512, back_tile)
+    for i, (left, right) in enumerate(((gg_s, gate_w), (gu_s, up_w))):
+        total = product(left[...], right[:, side])
+        cols = pl.ds(width + i * rank, rank)
+        if add_tokens:
+            total += wide_value(back_prior[:, cols])
+        back_s[:, cols] = low(total)
+    mover.start(back_s, back_out)
+
+    def down_tile(at, n):
+        cols = pl.ds(at, n)
+        total = product(act_s[...], down_w[:, cols])
+        if add_tokens:
+            total += wide_value(down_prior[:, cols])
+        down_s[:, cols] = low(total)
+
+    each_tile(width + rank, 512, down_tile)
+    mover.start(down_s, down_out)
+    mover.wait()
+
+
+def feed(tokens, which, weights, quarter=None, add_tokens=None, add_grads=None, settle=False, size=512):
+    far = quarter is not None
+    length, width = tokens[0].shape
+    rank = tokens[1].shape[2]
+    units = 4 * weights[0].shape[1] if far else weights[0].shape[0]
+    bf, f32 = jnp.bfloat16, jnp.float32
+    args = ([quarter] if far else []) + list(tokens) + list(weights)
+    kinds = ("s" if far else "") + "v" * 4 + "a" * len(weights)
+    for prior in (add_tokens or (), () if add_grads is None else (add_grads,)):
+        args += list(prior)
+        kinds += "v" * len(prior)
+    shapes = [(length, width + rank), (length, width + 2 * rank), (units, 3 * rank)]
+    kept = [bf, bf, f32]
+    outs = [shaped(*pair) for pair in zip(shapes, kept)]
+    if settle:
+        outs[2] = shaped((4, units // 4, 3 * rank), f32)
+    return kernel_call(
+        functools.partial(feed_kernel, far, add_tokens is not None, add_grads is not None, settle, size, which),
+        "feed_far" if far else "feed_near",
+        args,
+        kinds,
+        outs,
+        [pltpu.VMEM((units, width + rank), bf)] * 3
+        + [pltpu.VMEM((length, units), bf)] * 3
+        + [pltpu.VMEM(*pair) for pair in zip(shapes, kept)],
+        40,
+        12 * length * units * (width + 2 * rank),
+        30_000_000,
+    )
+
+
+def branch_kernel(plan, *refs):
+    refs = list(refs)
+
+    def take(n):
+        return [refs.pop(0) for _ in range(n)]
+
+    place_ref, came, mine, hidden, grad, two, gated, lows, select, gain_two, entry, exits = take(12)
+    kept, out_own = take(2)
+    pieces = take(len(plan))
+    grad_hidden_out, filtered_out, gates_out, edge_out, wide_out = take(5)
+    out_s, kept_s, w_s, gb_s, lo_s, gf_s, gate_s, edge_s, wide_s, sems = refs
+    length, width = hidden.shape
+    share, rank = width // 4, select.shape[1]
+    mover = Mover(sems)
+    located = [(ref, r, piece_index(place_ref, kind, flip), Pack(width, share, rank, PACK_COUNT[kind]), flip) for ref, (r, kind, flip) in zip(pieces, plan)]
+    start_out(mover, [], out_own, located, out_s, width, share)
+    mover.start(kept.at[1], kept_s.at[0])
+    mover.start(kept.at[3], kept_s.at[1])
+    loads = list(mover.pending)
+    side = pl.ds(width, 2 * rank)
+    inner = wide_value(came[:, side]) + wide_value(mine[:, side])
+    lo_s[0] = low(inner[:, :rank]) * select[...]
+    lo_s[1] = low(inner[:, rank:]) * select[...]
+
+    def combine(at, n):
+        cols = pl.ds(at, n)
+        total = wide_value(came[:, cols]) + wide_value(mine[:, cols])
+        total += product_t(lo_s[0], entry[cols, pl.ds(2 * rank, rank)])
+        total += product_t(lo_s[1], entry[cols, pl.ds(3 * rank, rank)])
+        w_s[:, cols] = total * gain_two[:, cols]
+
+    each_tile(width, width // 3, combine)
+
+    def norm(at, n):
+        rows = pl.ds(at, n)
+        h, w = hidden[rows, :], w_s[rows, :]
+        scale = lax.rsqrt(jnp.sum(h * h, 1, keepdims=True) / width + EPS)
+        moment = jnp.sum(w * h, 1, keepdims=True) / width
+        value = wide_value(grad[rows, :]) + scale * w - h * (scale * scale * scale * moment)
+        w_s[rows, :] = value
+        gb_s[rows, :] = low(value)
+
+    each_tile(length, 32, norm)
+    mover.start(w_s, grad_hidden_out)
+    lo_s[2] = low(product_t(gb_s[...], exits[pl.ds(0, rank), :])) * select[...]
+    mover.wait(loads)
+    for r in range(4):
+        cols = pl.ds(r * share, share)
+        rows = pl.ds(pl.multiple_of(jnp.bitwise_xor(place_ref[0], r) * share, 128), share)
+        gg = product_t(gb_s[...], out_s[cols, :]) + product_t(lo_s[2], entry[rows, pl.ds(rank, rank)])
+        gf = gg * wide_value(kept_s[0, :, cols])
+        gf_s[:, cols] = low(gf)
+        edge_s[:, cols] = gf[:8]
+        gate_s[:, cols] = low(gg * wide_value(kept_s[1, :, cols]))
+    mover.start(gf_s, filtered_out)
+    mover.start(gate_s, gates_out)
+    mover.start(edge_s, edge_out)
+    for i, (left, right) in enumerate(((lo_s.at[0], two), (lo_s.at[1], two), (lows.at[1], gb_s), (lo_s.at[2], gated))):
+        turned = left[...].T
+
+        def wide_tile(at, n):
+            cols = pl.ds(at, n)
+            wide_s[i, :, cols] = low(product(turned, right[:, cols]))
+
+        each_tile(width, width // 3, wide_tile)
+        for r in range(4):
+            at = r * share if i == 3 else pl.multiple_of(jnp.bitwise_xor(place_ref[0], r) * share, 128)
+            mover.start(wide_s.at[i, :, pl.ds(at, share)], wide_out.at[r, i])
+    mover.wait()
+
+
+def branch_back(place_ids, small, kept, own, pieces):
+    length, width = small[2].shape
+    share, rank = width // 4, small[6].shape[2]
+    bf, f32, v = jnp.bfloat16, jnp.float32, pltpu.VMEM
+    return kernel_call(
+        functools.partial(branch_kernel, [p[1:] for p in pieces]),
+        "branch_back",
+        [place_ids, *small, kept, own, *[p[0] for p in pieces]],
+        "s" + "v" * len(small) + "a" * (2 + len(pieces)),
+        [
+            shaped((length, width), f32),
+            shaped((length, width)),
+            shaped((length, width)),
+            shaped((8, width), f32),
+            shaped((4, 4, rank, share)),
+        ],
+        [
+            v((width, width), bf),
+            v((2, length, width), bf),
+            v((length, width), f32),
+            v((length, width), bf),
+            v((3, length, rank), bf),
+            v((length, width), bf),
+            v((length, width), bf),
+            v((8, width), f32),
+            v((4, rank, width), bf),
+        ],
+        80,
+        2 * length * width * width + 8 * length * rank * width,
+        40_000_000,
+    )
+
+
+def input_kernel(plan, *refs):
+    refs = list(refs)
+
+    def take(n):
+        return [refs.pop(0) for _ in range(n)]
+
+    place_ref, filtered, gates, tail, taps, prev, grad_hidden, tokens, normed, lows, select, gain_one, entry, column = take(14)
+    kept, in_own = take(2)
+    pieces = take(len(plan))
+    grad_out, wide_out = take(2)
+    in_s, kept_s, near_s, far_s, gp_s, w_s, gi_s, lo_s, wide_s, entry_s, sems = refs
+    length, width = filtered.shape
+    share, rank = width // 4, select.shape[1]
+    mover = Mover(sems)
+    first = [mover.start(kept.at[0], kept_s.at[0]), mover.start(kept.at[2], kept_s.at[1])]
+    loads = []
+    located = [(ref, r, piece_index(place_ref, kind, flip), Pack(width, share, rank, PACK_COUNT[kind]), flip) for ref, (r, kind, flip) in zip(pieces, plan)]
+    start_in(mover, loads, in_own, located, in_s, width, share)
+    mover.wait(first)
+    for r in range(4):
+        lanes = pl.ds(r * share, share)
+        tap = [taps[pl.ds(i, 1), lanes] for i in range(3)]
+        for at, n in spans(length, 128):
+            rows = pl.ds(at, n)
+            value = wide_value(filtered[rows, lanes])
+            near_s[rows, :] = tap[1] * (prev[rows, pl.ds(0, 1)] * value)
+            far_s[rows, :] = tap[0] * (prev[rows, pl.ds(1, 1)] * value)
+        near_s[pl.ds(length, 8), :] = jnp.zeros((8, share), jnp.float32)
+        far_s[pl.ds(length, 8), :] = tail[:, lanes]
+        for at, n in spans(length, 128):
+            rows = pl.ds(at, n)
+            mixed = tap[2] * wide_value(filtered[rows, lanes]) + near_s[pl.ds(at + 1, n), :] + far_s[pl.ds(at + 2, n), :]
+            gp_s[rows, pl.ds(r * share, share)] = low(mixed * wide_value(kept_s[1, rows, lanes]))
+            gp_s[rows, pl.ds(2 * width + r * share, share)] = low(mixed * wide_value(kept_s[0, rows, lanes]))
+    gp_s[:, pl.ds(width, width)] = gates[...]
+    inner = 0.0
+    for i in range(3):
+        inner = inner + product_t(gp_s[:, pl.ds(i * width, width)], column[pl.ds(i * rank, rank), :])
+    lo_s[...] = low(inner) * select[...]
+    turned = lows[0].T
+    turned_back = lo_s[...].T
+
+    def exit_tile(at, n):
+        cols = pl.ds(at, n)
+        wide_s[:, cols] = low(product(turned, gp_s[:, cols]))
+
+    each_tile(3 * width, width // 3, exit_tile)
+
+    def entry_tile(at, n):
+        cols = pl.ds(at, n)
+        entry_s[:, cols] = low(product(turned_back, normed[:, cols]))
+
+    each_tile(width, width // 3, entry_tile)
+    for r in range(4):
+        at = pl.multiple_of(jnp.bitwise_xor(place_ref[0], r) * share, 128)
+        mover.start(entry_s.at[:, pl.ds(at, share)], wide_out.at[r, 0])
+        for i in range(3):
+            mover.start(wide_s.at[:, pl.ds(i * width + r * share, share)], wide_out.at[r, 1 + i])
+    mover.wait(loads)
+
+    def back(at, n):
+        cols = pl.ds(at, n)
+        total = product_t(gp_s[...], in_s[cols, :]) + product_t(lo_s[...], entry[cols, pl.ds(0, rank)])
+        w_s[:, cols] = total * gain_one[:, cols]
+
+    each_tile(width, width // 3, back)
+
+    def norm(at, n):
+        rows = pl.ds(at, n)
+        x, w = wide_value(tokens[rows, :]), w_s[rows, :]
+        scale = lax.rsqrt(jnp.sum(x * x, 1, keepdims=True) / width + EPS)
+        moment = jnp.sum(w * x, 1, keepdims=True) / width
+        gi_s[rows, :] = low(grad_hidden[rows, :] + scale * w - x * (scale * scale * scale * moment))
+
+    each_tile(length, 32, norm)
+    for r in range(4):
+        at = pl.multiple_of(jnp.bitwise_xor(place_ref[0], r) * share, 128)
+        mover.start(gi_s.at[:, pl.ds(at, share)], grad_out.at[r])
+    mover.wait()
+
+
+def input_back(place_ids, small, kept, own, pieces):
+    length, width = small[0].shape
+    share, rank = width // 4, small[9].shape[1]
+    bf, f32, v = jnp.bfloat16, jnp.float32, pltpu.VMEM
+    return kernel_call(
+        functools.partial(input_kernel, [p[1:] for p in pieces]),
+        "input_back",
+        [place_ids, *small, kept, own, *[p[0] for p in pieces]],
+        "s" + "v" * len(small) + "a" * (2 + len(pieces)),
+        [shaped((4, length, share)), shaped((4, 4, rank, share))],
+        [
+            v((width, 3 * width), bf),
+            v((2, length, width), bf),
+            v((length + 8, share), f32),
+            v((length + 8, share), f32),
+            v((length, 3 * width), bf),
+            v((length, width), f32),
+            v((length, width), bf),
+            v((length, rank), bf),
+            v((rank, 3 * width), bf),
+            v((rank, width), bf),
+        ],
+        64,
+        6 * length * width * width,
+        40_000_000,
+    )
+
+
+def swap(value, axis, bit):
+    return lax.ppermute(value, axis, [(i, i ^ bit) for i in range(lax.axis_size(axis))])
+
+
+def after(value, *others):
+    return lax.optimization_barrier((value, others))[0]
+
+
+def place(relative, me):
+    stacked = jnp.stack(relative)
+    return [lax.dynamic_index_in_dim(stacked, a ^ me, 0, keepdims=False) for a in range(len(relative))]
+
+
+def part_of(block, dim, index, count):
+    rows = block.shape[dim] // count
+    return lax.dynamic_slice_in_dim(block, index * rows, rows, dim)
+
+
+def seq_step(value, bit):
+    return low(wide_value(value) + wide_value(swap(value, "seq", bit)))
+
+
+def seq_total(value, bits=None):
+    for bit in bits or [2**k for k in range(1, 16) if 2**k < lax.axis_size("seq")]:
+        value = seq_step(value, bit)
+    return value
+
+
+def chip_half(value, dim, core):
+    other = swap(low(part_of(value, dim, 1 - core, 2)), "seq", 1)
+    return low(wide_value(part_of(value, dim, core, 2)) + wide_value(other))
+
+
+def own_block(chip):
+    total = wide_value(chip[0])
+    for r in (3, 1, 2):
+        total = total + wide_value(swap(chip[r], "mp", r))
+    return low(total)
+
+
+def both_halves(own, core):
+    return wide_value(jnp.concatenate(place([own, swap(own, "seq", 1)], core), 0))
+
+
+def fast_local(
+    inputs,
+    cotangent,
+    mixer_gain,
+    in_weight,
+    in_entry,
+    in_exit,
+    conv_weight,
+    out_weight,
+    out_entry,
+    out_exit,
+    ffn_gain,
+    gate_weight,
+    gate_entry,
+    gate_exit,
+    up_weight,
+    up_entry,
+    up_exit,
+    down_weight,
+    down_entry,
+    down_exit,
+    doc_starts,
+    adapter_ids,
+):
+    seqs, length, share = inputs.shape
+    width = 4 * share
+    rank = in_entry.shape[1]
+    units = gate_weight.shape[1]
+    m = lax.axis_index("mp")
+    s = lax.axis_index("seq")
+    x, y, core, quarter = m % 2, m // 2, s % 2, s % 4
+    place_ids = jnp.stack([m, core, quarter]).astype(jnp.int32)
+    halo = 16
+
+    def block_for(stack, r):
+        return lax.dynamic_index_in_dim(stack, m ^ r, 0, keepdims=False)
+
+    in_slabs = in_weight.swapaxes(0, 1)
+    own_taps = jnp.pad(conv_weight, ((0, TAP_ROWS - 3), (0, 0)))
+    entries = (in_entry, out_entry, gate_entry, up_entry)
+    sides = (in_exit.swapaxes(0, 1), out_exit, down_exit)
+    quarter_pack, half_pack, *own_blocks = pack_first(
+        place_ids, inputs, in_slabs, out_weight, entries, sides, own_taps
+    )
+    from_g = swap(quarter_pack, "mp", 3)
+    from_y = swap(quarter_pack, "mp", 2)
+    from_x = swap(half_pack, "mp", 1)
+    blocks = [own_blocks[0]] + [swap(own_blocks[r], "mp", r) for r in (1, 2, 3)]
+    head = from_behind(jnp.stack([b[length - halo :] for b in blocks]), "seq", 1)
+    over_g, over_y = swap(from_g, "seq", 2), swap(from_y, "seq", 2)
+    pieces = []
+    for r, got, over in ((3, from_g, over_g), (2, from_y, over_y)):
+        pieces += [(got, r, "quarter", 0), (swap(got, "seq", 1), r, "quarter", 1)]
+        pieces += [(over, r, "quarter", 2), (swap(over, "seq", 1), r, "quarter", 3)]
+    pieces += [(from_x, 1, "half", 0), (swap(from_x, "seq", 1), 1, "half", 1)]
+
+    near = [gate_weight.T, gate_exit.T, up_weight.T, up_exit.T, down_weight, down_entry]
+    first_rows = units // 8 // 16 * 16 + 16
+    cuts = ((0, first_rows), (first_rows, units // 4 - first_rows))
+    ct_own, ct_other, ct_row, *packed = pack_second(after(place_ids, quarter_pack), cotangent, near, cuts)
+
+    came_row = swap(after(ct_row, from_y), "mp", 2)
+    came_own, came_other = came_row[0], came_row[1]
+    mine_pieces = [ct_own, swap(ct_other, "mp", 1), came_own, swap(came_other, "mp", 1)]
+    other_pieces = [ct_other, swap(ct_own, "mp", 1), came_other, swap(came_own, "mp", 1)]
+    far_first = [swap(after(p, from_y), "mp", 2) for p in packed]
+
+    starts = jnp.stack([doc_starts[m], doc_starts[m ^ 1]])[:, None, :]
+    ids = jnp.stack([adapter_ids[m], adapter_ids[m ^ 1]])
+    steps = (ids - jnp.pad(ids, ((0, 0), (1, 0)))[:, :-1])[:, None, :]
+    position = (s * length - halo + jnp.arange(halo + length, dtype=jnp.int32))[None, :, None]
+    adapter = jnp.sum(jnp.where(starts <= position, steps, 0), 2)
+    lane = jnp.arange(rank, dtype=jnp.int32) // RANK
+    select_ext = (adapter[:, :, None] == lane).astype(jnp.bfloat16)
+    select = select_ext[:, halo:]
+    begins = jnp.any(starts[0] == position[0], 1).astype(jnp.float32)
+    prev_one = 1.0 - begins[halo:]
+    prev_two = prev_one * (1.0 - begins[halo - 1 : halo - 1 + length])
+    prev = jnp.stack([prev_one, prev_two], 1)
+    gain_one = wide_value(mixer_gain)[None]
+    gain_two = wide_value(ffn_gain)[None]
+
+    kept, gated, tokens, normed, hidden, normed_two, lows, entry_full, column_full, exit_full, taps = mixer(
+        place_ids,
+        (select_ext[0], prev, gain_one, gain_two),
+        (head, in_slabs, out_weight, *entries, *sides, own_taps),
+        blocks,
+        pieces,
+    )
+    normed_next = swap(normed_two, "mp", 1)
+    grad_mine, back_low_mine = ready(place_ids, select[0], exit_full, mine_pieces)
+    grad_other, lows_other = ready(place_ids, select[1], exit_full, other_pieces, normed_next, entry_full)
+    mine = (normed_two, lows, grad_mine, back_low_mine), 2
+    other = (normed_next, lows_other, grad_other, lows_other), 1
+    at_quarter = jnp.full((1,), quarter, jnp.int32)
+
+    def spread(first, then, last):
+        over = swap(after(first, then), "seq", 2)
+        return [first, over, swap(after(first, last), "seq", 1), swap(after(over, last), "seq", 1)]
+
+    near_mine = feed(*mine, near)
+    near_next = feed(*other, near, add_grads=near_mine[2])
+    far_zero = spread(far_first[0], near_mine[2], near_next[2])
+    next_zero = feed(*other, far_zero, at_quarter, add_tokens=near_next[:2])
+    mine_zero = feed(*mine, far_zero, at_quarter, add_tokens=near_mine[:2], add_grads=next_zero[2], settle=True)
+    far_one = spread(far_first[1], near_next[2], next_zero[2])
+    down_next, back_next, grads_one = feed(*other, far_one, at_quarter, add_tokens=next_zero[:2])
+    got_back = swap(back_next, "mp", 1)
+    down_mine, back_mine, grads_one = feed(
+        *mine, far_one, at_quarter, add_tokens=mine_zero[:2], add_grads=grads_one, settle=True
+    )
+    far_grads = jnp.concatenate([mine_zero[2], grads_one], 1).reshape(units, 3 * rank)
+    unit_chip = chip_half(jnp.stack([near_next[2], far_grads]), 1, core)
+
+    grad_hidden, grad_filtered, grad_gates, top_rows, wide_one = branch_back(
+        place_ids,
+        (got_back, after(back_mine, unit_chip), hidden, grad_mine, normed_two, gated, lows, select[0], gain_two, entry_full, exit_full),
+        kept,
+        out_weight,
+        pieces,
+    )
+    unit_came = after(swap(unit_chip[1], "mp", 2), top_rows)
+    unit_own = low(wide_value(unit_chip[0]) + wide_value(unit_came))
+
+    down_mine, down_next = after((down_mine, down_next), grad_hidden)
+    inner = jnp.stack([down_mine[:, width:], down_next[:, width:]])
+    inner_got = swap(inner, "mp", 1)
+    low_down = low(wide_value(inner) + wide_value(inner_got[::-1])) * select
+
+    def quarter_stack(value):
+        return jnp.stack([value[:, i * share : (i + 1) * share] for i in range(4)])
+
+    stack_mine = quarter_stack(hidden + wide_value(down_mine[:, :width]))
+    stack_next = quarter_stack(down_next[:, :width])
+    sent = [block_for(stack_mine, 1), block_for(stack_mine, 3), block_for(stack_next, 1), block_for(stack_next, 3)]
+    came = swap(after(jnp.stack([low(v) for v in sent]), back_mine), "mp", 1)
+
+    near_row = taps[1] * prev_one[:2, None] * top_rows[:2]
+    far_row = taps[0] * prev_two[:2, None] * top_rows[:2]
+    edge = jnp.concatenate([far_row[:1], near_row[:1] + far_row[1:], jnp.zeros((6, width), jnp.float32)], 0)
+    came_edge = from_behind(edge, "seq", -1)
+    down_exit_grad = low(contract(low_down[0], grad_mine, 0, 0))
+    exit_parts = quarter_stack(down_exit_grad)
+    wide_one = jnp.concatenate([wide_one, jnp.stack([block_for(exit_parts, r) for r in range(4)])[:, None]], 1)
+    chip_one = chip_half(wide_one.reshape(4, 5 * rank, share), 1, core)
+    grad_blocks, wide_two = input_back(
+        place_ids,
+        (grad_filtered, grad_gates, after(came_edge, unit_own, chip_one), taps, prev, grad_hidden, tokens, normed, lows, select[0], gain_one, entry_full, column_full),
+        kept,
+        in_slabs,
+        pieces,
+    )
+    grad_rows = [grad_blocks[0]] + [swap(grad_blocks[r], "mp", r) for r in (1, 2, 3)]
+    grad_inputs = wide_value(jnp.stack(place(grad_rows, m)))
+    chip_two = chip_half(wide_two.reshape(4, 4 * rank, share), 1, core)
+    wide_own = jnp.concatenate([own_block(chip_one), own_block(chip_two)], 0)
+    unit_own, wide_own = seq_total(unit_own), seq_total(wide_own)
+    unit_grads = both_halves(unit_own, core)
+    cut = 5 * rank // 2
+    wide_one = both_halves(wide_own[:cut], core).reshape(5, rank, share)
+    wide_two = both_halves(wide_own[cut:], core).reshape(4, rank, share)
+
+    came = wide_value(after(came, grad_blocks))
+    exit_stack = quarter_stack(exit_full[rank:])
+    results = []
+    for i, r in ((0, 0), (1, 2)):
+        for t, stack in ((0, stack_mine), (1, stack_next)):
+            tail = product(low_down[t], block_for(exit_stack, r))
+            results.append(low(wide_value(block_for(stack, r)) + came[2 * (1 - t) + i] + tail))
+    kept_rows = jnp.stack(place(results[:2], x))
+    sent_rows = jnp.stack(place(results[2:], x))
+    output = jnp.concatenate(place([kept_rows, swap(sent_rows, "mp", 2)], y), 0)
+    return (
+        output,
+        grad_inputs,
+        wide_two[0].T,
+        wide_two[1:].swapaxes(0, 1),
+        wide_one[3].T,
+        wide_one[2],
+        wide_one[0].T,
+        unit_grads[:, :rank].T,
+        wide_one[1].T,
+        unit_grads[:, rank : 2 * rank].T,
+        unit_grads[:, 2 * rank :],
+        wide_one[4],
+    )
+
+
 def solution(mesh):
+    fast = mesh.shape["mp"] == 4 and mesh.shape["seq"] % 4 == 0
     return jax.shard_map(
-        local,
+        fast_local if fast else general_local,
         mesh=mesh,
         in_specs=(
             P(None, "seq", "mp"),

time: 1500 us -> 623 us (0.42)
  blocking collectives: 601 us -> 0 us
  matrix products: 276 us -> 1.45 us
  Pallas kernels: 0 us -> 252 us
  waiting for transfers between devices: 450 us -> 251 us
  starting transfers between devices: 4.33 us -> 54.8 us
  other arithmetic: 73.4 us -> 24.6 us
  local copies, waits for them, and re-layouts: 67.3 us -> 29.7 us
    psum x9 -> x0, blocking collectives: 601 us -> none  [the longest x7 580 us: mid_total(): return lax.psum(parts, 'mp')]
    psum x2 -> x0, waiting for transfers between devices: 280 us -> none  [the longest x1 217 us: local(): lax.psum(lax.dynamic_update_slice_in_dim(partial_value, own, column, 1),...]
    pallas_call x0 -> x13, Pallas kernels: none -> 252 us  [kernel_call(): pl.pallas_call(body, out_shape=tuple(outs), in_specs=[pl.BlockSpec(memory...]
    ppermute x0 -> x51, waiting for transfers between devices: none -> 251 us  [swap(): lax.ppermute(value, axis, [(i, i ^ bit) for i in range(lax.axis_size(axis...]
    dot_general x25 -> x1, matrix products: 158 us -> 0.4 us  [contract(): lax.dot_general(left, right, (((left_dim,), (right_extent,)), ((), ())),...]
    reduce_scatter x3 -> x0, waiting for transfers between devices: 127 us -> none  [share_total(): lax.psum_scatter(partial_value, 'mp', scatter_dimension=1, tiled=True)]
    dot_general x16 -> x4, matrix products: 118 us -> 1.05 us  [product(): return jnp.dot(left, right, preferred_element_type=jnp.float32)]
    ppermute x0 -> x51, starting transfers between devices: none -> 52.2 us  [swap(): lax.ppermute(value, axis, [(i, i ^ bit) for i in range(lax.axis_size(axis...]
  transfers between devices with their start and end apart: 10 -> 53, of which waited for: 8 -> 21; matrix products, arithmetic and copies ran while one was open for 13% -> 6% of each run, Pallas kernels for 0% -> 33%
where the time goes in v2:
time: 623 us; the launch traced here: 616 us
  Pallas kernels  252 us (40%)
  waiting for transfers between devices  251 us (40%)
  starting transfers between devices  54.8 us (9%)
  local copies, waits for them, and re-layouts  29.7 us (5%)
  other arithmetic  24.6 us (4%)
    pallas_call x13, Pallas kernels, kernel_call(): pl.pallas_call(body, out_shape=tuple(outs), in_specs=[pl.BlockSpec(memory...  252 us
    ppermute x51, waiting for transfers between devices, swap(): lax.ppermute(value, axis, [(i, i ^ bit) for i in range(lax.axis_size(axis...  251 us
    ppermute x51, starting transfers between devices, swap(): lax.ppermute(value, axis, [(i, i ^ bit) for i in range(lax.axis_size(axis...  52.2 us
  transfers between devices with their start and end apart: 53, of which 21 were waited for; matrix products, arithmetic and copies ran while one was open for 6% of the time, Pallas kernels for 33%

profile of v2, /device:TPU:0, one launch (start us, length us, event | category | flops | bytes accessed | tf_op | source)
XLA Modules:
  0.0 615.9 jit_solution(13464187667886681716)
XLA Ops:
  2.6 6.6 %pack_first.1 = (bf16[1904,384]{1,0:T(8,128)(2,1)}, bf16[3792,384]{1,0:T(8,128)(2,1)}, bf16[512,384]{1,0:T(8,128)(2,1)}, bf16[512,384]{1,0:T(8,128)(2,1)}, bf16[...) custom-call(s32[3]{0:T(128)} %pad_add_fusion.2.place_ref.refs_0_, bf16[4,512,384]{2,1,0:T(8,128)(2,1)} %inputs.1, ...), custom_call_target="tpu_custom_call" | custom-call | bytes 16000000 | tf_op jit(solution)/shard_map/pack_first/pallas_call | solution.py:341
  9.2 3.0 collective-permute-start.12
  17.3 30.1 %collective-permute-done.8.refs_24_.refs_18_.refs_20_ = bf16[1904,384]{1,0:T(8,128)(2,1)} collective-permute-done((bf16[1904,384]{1,0:T(8,128)(2,1)}, bf16[1904,384]{1,0:T(8,128)(2,1)}, u32[]{:S(2)}, u32[]{:S(2)}) %collective-permute-start.8) | collective-permute-done | bytes 1462304 | tf_op jit(solution)/shard_map/ppermute | solution.py:1001
  49.0 60.3 %collective-permute-done.4.refs_20_.refs_14_.refs_16_ = bf16[1904,384]{1,0:T(8,128)(2,1)} collective-permute-done((bf16[1904,384]{1,0:T(8,128)(2,1)}, bf16[1904,384]{1,0:T(8,128)(2,1)}, u32[]{:S(2)}, u32[]{:S(2)}) %collective-permute-start.4) | collective-permute-done | bytes 1462304 | tf_op jit(solution)/shard_map/ppermute | solution.py:1001
  111.0 6.6 %pack_second.1 = (bf16[512,384]{1,0:T(8,128)(2,1)}, bf16[512,384]{1,0:T(8,128)(2,1)}, bf16[2,512,384]{2,1,0:T(8,128)(2,1)}, bf16[3,224,1664]{2,1,0:T(8,128)(2,1)}, bf16[3,208,1664]{2,1,0:T(8,128)(2,1)}) custom-call(s32[3]{0:T(128)} %pad_add_fusion.2.place_ref.refs_0_, bf16[4,512,384]{2,1,0:T(8,128)(2,1)} %cotangent.1, bf16[1728,1536]{1,0:T(8,128)(2,1)} %bitcast.203, ...), custom_call_target="tpu_custom_call" | custom-call | bytes 20000000 | tf_op jit(solution)/shard_map/pack_second/pallas_call | solution.py:341
  122.8 7.9 %collective-permute-done.2.refs_19_ = bf16[512,384]{1,0:T(8,128)(2,1)S(1)} collective-permute-done((bf16[512,384]{1,0:T(8,128)(2,1)S(1)}, bf16[512,384]{1,0:T(8,128)(2,1)S(1)}, u32[]{:S(2)}, u32[]{:S(2)}) %collective-permute-start.2) | collective-permute-done | bytes 393248 | tf_op jit(solution)/shard_map/ppermute | solution.py:1001
  134.1 4.2 collective-permute-start.9
  138.3 9.2 %collective-permute-done.15 = bf16[2,512,384]{2,1,0:T(8,128)(2,1)} collective-permute-done((bf16[2,512,384]{2,1,0:T(8,128)(2,1)}, bf16[2,512,384]{2,1,0:T(8,128)(2,1)}, u32[]{:S(2)}, u32[]{:S(2)}) %collective-permute-start.15) | collective-permute-done | bytes 786464 | tf_op jit(solution)/shard_map/ppermute | solution.py:1001
  155.3 31.0 %mixer.1 = (bf16[4,512,1536]{2,1,0:T(8,128)(2,1)}, bf16[512,1536]{1,0:T(8,128)(2,1)}, bf16[512,1536]{1,0:T(8,128)(2,1)}, bf16[512,1536]{1,0:T(8,128)(2,1)}, f32[...) custom-call(s32[3]{0:T(128)} %pad_add_fusion.2.place_ref.refs_0_, ...), custom_call_target="tpu_custom_call" | custom-call | flops 9663676416 | bytes 50000000 | tf_op jit(solution)/shard_map/mixer/pallas_call | solution.py:341
  188.1 3.9 ready.2
  192.0 33.3 %feed_near.2 = (bf16[512,1664]{1,0:T(8,128)(2,1)}, bf16[512,1792]{1,0:T(8,128)(2,1)}, f32[1728,384]{1,0:T(8,128)}) custom-call(bf16[512,1536]{1,0:T(8,128)(2,1)} %get-tuple-element.87.refs_0_.refs_1_.refs_5_, bf16[4,512,128]{2,1,0:T(8,128)(2,1)} %get-tuple-element.88.refs_1_.refs_2_.refs_7_.refs_9_, ...), custom_call_target="tpu_custom_call" | custom-call | flops 19025362944 | bytes 30000000 | tf_op jit(solution)/shard_map/feed_near/pallas_call | solution.py:341
  228.8 8.9 %collective-permute-done.19.refs_6_ = bf16[512,384]{1,0:T(8,128)(2,1)S(1)} collective-permute-done((bf16[512,384]{1,0:T(8,128)(2,1)S(1)}, bf16[512,384]{1,0:T(8,128)(2,1)S(1)}, u32[]{:S(2)}, u32[]{:S(2)}) %collective-permute-start.19) | collective-permute-done | bytes 393248 | tf_op jit(solution)/shard_map/ppermute | solution.py:1001
  237.7 7.0 %collective-permute-done.20.refs_8_ = bf16[512,384]{1,0:T(8,128)(2,1)S(1)} collective-permute-done((bf16[512,384]{1,0:T(8,128)(2,1)S(1)}, bf16[512,384]{1,0:T(8,128)(2,1)S(1)}, u32[]{:S(2)}, u32[]{:S(2)}) %collective-permute-start.20) | collective-permute-done | bytes 393248 | tf_op jit(solution)/shard_map/ppermute | solution.py:1001
  246.0 5.3 ready.3
  251.4 34.2 %feed_near.3 = (bf16[512,1664]{1,0:T(8,128)(2,1)}, bf16[512,1792]{1,0:T(8,128)(2,1)}, f32[1728,384]{1,0:T(8,128)}) custom-call(bf16[512,1536]{1,0:T(8,128)(2,1)} %copy-done.16, bf16[3,512,128]{2,1,0:T(8,128)(2,1)} %get-tuple-element.100.refs_1_.refs_3_.refs_2_.refs_4_, bf16[512,1536]{1,0:T(8,128)(2,1)} %get-tuple-element.101.refs_2_.refs_3_, ...), custom_call_target="tpu_custom_call" | custom-call | flops 19025362944 | bytes 30000000 | tf_op jit(solution)/shard_map/feed_near/pallas_call | solution.py:341
  290.2 3.2 collective-permute-done.25.refs_8_
  294.9 21.6 %feed_far.4 = (bf16[512,1664]{1,0:T(8,128)(2,1)}, bf16[512,1792]{1,0:T(8,128)(2,1)}, f32[896,384]{1,0:T(8,128)}) custom-call(s32[1]{0:T(128)} %bitcast.2.refs_0_, bf16[512,1536]{1,0:T(8,128)(2,1)} %copy-done.16, bf16[3,512,128]{2,1,0:T(8,128)(2,1)} %get-tuple-element.100.refs_1_.refs_3_.refs_2_.refs_4_, ...), custom_call_target="tpu_custom_call" | custom-call | flops 9865003008 | bytes 30000000 | tf_op jit(solution)/shard_map/feed_far/pallas_call | solution.py:341
  316.5 17.2 %collective-permute-done.21.refs_6_ = bf16[3,208,1664]{2,1,0:T(8,128)(2,1)} collective-permute-done((bf16[3,208,1664]{2,1,0:T(8,128)(2,1)}, bf16[3,208,1664]{2,1,0:T(8,128)(2,1)}, u32[]{:S(2)}, u32[]{:S(2)}) %collective-permute-start.21) | collective-permute-done | bytes 2076704 | tf_op jit(solution)/shard_map/ppermute | solution.py:1001
  334.2 22.1 %feed_far.5 = (bf16[512,1664]{1,0:T(8,128)(2,1)}, bf16[512,1792]{1,0:T(8,128)(2,1)}, f32[4,224,384]{2,1,0:T(8,128)}) custom-call(s32[1]{0:T(128)} %bitcast.2.refs_0_, bf16[512,1536]{1,0:T(8,128)(2,1)} %get-tuple-element.87.refs_0_.refs_1_.refs_5_, bf16[4,512,128]{2,1,0:T(8,128)(2,1)} %get-tuple-element.88.refs_1_.refs_2_.refs_7_.refs_9_, ...), custom_call_target="tpu_custom_call" | custom-call | flops 9865003008 | bytes 30000000 | tf_op jit(solution)/shard_map/feed_far/pallas_call | solution.py:341
  357.7 21.4 %feed_far.6 = (bf16[512,1664]{1,0:T(8,128)(2,1)}, bf16[512,1792]{1,0:T(8,128)(2,1)}, f32[832,384]{1,0:T(8,128)}) custom-call(s32[1]{0:T(128)} %bitcast.2.refs_0_, bf16[512,1536]{1,0:T(8,128)(2,1)} %copy-done.16, bf16[3,512,128]{2,1,0:T(8,128)(2,1)} %get-tuple-element.100.refs_1_.refs_3_.refs_2_.refs_4_, ...), custom_call_target="tpu_custom_call" | custom-call | flops 9160359936 | bytes 30000000 | tf_op jit(solution)/shard_map/feed_far/pallas_call | solution.py:341
  379.1 21.5 %feed_far.7 = (bf16[512,1664]{1,0:T(8,128)(2,1)}, bf16[512,1792]{1,0:T(8,128)(2,1)}, f32[4,208,384]{2,1,0:T(8,128)}) custom-call(s32[1]{0:T(128)} %bitcast.2.refs_0_, bf16[512,1536]{1,0:T(8,128)(2,1)} %get-tuple-element.87.refs_0_.refs_1_.refs_5_, bf16[4,512,128]{2,1,0:T(8,128)(2,1)} %get-tuple-element.88.refs_1_.refs_2_.refs_7_.refs_9_, ...), custom_call_target="tpu_custom_call" | custom-call | flops 9160359936 | bytes 30000000 | tf_op jit(solution)/shard_map/feed_far/pallas_call | solution.py:341
  410.7 36.1 %collective-permute-done.28.refs_1_ = bf16[512,1792]{1,0:T(8,128)(2,1)} collective-permute-done((bf16[512,1792]{1,0:T(8,128)(2,1)}, bf16[512,1792]{1,0:T(8,128)(2,1)}, u32[]{:S(2)}, u32[]{:S(2)}) %collective-permute-start.28) | collective-permute-done | bytes 1835040 | tf_op jit(solution)/shard_map/ppermute | solution.py:1001
  446.8 19.1 %branch_back.1 = (f32[512,1536]{1,0:T(8,128)}, bf16[512,1536]{1,0:T(8,128)(2,1)}, bf16[512,1536]{1,0:T(8,128)(2,1)}, f32[8,1536]{1,0:T(8,128)}, bf16[4,4,128,384]{3,2,1,0:T(8,128)(2,1)}) custom-call(s32[3]{0:T(128)} %pad_add_fusion.2.place_ref.refs_0_, bf16[512,1792]{1,0:T(8,128)(2,1)} %collective-permute-done.28.refs_1_, ...), custom_call_target="tpu_custom_call" | custom-call | flops 3221225472 | bytes 40000000 | tf_op jit(solution)/shard_map/branch_back/pallas_call | solution.py:341
  474.6 4.0 collective-permute-done.33
  484.3 5.7 collective-permute-done.50
  498.9 25.3 %input_back.1 = (bf16[4,512,384]{2,1,0:T(8,128)(2,1)}, bf16[4,4,128,384]{3,2,1,0:T(8,128)(2,1)}) custom-call(s32[3]{0:T(128)} %pad_add_fusion.2.place_ref.refs_0_, bf16[512,1536]{1,0:T(8,128)(2,1)} %get-tuple-element.135.refs_1_, bf16[512,1536]{1,0:T(8,128)(2,1)} %get-tuple-element.136.refs_2_, f32[8,1536]{1,0:T(8,128)} %copy-done.25, ...), custom_call_target="tpu_custom_call" | custom-call | flops 7247757312 | bytes 40000000 | tf_op jit(solution)/shard_map/input_back/pallas_call | solution.py:341
  536.6 3.9 collective-permute-done.38
  541.0 7.5 %collective-permute-done.37 = bf16[512,384]{1,0:T(8,128)(2,1)S(1)} collective-permute-done((bf16[512,384]{1,0:T(8,128)(2,1)S(1)}, bf16[512,384]{1,0:T(8,128)(2,1)S(1)}, u32[]{:S(2)}, u32[]{:S(2)}) %collective-permute-start.37) | collective-permute-done | bytes 393248 | tf_op jit(solution)/shard_map/ppermute | solution.py:1001
  555.9 3.1 collective-permute-done.43
  559.0 14.8 %collective-permute-done.45 = bf16[256,384]{1,0:T(8,128)(2,1)S(1)} collective-permute-done((bf16[256,384]{1,0:T(8,128)(2,1)S(1)}, bf16[256,384]{1,0:T(8,128)(2,1)S(1)}, u32[]{:S(2)}, u32[]{:S(2)}) %collective-permute-start.45) | collective-permute-done | bytes 196640 | tf_op jit(solution)/shard_map/ppermute | solution.py:1001
  576.3 9.8 %collective-permute-done.46 = bf16[576,384]{1,0:T(8,128)(2,1)S(1)} collective-permute-done((bf16[576,384]{1,0:T(8,128)(2,1)S(1)}, bf16[576,384]{1,0:T(8,128)(2,1)S(1)}, u32[]{:S(2)}, u32[]{:S(2)}) %collective-permute-start.46) | collective-permute-done | bytes 442400 | tf_op jit(solution)/shard_map/ppermute | solution.py:1001
  589.9 18.1 %collective-permute-done.47 = bf16[576,384]{1,0:T(8,128)(2,1)S(1)} collective-permute-done((bf16[576,384]{1,0:T(8,128)(2,1)S(1)}, bf16[576,384]{1,0:T(8,128)(2,1)S(1)}, u32[]{:S(2)}, u32[]{:S(2)}) %collective-permute-start.47) | collective-permute-done | bytes 442400 | tf_op jit(solution)/shard_map/ppermute | solution.py:1001
  (262 shorter events, 107.8 us)
Async XLA Ops:
  9.2 101.7 %collective-permute-start.12 = (bf16[3792,384]{1,0:T(8,128)(2,1)}, bf16[3792,384]{1,0:T(8,128)(2,1)S(1)}, u32[]{:S(2)}, u32[]{:S(2)}) collective-permute-start(bf16[3792,384]{1,0:T(8,128)(2,1)} %get-tuple-element.85), channel_id=1, source_target_pairs={{0,1},{1,0},{2,3},{3,2},{4,5},{5,4},{6,7},{7,6},{8,9},{9,8},{10,11... | collective-permute-start | bytes 8736776 | tf_op jit(solution)/shard_map/ppermute | solution.py:1001
  12.2 35.3 %collective-permute-start.8 = (bf16[1904,384]{1,0:T(8,128)(2,1)}, bf16[1904,384]{1,0:T(8,128)(2,1)}, u32[]{:S(2)}, u32[]{:S(2)}) collective-permute-start(bf16[1904,384]{1,0:T(8,128)(2,1)} %get-tuple-element.84), channel_id=1, source_target_pairs={{0,2},{1,3},{2,0},{3,1},{4,6},{5,7},{6,4},{7,5},{8,10},{9,11},{10,... | collective-permute-start | bytes 4386824 | tf_op jit(solution)/shard_map/ppermute | solution.py:1001
  13.7 95.6 %collective-permute-start.4 = (bf16[1904,384]{1,0:T(8,128)(2,1)}, bf16[1904,384]{1,0:T(8,128)(2,1)}, u32[]{:S(2)}, u32[]{:S(2)}) collective-permute-start(bf16[1904,384]{1,0:T(8,128)(2,1)} %get-tuple-element.84), channel_id=1, source_target_pairs={{0,3},{1,2},{2,1},{3,0},{4,7},{5,6},{6,5},{7,4},{8,11},{9,10},{10,... | collective-permute-start | bytes 4386824 | tf_op jit(solution)/shard_map/ppermute | solution.py:1001
  13.7 104.6 %collective-permute-start = (bf16[512,384]{1,0:T(8,128)(2,1)}, bf16[512,384]{1,0:T(8,128)(2,1)}, u32[]{:S(2)}, u32[]{:S(2)}) collective-permute-start(bf16[512,384]{1,0:T(8,128)(2,1)} %get-tuple-element.81), channel_id=1, source_target_pairs={{0,1},{1,0},{2,3},{3,2},{4,5},{5,4},{6,7},{7,6},{8,9},{9,8},{10,11... | collective-permute-start | bytes 1179656 | tf_op jit(solution)/shard_map/ppermute | solution.py:1001
  15.7 104.2 %collective-permute-start.1 = (bf16[512,384]{1,0:T(8,128)(2,1)}, bf16[512,384]{1,0:T(8,128)(2,1)}, u32[]{:S(2)}, u32[]{:S(2)}) collective-permute-start(bf16[512,384]{1,0:T(8,128)(2,1)} %get-tuple-element.82), channel_id=1, source_target_pairs={{0,2},{1,3},{2,0},{3,1},{4,6},{5,7},{6,4},{7,5},{8,10},{9,11},{10,... | collective-permute-start | bytes 1179656 | tf_op jit(solution)/shard_map/ppermute | solution.py:1001
  47.5 100.0 %collective-permute-start.10 = (bf16[1904,384]{1,0:T(8,128)(2,1)}, bf16[1904,384]{1,0:T(8,128)(2,1)}, u32[]{:S(2)}, u32[]{:S(2)}) collective-permute-start(bf16[1904,384]{1,0:T(8,128)(2,1)} %collective-permute-done.8.refs_24_.refs_18_.refs_20_), channel_id=1, source_target_pairs={{0,8},{4,12},{8,0},{12,4},{16,24},{20,28},{24,16},{28,20},{1,9},{5... | collective-permute-start | bytes 4386824 | tf_op jit(solution)/shard_map/ppermute | solution.py:1001
  109.3 38.7 %collective-permute-start.6 = (bf16[1904,384]{1,0:T(8,128)(2,1)}, bf16[1904,384]{1,0:T(8,128)(2,1)}, u32[]{:S(2)}, u32[]{:S(2)}) collective-permute-start(bf16[1904,384]{1,0:T(8,128)(2,1)} %collective-permute-done.4.refs_20_.refs_14_.refs_16_), channel_id=1, source_target_pairs={{0,8},{4,12},{8,0},{12,4},{16,24},{20,28},{24,16},{28,20},{1,9},{5... | collective-permute-start | bytes 4386824 | tf_op jit(solution)/shard_map/ppermute | solution.py:1001
  110.9 44.4 %collective-permute-start.13 = (bf16[3792,384]{1,0:T(8,128)(2,1)S(1)}, bf16[3792,384]{1,0:T(8,128)(2,1)}, u32[]{:S(2)}, u32[]{:S(2)}) collective-permute-start(bf16[3792,384]{1,0:T(8,128)(2,1)S(1)} %collective-permute-done.12.refs_28_.refs_22_.refs_24_), channel_id=1, source_target_pairs={{0,4},{4,0},{8,12},{12,8},{16,20},{20,16},{24,28},{28,24},{1,5},{5... | collective-permute-start | bytes 8736776 | tf_op jit(solution)/shard_map/ppermute | solution.py:1001
  119.8 27.7 %collective-permute-start.15 = (bf16[2,512,384]{2,1,0:T(8,128)(2,1)}, bf16[2,512,384]{2,1,0:T(8,128)(2,1)}, u32[]{:S(2)}, u32[]{:S(2)}) collective-permute-start(bf16[2,512,384]{2,1,0:T(8,128)(2,1)} %get-tuple-element.94), channel_id=1, source_target_pairs={{0,2},{1,3},{2,0},{3,1},{4,6},{5,7},{6,4},{7,5},{8,10},{9,11},{10,... | collective-permute-start | bytes 2359304 | tf_op jit(solution)/shard_map/ppermute | solution.py:1001
  151.9 35.4 %collective-permute-start.14 = (bf16[512,384]{1,0:T(8,128)(2,1)S(1)}, bf16[512,384]{1,0:T(8,128)(2,1)S(1)}, u32[]{:S(2)}, u32[]{:S(2)}) collective-permute-start(bf16[512,384]{1,0:T(8,128)(2,1)S(1)} %copy-done.20), channel_id=1, source_target_pairs={{0,1},{1,0},{2,3},{3,2},{4,5},{5,4},{6,7},{7,6},{8,9},{9,8},{10,11... | collective-permute-start | bytes 1179656 | tf_op jit(solution)/shard_map/ppermute | solution.py:1001
  153.0 72.3 %collective-permute-start.22 = (bf16[3,224,1664]{2,1,0:T(8,128)(2,1)}, bf16[3,224,1664]{2,1,0:T(8,128)(2,1)}, u32[]{:S(2)}, u32[]{:S(2)}) collective-permute-start(bf16[3,224,1664]{2,1,0:T(8,128)(2,1)} %get-tuple-element.106), channel_id=1, source_target_pairs={{0,2},{1,3},{2,0},{3,1},{4,6},{5,7},{6,4},{7,5},{8,10},{9,11},{10,... | collective-permute-start | bytes 6709256 | tf_op jit(solution)/shard_map/ppermute | solution.py:1001
  154.0 33.4 %collective-permute-start.16 = (bf16[512,384]{1,0:T(8,128)(2,1)S(1)}, bf16[512,384]{1,0:T(8,128)(2,1)}, u32[]{:S(2)}, u32[]{:S(2)}) collective-permute-start(bf16[512,384]{1,0:T(8,128)(2,1)S(1)} %get-tuple-element.244.refs_7_), channel_id=1, source_target_pairs={{0,1},{1,0},{2,3},{3,2},{4,5},{5,4},{6,7},{7,6},{8,9},{9,8},{10,11... | collective-permute-start | bytes 1179656 | tf_op jit(solution)/shard_map/ppermute | solution.py:1001
  186.3 58.5 %collective-permute-start.18 = (bf16[512,1536]{1,0:T(8,128)(2,1)}, bf16[512,1536]{1,0:T(8,128)(2,1)S(1)}, u32[]{:S(2)}, u32[]{:S(2)}) collective-permute-start(bf16[512,1536]{1,0:T(8,128)(2,1)} %get-tuple-element.87.refs_0_.refs_1_.refs_5_), channel_id=1, source_target_pairs={{0,1},{1,0},{2,3},{3,2},{4,5},{5,4},{6,7},{7,6},{8,9},{9,8},{10,11... | collective-permute-start | bytes 4718600 | tf_op jit(solution)/shard_map/ppermute | solution.py:1001
  225.3 60.4 %collective-permute-start.23 = (bf16[3,224,1664]{2,1,0:T(8,128)(2,1)}, bf16[3,224,1664]{2,1,0:T(8,128)(2,1)}, u32[]{:S(2)}, u32[]{:S(2)}) collective-permute-start(bf16[3,224,1664]{2,1,0:T(8,128)(2,1)} %collective-permute-done.22.refs_5_), channel_id=1, source_target_pairs={{0,8},{4,12},{8,0},{12,4},{16,24},{20,28},{24,16},{28,20},{1,9},{5... | collective-permute-start | bytes 6709256 | tf_op jit(solution)/shard_map/ppermute | solution.py:1001
  227.7 58.5 %collective-permute-start.17 = (bf16[3,208,1664]{2,1,0:T(8,128)(2,1)}, bf16[3,208,1664]{2,1,0:T(8,128)(2,1)}, u32[]{:S(2)}, u32[]{:S(2)}) collective-permute-start(bf16[3,208,1664]{2,1,0:T(8,128)(2,1)} %get-tuple-element.98), channel_id=1, source_target_pairs={{0,2},{1,3},{2,0},{3,1},{4,6},{5,7},{6,4},{7,5},{8,10},{9,11},{10,... | collective-permute-start | bytes 6230024 | tf_op jit(solution)/shard_map/ppermute | solution.py:1001
  286.2 47.5 %collective-permute-start.21 = (bf16[3,208,1664]{2,1,0:T(8,128)(2,1)}, bf16[3,208,1664]{2,1,0:T(8,128)(2,1)}, u32[]{:S(2)}, u32[]{:S(2)}) collective-permute-start(bf16[3,208,1664]{2,1,0:T(8,128)(2,1)} %collective-permute-done.17.refs_5_), channel_id=1, source_target_pairs={{0,8},{4,12},{8,0},{12,4},{16,24},{20,28},{24,16},{28,20},{1,9},{5... | collective-permute-start | bytes 6230024 | tf_op jit(solution)/shard_map/ppermute | solution.py:1001
  333.7 22.7 %collective-permute-start.26 = (bf16[3,208,1664]{2,1,0:T(8,128)(2,1)}, bf16[3,208,1664]{2,1,0:T(8,128)(2,1)S(1)}, u32[]{:S(2)}, u32[]{:S(2)}) collective-permute-start(bf16[3,208,1664]{2,1,0:T(8,128)(2,1)} %collective-permute-done.17.refs_5_), channel_id=1, source_target_pairs={{0,4},{4,0},{8,12},{12,8},{16,20},{20,16},{24,28},{28,24},{1,5},{5... | collective-permute-start | bytes 6230024 | tf_op jit(solution)/shard_map/ppermute | solution.py:1001
  333.7 22.7 %collective-permute-start.27 = (bf16[3,208,1664]{2,1,0:T(8,128)(2,1)}, bf16[3,208,1664]{2,1,0:T(8,128)(2,1)}, u32[]{:S(2)}, u32[]{:S(2)}) collective-permute-start(bf16[3,208,1664]{2,1,0:T(8,128)(2,1)} %collective-permute-done.21.refs_6_), channel_id=1, source_target_pairs={{0,4},{4,0},{8,12},{12,8},{16,20},{20,16},{24,28},{28,24},{1,5},{5... | collective-permute-start | bytes 6230024 | tf_op jit(solution)/shard_map/ppermute | solution.py:1001
  404.1 42.7 %collective-permute-start.28 = (bf16[512,1792]{1,0:T(8,128)(2,1)}, bf16[512,1792]{1,0:T(8,128)(2,1)}, u32[]{:S(2)}, u32[]{:S(2)}) collective-permute-start(bf16[512,1792]{1,0:T(8,128)(2,1)} %get-tuple-element.124), channel_id=1, source_target_pairs={{0,1},{1,0},{2,3},{3,2},{4,5},{5,4},{6,7},{7,6},{8,9},{9,8},{10,11... | collective-permute-start | bytes 5505032 | tf_op jit(solution)/shard_map/ppermute | solution.py:1001
  409.7 61.4 %collective-permute-start.32 = (bf16[864,384]{1,0:T(8,128)(2,1)S(1)}, bf16[864,384]{1,0:T(8,128)(2,1)S(1)}, u32[]{:S(2)}, u32[]{:S(2)}) collective-permute-start(bf16[864,384]{1,0:T(8,128)(2,1)S(1)} %slice_bitcast_fusion.6), channel_id=1, source_target_pairs={{0,2},{1,3},{2,0},{3,1},{4,6},{5,7},{6,4},{7,5},{8,10},{9,11},{10,... | collective-permute-start | bytes 1990664 | tf_op jit(solution)/shard_map/ppermute | solution.py:1001
  468.1 26.6 %collective-permute-start.31 = (f32[8,1536]{1,0:T(8,128)S(1)}, f32[8,1536]{1,0:T(8,128)S(1)}, u32[]{:S(2)}, u32[]{:S(2)}) collective-permute-start(f32[8,1536]{1,0:T(8,128)S(1)} %maximum_maximum_fusion), channel_id=1, source_target_pairs={{4,0},{8,4},{12,8},{16,12},{20,16},{24,20},{28,24},{5,1},{9,5},{13... | collective-permute-start | bytes 147464 | tf_op jit(solution)/shard_map/ppermute | solution.py:21
  483.2 49.7 %collective-permute-start.30 = (bf16[4,512,384]{2,1,0:T(8,128)(2,1)}, bf16[4,512,384]{2,1,0:T(8,128)(2,1)}, u32[]{:S(2)}, u32[]{:S(2)}) collective-permute-start(bf16[4,512,384]{2,1,0:T(8,128)(2,1)} %pad_maximum_fusion.4), channel_id=1, source_target_pairs={{0,1},{1,0},{2,3},{3,2},{4,5},{5,4},{6,7},{7,6},{8,9},{9,8},{10,11... | collective-permute-start | bytes 4718600 | tf_op jit(solution)/shard_map/ppermute | solution.py:1001
  491.0 35.0 %collective-permute-start.51 = (bf16[864,384]{1,0:T(8,128)(2,1)}, bf16[864,384]{1,0:T(8,128)(2,1)}, u32[]{:S(2)}, u32[]{:S(2)}) collective-permute-start(bf16[864,384]{1,0:T(8,128)(2,1)} %add_convert_fusion.3), channel_id=1, source_target_pairs={{0,16},{4,20},{8,24},{12,28},{16,0},{20,4},{24,8},{28,12},{1,17},{... | collective-permute-start | bytes 1990664 | tf_op jit(solution)/shard_map/ppermute | solution.py:1001
  495.4 32.2 %collective-permute-start.39 = (bf16[320,384]{1,0:T(8,128)(2,1)}, bf16[320,384]{1,0:T(8,128)(2,1)S(1)}, u32[]{:S(2)}, u32[]{:S(2)}) collective-permute-start(bf16[320,384]{1,0:T(8,128)(2,1)} %get-tuple-element.230), channel_id=1, source_target_pairs={{0,3},{1,2},{2,1},{3,0},{4,7},{5,6},{6,5},{7,4},{8,11},{9,10},{10,... | collective-permute-start | bytes 737288 | tf_op jit(solution)/shard_map/ppermute | solution.py:1001
  496.8 32.3 %collective-permute-start.41 = (bf16[320,384]{1,0:T(8,128)(2,1)}, bf16[320,384]{1,0:T(8,128)(2,1)}, u32[]{:S(2)}, u32[]{:S(2)}) collective-permute-start(bf16[320,384]{1,0:T(8,128)(2,1)} %get-tuple-element.231), channel_id=1, source_target_pairs={{0,2},{1,3},{2,0},{3,1},{4,6},{5,7},{6,4},{7,5},{8,10},{9,11},{10,... | collective-permute-start | bytes 737288 | tf_op jit(solution)/shard_map/ppermute | solution.py:1001
  497.9 32.8 %collective-permute-start.40 = (bf16[320,384]{1,0:T(8,128)(2,1)}, bf16[320,384]{1,0:T(8,128)(2,1)}, u32[]{:S(2)}, u32[]{:S(2)}) collective-permute-start(bf16[320,384]{1,0:T(8,128)(2,1)} %get-tuple-element.232), channel_id=1, source_target_pairs={{0,1},{1,0},{2,3},{3,2},{4,5},{5,4},{6,7},{7,6},{8,9},{9,8},{10,11... | collective-permute-start | bytes 737288 | tf_op jit(solution)/shard_map/ppermute | solution.py:1001
  526.0 22.8 %collective-permute-start.42 = (bf16[4,256,384]{2,1,0:T(8,128)(2,1)S(1)}, bf16[4,256,384]{2,1,0:T(8,128)(2,1)S(1)}, u32[]{:S(2)}, u32[]{:S(2)}) collective-permute-start(bf16[4,256,384]{2,1,0:T(8,128)(2,1)S(1)} %constant_dynamic-slice_fusion), channel_id=1, source_target_pairs={{0,4},{4,0},{8,12},{12,8},{16,20},{20,16},{24,28},{28,24},{1,5},{5... | collective-permute-start | bytes 2359304 | tf_op jit(solution)/shard_map/ppermute | solution.py:1001
  532.9 42.7 %collective-permute-start.52 = (bf16[864,384]{1,0:T(8,128)(2,1)S(1)}, bf16[864,384]{1,0:T(8,128)(2,1)S(1)}, u32[]{:S(2)}, u32[]{:S(2)}) collective-permute-start(bf16[864,384]{1,0:T(8,128)(2,1)S(1)} %add_convert_fusion.2), channel_id=1, source_target_pairs={{0,4},{4,0},{8,12},{12,8},{16,20},{20,16},{24,28},{28,24},{1,5},{5... | collective-permute-start | bytes 1990664 | tf_op jit(solution)/shard_map/ppermute | solution.py:1001
  540.5 47.4 %collective-permute-start.35 = (bf16[2,512,384]{2,1,0:T(8,128)(2,1)S(1)}, bf16[2,512,384]{2,1,0:T(8,128)(2,1)S(1)}, u32[]{:S(2)}, u32[]{:S(2)}) collective-permute-start(bf16[2,512,384]{2,1,0:T(8,128)(2,1)S(1)} %pad_maximum_fusion.7), channel_id=1, source_target_pairs={{0,2},{1,3},{2,0},{3,1},{4,6},{5,7},{6,4},{7,5},{8,10},{9,11},{10,... | collective-permute-start | bytes 2359304 | tf_op jit(solution)/shard_map/ppermute | solution.py:1001
  551.7 22.0 %collective-permute-start.45 = (bf16[256,384]{1,0:T(8,128)(2,1)S(1)}, bf16[256,384]{1,0:T(8,128)(2,1)S(1)}, u32[]{:S(2)}, u32[]{:S(2)}) collective-permute-start(bf16[256,384]{1,0:T(8,128)(2,1)S(1)} %get-tuple-element.234), channel_id=1, source_target_pairs={{0,2},{1,3},{2,0},{3,1},{4,6},{5,7},{6,4},{7,5},{8,10},{9,11},{10,... | collective-permute-start | bytes 589832 | tf_op jit(solution)/shard_map/ppermute | solution.py:1001
  552.8 21.0 %collective-permute-start.44 = (bf16[256,384]{1,0:T(8,128)(2,1)S(1)}, bf16[256,384]{1,0:T(8,128)(2,1)S(1)}, u32[]{:S(2)}, u32[]{:S(2)}) collective-permute-start(bf16[256,384]{1,0:T(8,128)(2,1)S(1)} %get-tuple-element.235), channel_id=1, source_target_pairs={{0,1},{1,0},{2,3},{3,2},{4,5},{5,4},{6,7},{7,6},{8,9},{9,8},{10,11... | collective-permute-start | bytes 589832 | tf_op jit(solution)/shard_map/ppermute | solution.py:1001
  586.2 21.7 %collective-permute-start.47 = (bf16[576,384]{1,0:T(8,128)(2,1)S(1)}, bf16[576,384]{1,0:T(8,128)(2,1)S(1)}, u32[]{:S(2)}, u32[]{:S(2)}) collective-permute-start(bf16[576,384]{1,0:T(8,128)(2,1)S(1)} %add_convert_fusion.5), channel_id=1, source_target_pairs={{0,16},{4,20},{8,24},{12,28},{16,0},{20,4},{24,8},{28,12},{1,17},{... | collective-permute-start | bytes 1327112 | tf_op jit(solution)/shard_map/ppermute | solution.py:1001
  (57 other events, 653.4 us)

commit v3 on v2

--- a/solution.py
+++ b/solution.py
@@ -317,23 +317,23 @@
     return jnp.bitwise_xor(place_ref[1 if kind == "half" else 2], flip)
 
 
-def start_in(mover, loads, own, located, target, width, share):
+def start_in(mover, loads, own, pieces, plan, place_ref, target, width, share):
     for i in range(3):
         loads.append(mover.start(own.at[i], target.at[:, pl.ds(i * width, share)]))
-    for ref, r, index, pack, _ in located:
-        rows = pl.ds(pl.multiple_of(index * pack.in_rows, 16), pack.in_rows)
+    for ref, (r, kind, flip, _) in zip(pieces, plan):
+        n = width // COUNT[kind]
+        rows = pl.ds(pl.multiple_of(piece_index(place_ref, kind, flip) * n, 16), n)
         for i in range(3):
-            source = ref.at[pl.ds(i * pack.in_rows, pack.in_rows)]
-            loads.append(mover.start(source, target.at[rows, pl.ds(i * width + r * share, share)]))
-
-
-def start_out(mover, loads, own, located, target, width, share):
+            loads.append(mover.start(ref.at[pl.ds(i * n, n)], target.at[rows, pl.ds(i * width + r * share, share)]))
+
+
+def start_out(mover, loads, own, pieces, plan, place_ref, target, share):
     loads.append(mover.start(own, target.at[pl.ds(0, share)]))
-    for ref, r, index, pack, _ in located:
-        rows = pl.ds(pl.multiple_of(r * share + index * pack.out_rows, 16), pack.out_rows)
+    for ref, (r, kind, flip, base) in zip(pieces, plan):
+        n = share // COUNT[kind]
+        rows = pl.ds(pl.multiple_of(r * share + piece_index(place_ref, kind, flip) * n, 16), n)
         for i in range(4):
-            source = ref.at[pl.ds(pack.out_at + i * pack.out_rows, pack.out_rows)]
-            loads.append(mover.start(source, target.at[rows, pl.ds(i * share, share)]))
+            loads.append(mover.start(ref.at[pl.ds(base + i * n, n)], target.at[rows, pl.ds(i * share, share)]))
 
 
 def kernel_call(body, name, args, kinds, outs, scratch, sems, flops, size, out_space=pl.ANY):
@@ -357,63 +357,80 @@
 TAP_ROWS = 16
 
 
-class Pack:
-    def __init__(self, width, share, rank, count):
-        self.in_rows, self.out_rows, self.side_rows = width // count, share // count, rank // count
-        self.out_at = 3 * self.in_rows
-        self.entry_at = self.out_at + 4 * self.out_rows
+class Rest:
+    def __init__(self, share, rank, count):
+        self.out_rows, self.side_rows = share // count, rank // count
+        self.entry_at = 4 * self.out_rows
         self.side_at = self.entry_at + 2 * self.out_rows
         self.tap_at = self.side_at + 5 * self.side_rows
         self.rows = self.tap_at + TAP_ROWS
 
 
-PACK_COUNT = {"half": 2, "quarter": 4}
-
-
-def pack_first_kernel(place_ref, inputs, in_weight, out_weight, *refs):
+COUNT = {"half": 2, "quarter": 4}
+
+
+def pack_in_kernel(place_ref, in_weight, out, sems):
+    rows = in_weight.shape[1] // 4
+    mover = Mover(sems)
+    for i in range(3):
+        part = pl.ds(pl.multiple_of(place_ref[2] * rows, 16), rows)
+        mover.start(in_weight.at[i, part], out.at[pl.ds(i * rows, rows)])
+    mover.wait()
+
+
+def pack_in(place_ids, in_weight):
+    _, width, share = in_weight.shape
+    return kernel_call(
+        pack_in_kernel, "pack_in", [place_ids, in_weight], "sa", [shaped((3 * width // 4, share))], [], 4, 0, 2_000_000, pltpu.VMEM
+    )[0]
+
+
+def pack_first_kernel(place_ref, inputs, cotangent, in_weight, out_weight, *refs):
     entries, (in_exit, out_exit, down_exit, taps), outs, sems = refs[:4], refs[4:8], refs[8:-1], refs[-1]
+    far, beside, below, own_block, ct_rows, ct_far = outs
     share, width = out_weight.shape
-    rank = entries[0].shape[1]
+    length, rank = inputs.shape[1], entries[0].shape[1]
     mover = Mover(sems)
-    for index, out in ((2, outs[0]), (1, outs[1])):
-        pack = Pack(width, share, rank, 4 if index == 2 else 2)
-
-        def part(rows):
-            return pl.ds(pl.multiple_of(place_ref[index] * rows, 16), rows)
-
-        for i in range(3):
-            mover.start(in_weight.at[i, part(pack.in_rows)], out.at[pl.ds(i * pack.in_rows, pack.in_rows)])
-        rows = part(pack.out_rows)
+
+    def part(index, rows):
+        return pl.ds(pl.multiple_of(place_ref[index] * rows, 16), rows)
+
+    in_rows = width // 4
+    for i in range(3):
+        mover.start(in_weight.at[i, part(2, in_rows)], far.at[pl.ds(i * in_rows, in_rows)])
+    for index, target, base in ((2, far, 3 * in_rows), (1, beside, length), (1, below, length)):
+        rest = Rest(share, rank, 4 if index == 2 else 2)
+        rows = part(index, rest.out_rows)
         for i in range(4):
-            target = out.at[pl.ds(pack.out_at + i * pack.out_rows, pack.out_rows)]
-            mover.start(out_weight.at[rows, pl.ds(i * share, share)], target)
-            target = out.at[pl.ds(pack.entry_at + i // 3 * pack.out_rows, pack.out_rows), pl.ds(i % 3 * rank, rank)]
-            mover.start(entries[i].at[rows], target)
-        rows = part(pack.side_rows)
+            spot = target.at[pl.ds(base + i * rest.out_rows, rest.out_rows)]
+            mover.start(out_weight.at[rows, pl.ds(i * share, share)], spot)
+            spot = target.at[pl.ds(base + rest.entry_at + i // 3 * rest.out_rows, rest.out_rows), pl.ds(i % 3 * rank, rank)]
+            mover.start(entries[i].at[rows], spot)
+        rows = part(index, rest.side_rows)
         for i, side in enumerate((in_exit.at[0], in_exit.at[1], in_exit.at[2], out_exit, down_exit)):
-            mover.start(side.at[rows], out.at[pl.ds(pack.side_at + i * pack.side_rows, pack.side_rows)])
-        mover.start(taps, out.at[pl.ds(pack.tap_at, TAP_ROWS)])
-    for r in range(4):
-        mover.start(inputs.at[jnp.bitwise_xor(place_ref[0], r)], outs[2 + r])
+            mover.start(side.at[rows], target.at[pl.ds(base + rest.side_at + i * rest.side_rows, rest.side_rows)])
+        mover.start(taps, target.at[pl.ds(base + rest.tap_at, TAP_ROWS)])
+    far_block = far.at[pl.ds(far.shape[0] - length, length)]
+    for r, target in enumerate((own_block, beside.at[pl.ds(0, length)], below.at[pl.ds(0, length)], far_block)):
+        index = jnp.bitwise_xor(place_ref[0], r)
+        mover.start(inputs.at[index], target)
+        mover.start(cotangent.at[index], (ct_rows, ct_far)[r // 2].at[r % 2])
     mover.wait()
 
 
-def pack_first(place_ids, inputs, in_weight, out_weight, entries, sides, taps):
+def pack_first(place_ids, inputs, cotangent, in_weight, out_weight, entries, sides, taps):
     length, share = inputs.shape[1:]
     width, rank = in_weight.shape[1], entries[0].shape[1]
-    args = [place_ids, inputs, in_weight, out_weight, *entries, *sides, taps]
-    outs = [shaped((Pack(width, share, rank, count).rows, share)) for count in (4, 2)] + [shaped((length, share))] * 4
-    return kernel_call(pack_first_kernel, "pack_first", args, "s" + "a" * 11, outs, [], 64, 0, 16_000_000, pltpu.VMEM)
-
-
-def pack_second_kernel(cuts, place_ref, cotangent, *refs):
-    near, (own, other, far_row), packs, sems = refs[:6], refs[6:9], refs[9:-1], refs[-1]
+    args = [place_ids, inputs, cotangent, in_weight, out_weight, *entries, *sides, taps]
+    in_rows = 3 * width // 4
+    heights = [in_rows + Rest(share, rank, 4).rows + length] + [length + Rest(share, rank, 2).rows] * 2 + [length]
+    outs = [shaped((n, share)) for n in heights] + [shaped((2, length, share))] * 2
+    return kernel_call(pack_first_kernel, "pack_first", args, "s" + "a" * 12, outs, [], 80, 0, 16_000_000, pltpu.VMEM)
+
+
+def pack_second_kernel(cuts, place_ref, *refs):
+    near, packs, sems = refs[:6], refs[6:-1], refs[-1]
     mover = Mover(sems)
-    mine = place_ref[0]
-    mover.start(cotangent.at[jnp.bitwise_xor(mine, 2)], far_row.at[0])
-    mover.start(cotangent.at[jnp.bitwise_xor(mine, 3)], far_row.at[1])
-    mover.start(cotangent.at[mine], own)
-    mover.start(cotangent.at[jnp.bitwise_xor(mine, 1)], other)
     quarter_rows = near[0].shape[0] // 4
     width = near[0].shape[1]
     for (at, n), pack in zip(cuts, packs):
@@ -424,16 +441,14 @@
     mover.wait()
 
 
-def pack_second(place_ids, cotangent, near, cuts):
-    length, share = cotangent.shape[1:]
-    outs = [shaped((length, share)), shaped((length, share)), shaped((2, length, share))]
-    outs += [shaped((3, n, near[0].shape[1] + near[1].shape[1])) for _, n in cuts]
+def pack_second(place_ids, near, cuts):
+    outs = [shaped((3, n, near[0].shape[1] + near[1].shape[1])) for _, n in cuts]
     return kernel_call(
-        functools.partial(pack_second_kernel, cuts), "pack_second", [place_ids, cotangent, *near], "s" + "a" * 7, outs, [], 32, 0, 20_000_000, pltpu.VMEM
-    )
-
-
-def mixer_kernel(plan, *refs):
+        functools.partial(pack_second_kernel, cuts), "pack_second", [place_ids, *near], "s" + "a" * 6, outs, [], 32, 0, 20_000_000, pltpu.VMEM
+    )
+
+
+def mixer_kernel(in_plan, rest_plan, *refs):
     refs = list(refs)
 
     def take(n):
@@ -443,7 +458,7 @@
     head, in_own, out_own, *own = take(11)
     entries_own, (in_exit, out_exit, down_exit, taps_own) = own[:4], own[4:]
     blocks = take(4)
-    pieces = take(len(plan))
+    in_pieces, rest_pieces = take(len(in_plan)), take(len(rest_plan))
     kept_out, gated_out, tokens_out, normed_out, hidden_out, two_out, lows_out, entry_out, column_out, exit_out, taps_out = take(11)
     (x_s, n_s, in_s, out_s, entry_s, col_s, exit_s, tap_s, taps_s, proj_s, mix_s) = take(11)
     kept_s, gated_s, hid_s, two_s, low_in_s, lows_s, sems = refs
@@ -456,7 +471,8 @@
 
     for r in range(4):
         lanes = pl.ds(absolute(r), share)
-        mover.start(blocks[r], x_s.at[pl.ds(edge, length), lanes])
+        first = blocks[r].shape[0] - length if r == 3 else 0
+        mover.start(blocks[r].at[pl.ds(first, length)], x_s.at[pl.ds(edge, length), lanes])
         mover.start(head.at[r], x_s.at[pl.ds(0, edge), lanes])
     token_loads = list(mover.pending)
     row_loads, column_loads, loads, out_loads = [], [], [], []
@@ -465,22 +481,21 @@
     for i, source in enumerate((in_exit.at[0], in_exit.at[1], in_exit.at[2], out_exit, down_exit)):
         column_loads.append(mover.start(source, col_s.at[pl.ds(i * rank, rank), pl.ds(0, share)]))
     column_loads.append(mover.start(taps_own, tap_s.at[:, pl.ds(0, share)]))
-    located = [(ref, r, piece_index(place_ref, kind, flip), Pack(width, share, rank, PACK_COUNT[kind]), flip) for ref, (r, kind, flip) in zip(pieces, plan)]
-    for ref, r, index, pack, flip in located:
-        rows = pl.ds(pl.multiple_of(absolute(r) + index * pack.out_rows, 16), pack.out_rows)
-        source = ref.at[pl.ds(pack.entry_at, pack.out_rows)]
+    for ref, (r, kind, flip, base) in zip(rest_pieces, rest_plan):
+        rest, index, lanes = Rest(share, rank, COUNT[kind]), piece_index(place_ref, kind, flip), pl.ds(r * share, share)
+        rows = pl.ds(pl.multiple_of(absolute(r) + index * rest.out_rows, 16), rest.out_rows)
+        source = ref.at[pl.ds(base + rest.entry_at, rest.out_rows)]
         row_loads.append(mover.start(source, entry_s.at[rows, pl.ds(0, 3 * rank)]))
-        source = ref.at[pl.ds(pack.entry_at + pack.out_rows, pack.out_rows), pl.ds(0, rank)]
+        source = ref.at[pl.ds(base + rest.entry_at + rest.out_rows, rest.out_rows), pl.ds(0, rank)]
         row_loads.append(mover.start(source, entry_s.at[rows, pl.ds(3 * rank, rank)]))
-        lanes = pl.ds(r * share, share)
         for i in range(5):
-            rows = pl.ds(pl.multiple_of(i * rank + index * pack.side_rows, 16), pack.side_rows)
-            source = ref.at[pl.ds(pack.side_at + i * pack.side_rows, pack.side_rows)]
+            rows = pl.ds(pl.multiple_of(i * rank + index * rest.side_rows, 16), rest.side_rows)
+            source = ref.at[pl.ds(base + rest.side_at + i * rest.side_rows, rest.side_rows)]
             column_loads.append(mover.start(source, col_s.at[rows, lanes]))
         if flip == 0:
-            column_loads.append(mover.start(ref.at[pl.ds(pack.tap_at, TAP_ROWS)], tap_s.at[:, lanes]))
-    start_in(mover, loads, in_own, located, in_s, width, share)
-    start_out(mover, out_loads, out_own, located, out_s, width, share)
+            column_loads.append(mover.start(ref.at[pl.ds(base + rest.tap_at, TAP_ROWS)], tap_s.at[:, lanes]))
+    start_in(mover, loads, in_own, in_pieces, in_plan, place_ref, in_s, width, share)
+    start_out(mover, out_loads, out_own, rest_pieces, rest_plan, place_ref, out_s, share)
     mover.wait(token_loads)
 
     def norm(at, n):
@@ -563,16 +578,16 @@
     mover.wait()
 
 
-def mixer(place_ids, small, own, blocks, pieces):
+def mixer(place_ids, small, own, blocks, in_pieces, rest_pieces):
     length, share = blocks[0].shape
     width, rank, edge = 4 * share, own[3].shape[1], own[0].shape[1]
     bf, f32 = jnp.bfloat16, jnp.float32
-    args = [place_ids, *small, *own, *blocks] + [p[0] for p in pieces]
+    args = [place_ids, *small, *own, *blocks] + [p[0] for p in in_pieces + rest_pieces]
     kinds = "s" + "v" * len(small) + "a" * (len(args) - 1 - len(small))
     v = pltpu.VMEM
     columns, taps = 5 * rank, TAP_ROWS
     return kernel_call(
-        functools.partial(mixer_kernel, [p[1:] for p in pieces]),
+        functools.partial(mixer_kernel, [p[1:] for p in in_pieces], [p[1:] for p in rest_pieces]),
         "mixer",
         args,
         kinds,
@@ -614,73 +629,84 @@
     )
 
 
-def ready_kernel(with_seen, *refs):
+def ready_kernel(place_ref, select, exits, rows_mine, rows_far, rows_x, rows_far_x, grad_out, back_out, grad_s, back_s, sems):
+    share, rank = rows_mine.shape[2], select.shape[2]
+    mover = Mover(sems)
+    for t in range(2):
+        for r, source in enumerate((rows_mine.at[t], rows_x.at[1 - t], rows_far.at[t], rows_far_x.at[1 - t])):
+            at = pl.multiple_of(jnp.bitwise_xor(place_ref[0], r) * share, 128)
+            mover.start(source, grad_s.at[t, :, pl.ds(at, share)])
+    mover.wait()
+    mover.start(grad_s, grad_out)
+    for t in range(2):
+        back_s[t] = low(product_t(grad_s[t], exits[pl.ds(rank, rank), :])) * select[t]
+    mover.start(back_s, back_out)
+    mover.wait()
+
+
+def ready(place_ids, select, exits, cotangents):
+    length, share = cotangents[0].shape[1:]
+    rank, width = select.shape[2], 4 * share
+    shapes = [(2, length, width), (2, length, rank)]
+    return kernel_call(
+        ready_kernel,
+        "ready",
+        [place_ids, select, exits, *cotangents],
+        "svvaaaa",
+        [shaped(v) for v in shapes],
+        [pltpu.VMEM(v, jnp.bfloat16) for v in shapes],
+        16,
+        4 * length * width * rank,
+        10_000_000,
+    )
+
+
+def lows_kernel(select, seen, entry, lows):
+    rank = select.shape[1]
+    inner = product(seen[...], entry[:, pl.ds(2 * rank, 2 * rank)])
+    lows[0] = low(inner[:, :rank]) * select[...]
+    lows[1] = low(inner[:, rank:]) * select[...]
+
+
+def lows_of(select, seen, entry):
+    length, rank = select.shape
+    return pl.pallas_call(
+        lows_kernel,
+        out_shape=shaped((2, length, rank)),
+        in_specs=[pl.BlockSpec(memory_space=pltpu.VMEM)] * 3,
+        out_specs=pl.BlockSpec(memory_space=pltpu.VMEM),
+        cost_estimate=pl.CostEstimate(flops=4 * length * rank * seen.shape[1], bytes_accessed=3_000_000, transcendentals=0),
+        compiler_params=pltpu.CompilerParams(vmem_limit_bytes=16 * 1024 * 1024),
+        name="lows",
+    )(select, seen, entry)
+
+
+FAR_FLIPS = (0, 2, 1, 3)
+
+
+def feed_kernel(far, add_tokens, add_grads, settle, sizes, which, turn, *refs):
     refs = list(refs)
 
     def take(n):
         return [refs.pop(0) for _ in range(n)]
 
-    place_ref, select, exits = take(3)
-    seen, entry = take(2) if with_seen else (None, None)
-    pieces = take(4)
-    grad_out, lows_out, grad_s, lows_s, sems = refs
-    share, rank = pieces[0].shape[1], select.shape[1]
-    mover = Mover(sems)
-    for r in range(4):
-        at = pl.multiple_of(jnp.bitwise_xor(place_ref[0], r) * share, 128)
-        mover.start(pieces[r], grad_s.at[:, pl.ds(at, share)])
-    if with_seen:
-        inner = product(seen[...], entry[:, pl.ds(2 * rank, 2 * rank)])
-        lows_s[1] = low(inner[:, :rank]) * select[...]
-        lows_s[2] = low(inner[:, rank:]) * select[...]
-    mover.wait()
-    mover.start(grad_s, grad_out)
-    lows_s[0] = low(product_t(grad_s[...], exits[pl.ds(rank, rank), :])) * select[...]
-    mover.start(lows_s, lows_out)
-    mover.wait()
-
-
-def ready(place_ids, select, exits, pieces, seen=None, entry=None):
-    length, share = pieces[0].shape
-    rank = select.shape[1]
-    more = [] if seen is None else [seen, entry]
-    count = 3 if more else 1
-    bf = jnp.bfloat16
-    return kernel_call(
-        functools.partial(ready_kernel, bool(more)),
-        "ready",
-        [place_ids, select, exits, *more, *pieces],
-        "svv" + "v" * len(more) + "aaaa",
-        [shaped((length, 4 * share)), shaped((count, length, rank))],
-        [pltpu.VMEM((length, 4 * share), bf), pltpu.VMEM((count, length, rank), bf)],
-        8,
-        2 * length * 4 * share * rank * count,
-        6_000_000,
-    )
-
-
-FAR_FLIPS = (0, 2, 1, 3)
-
-
-def feed_kernel(far, add_tokens, add_grads, settle, size, which, *refs):
-    refs = list(refs)
-
-    def take(n):
-        return [refs.pop(0) for _ in range(n)]
-
     (quarter_ref,) = take(1) if far else (None,)
-    seen, lows, grad, backs = take(4)
-    low_gate, low_up, low_back = lows.at[which], lows.at[which + 1], backs.at[0]
+    token_refs = take(4)
     weights = take(4 if far else 6)
-    down_prior, back_prior = take(2) if add_tokens else (None, None)
-    (grads_prior,) = take(1) if add_grads else (None,)
+    prior_refs = take(2 * add_tokens + add_grads)
     down_out, back_out, grads_out = take(3)
-    gate_w, up_w, down_w, act_s, gg_s, gu_s, down_s, back_s, grads_s, sems = refs
-    width, rank, units = seen.shape[1], low_gate.shape[1], gate_w.shape[0]
+    seen, lows, grad, low_back, gate_w, up_w, down_w, act_s, gg_s, gu_s, down_s, back_s, grads_s, *prior, sems = refs
+    low_gate, low_up = lows.at[0], lows.at[1]
+    width, rank, units = seen.shape[1], low_back.shape[1], gate_w.shape[0]
     whole, side = pl.ds(0, width), pl.ds(width, rank)
-    steps = spans(units, size)
+    steps = []
+    for size in sizes:
+        steps.append((sum(n for _, n in steps), size))
     quarter_rows = units // 4
     mover = Mover(sems)
+    token_refs[1] = token_refs[1].at[pl.ds(which, 2)]
+    token_refs[2], token_refs[3] = token_refs[2].at[turn], token_refs[3].at[turn]
+    token_loads = [mover.start(a, b) for a, b in zip(token_refs, (seen, lows, grad, low_back))]
     loads = []
     if far:
         for n, ref in enumerate(weights):
@@ -693,6 +719,12 @@
             for i, dst in enumerate((gate_w, up_w, down_w)):
                 loads.append((at, mover.start(weights[2 * i].at[rows], dst.at[rows, whole])))
                 loads.append((at, mover.start(weights[2 * i + 1].at[rows], dst.at[rows, side])))
+    prior_loads = [mover.start(a, b) for a, b in zip(prior_refs, prior)]
+    if add_tokens:
+        down_prior, back_prior = prior[:2]
+    if add_grads:
+        grads_prior = prior[-1]
+    mover.wait(token_loads)
 
     for at, n in steps:
         while loads and loads[0][0] < at + n:
@@ -707,6 +739,7 @@
         gu_s[:, cols] = low(ga * swish)
         gg_s[:, cols] = low(ga * up * (sigma + swish * (1.0 - sigma)))
 
+    mover.wait(prior_loads)
     for i, (left, right) in enumerate(((low_gate, gg_s), (low_up, gu_s), (low_back, act_s))):
         turned, lanes = left[...].T, pl.ds(i * rank, rank)
 
@@ -717,7 +750,7 @@
                 total += grads_prior[cols, lanes]
             grads_s[cols, lanes] = total
 
-        each_tile(units, 512, grad_tile)
+        each_tile(units, units if units < 640 else 512, grad_tile)
     if settle:
         for n, flip in enumerate(FAR_FLIPS):
             at = jnp.bitwise_xor(quarter_ref[0], flip)
@@ -753,32 +786,35 @@
     mover.wait()
 
 
-def feed(tokens, which, weights, quarter=None, add_tokens=None, add_grads=None, settle=False, size=512):
+def feed(tokens, which, turn, weights, quarter=None, add_tokens=None, add_grads=None, settle=False):
     far = quarter is not None
     length, width = tokens[0].shape
     rank = tokens[1].shape[2]
     units = 4 * weights[0].shape[1] if far else weights[0].shape[0]
-    bf, f32 = jnp.bfloat16, jnp.float32
+    sizes = [n for _, n in spans(units, 512)]
+    if len(sizes) > 1 and sizes[-1] < 256:
+        sizes[-2:] = [256, sizes[-2] + sizes[-1] - 256]
+    bf, f32, v = jnp.bfloat16, jnp.float32, pltpu.VMEM
     args = ([quarter] if far else []) + list(tokens) + list(weights)
-    kinds = ("s" if far else "") + "v" * 4 + "a" * len(weights)
-    for prior in (add_tokens or (), () if add_grads is None else (add_grads,)):
-        args += list(prior)
-        kinds += "v" * len(prior)
-    shapes = [(length, width + rank), (length, width + 2 * rank), (units, 3 * rank)]
-    kept = [bf, bf, f32]
-    outs = [shaped(*pair) for pair in zip(shapes, kept)]
+    shapes = [((length, width + rank), bf), ((length, width + 2 * rank), bf), ((units, 3 * rank), f32)]
+    prior = list(add_tokens or ()) + ([] if add_grads is None else [add_grads])
+    prior_scratch = (shapes[:2] if add_tokens else []) + ([] if add_grads is None else shapes[2:])
+    outs = [shaped(*pair) for pair in shapes]
     if settle:
         outs[2] = shaped((4, units // 4, 3 * rank), f32)
     return kernel_call(
-        functools.partial(feed_kernel, far, add_tokens is not None, add_grads is not None, settle, size, which),
+        functools.partial(
+            feed_kernel, far, add_tokens is not None, add_grads is not None, settle, tuple(sizes), which, turn
+        ),
         "feed_far" if far else "feed_near",
-        args,
-        kinds,
+        args + prior,
+        ("s" if far else "") + "a" * (4 + len(weights) + len(prior)),
         outs,
-        [pltpu.VMEM((units, width + rank), bf)] * 3
-        + [pltpu.VMEM((length, units), bf)] * 3
-        + [pltpu.VMEM(*pair) for pair in zip(shapes, kept)],
-        40,
+        [v((length, width), bf), v((2, length, rank), bf), v((length, width), bf), v((length, rank), bf)]
+        + [v((units, width + rank), bf)] * 3
+        + [v((length, units), bf)] * 3
+        + [v(*pair) for pair in shapes + prior_scratch],
+        48,
         12 * length * units * (width + 2 * rank),
         30_000_000,
     )
@@ -790,19 +826,32 @@
     def take(n):
         return [refs.pop(0) for _ in range(n)]
 
-    place_ref, came, mine, hidden, grad, two, gated, lows, select, gain_two, entry, exits = take(12)
-    kept, out_own = take(2)
+    place_ref, came, mine, hidden, grad, two, gated, lows, select, gain_two, entry, exits, taps, prev, down_mine, down_next = take(16)
+    kept, near, far_0, far_1, far_2, out_own = take(6)
     pieces = take(len(plan))
-    grad_hidden_out, filtered_out, gates_out, edge_out, wide_out = take(5)
-    out_s, kept_s, w_s, gb_s, lo_s, gf_s, gate_s, edge_s, wide_s, sems = refs
+    grad_hidden_out, filtered_out, gates_out, edge_out, keep_out, give_out, sent_out, own_out = take(8)
+    near_s, far_s, pack_s, part_s, out_s, kept_s, w_s, gb_s, lo_s, gf_s, gate_s, edge_s, wide_s, sems = refs
     length, width = hidden.shape
     share, rank = width // 4, select.shape[1]
     mover = Mover(sems)
-    located = [(ref, r, piece_index(place_ref, kind, flip), Pack(width, share, rank, PACK_COUNT[kind]), flip) for ref, (r, kind, flip) in zip(pieces, plan)]
-    start_out(mover, [], out_own, located, out_s, width, share)
+    start_out(mover, [], out_own, pieces, plan, place_ref, out_s, share)
     mover.start(kept.at[1], kept_s.at[0])
     mover.start(kept.at[3], kept_s.at[1])
     loads = list(mover.pending)
+    unit_loads = [mover.start(near, near_s)]
+    quarter_rows, at = near.shape[0] // 4, 0
+    for far in (far_0, far_1, far_2):
+        n = far.shape[1]
+        for q in range(4):
+            unit_loads.append(mover.start(far.at[q], far_s.at[pl.ds(q * quarter_rows + at, n)]))
+        at += n
+    part_s[0] = low(hidden[...] + wide_value(down_mine[:, pl.ds(0, width)]))
+    part_s[1] = down_next[:, pl.ds(0, width)]
+    for t in range(2):
+        for r in range(4):
+            lanes = pl.ds(pl.multiple_of(jnp.bitwise_xor(place_ref[0], r) * share, 128), share)
+            target = (own_out if r % 2 == 0 else sent_out).at[2 * t + r // 2]
+            mover.start(part_s.at[t, :, lanes], target)
     side = pl.ds(width, 2 * rank)
     inner = wide_value(came[:, side]) + wide_value(mine[:, side])
     lo_s[0] = low(inner[:, :rank]) * select[...]
@@ -822,7 +871,7 @@
         h, w = hidden[rows, :], w_s[rows, :]
         scale = lax.rsqrt(jnp.sum(h * h, 1, keepdims=True) / width + EPS)
         moment = jnp.sum(w * h, 1, keepdims=True) / width
-        value = wide_value(grad[rows, :]) + scale * w - h * (scale * scale * scale * moment)
+        value = wide_value(grad[0, rows, :]) + scale * w - h * (scale * scale * scale * moment)
         w_s[rows, :] = value
         gb_s[rows, :] = low(value)
 
@@ -836,12 +885,17 @@
         gg = product_t(gb_s[...], out_s[cols, :]) + product_t(lo_s[2], entry[rows, pl.ds(rank, rank)])
         gf = gg * wide_value(kept_s[0, :, cols])
         gf_s[:, cols] = low(gf)
-        edge_s[:, cols] = gf[:8]
+        first = gf[:8]
+        beside = taps[pl.ds(1, 1), cols] * (prev[pl.ds(0, 8), pl.ds(0, 1)] * first)
+        beyond = taps[pl.ds(0, 1), cols] * (prev[pl.ds(0, 8), pl.ds(1, 1)] * first)
+        edge_s[pl.ds(0, 1), cols] = beyond[0:1]
+        edge_s[pl.ds(1, 1), cols] = beside[0:1] + beyond[1:2]
+        edge_s[pl.ds(2, 6), cols] = jnp.zeros((6, share), jnp.float32)
         gate_s[:, cols] = low(gg * wide_value(kept_s[1, :, cols]))
     mover.start(gf_s, filtered_out)
     mover.start(gate_s, gates_out)
     mover.start(edge_s, edge_out)
-    for i, (left, right) in enumerate(((lo_s.at[0], two), (lo_s.at[1], two), (lows.at[1], gb_s), (lo_s.at[2], gated))):
+    for i, (left, right) in enumerate(((lo_s.at[0], two), (lo_s.at[1], two), (lows.at[1], gb_s))):
         turned = left[...].T
 
         def wide_tile(at, n):
@@ -849,29 +903,52 @@
             wide_s[i, :, cols] = low(product(turned, right[:, cols]))
 
         each_tile(width, width // 3, wide_tile)
-        for r in range(4):
-            at = r * share if i == 3 else pl.multiple_of(jnp.bitwise_xor(place_ref[0], r) * share, 128)
-            mover.start(wide_s.at[i, :, pl.ds(at, share)], wide_out.at[r, i])
+    turned = lo_s[2].T
+    for r in range(4):
+        lanes = pl.ds(pl.multiple_of(jnp.bitwise_xor(place_ref[0], r) * share, 128), share)
+        wide_s[3, :, lanes] = low(product(turned, gated[:, pl.ds(r * share, share)]))
+    mover.wait(unit_loads)
+    half = near.shape[0] // 2
+    for h, out in ((0, keep_out), (1, give_out)):
+        mine = jnp.bitwise_xor(place_ref[1], h)
+        rows = pl.ds(pl.multiple_of(mine * half, 16), half)
+        at = 0
+        for r, units in ((0, near_s), (2, far_s), (1, None), (3, None)):
+            lanes = pl.ds(pl.multiple_of(jnp.bitwise_xor(place_ref[0], r) * share, 128), share)
+            for j in range(2):
+                pack_s[h, pl.ds(at + j * rank, rank), :] = wide_s[mine * 2 + j, :, lanes]
+            at += 2 * rank
+            if units is not None:
+                pack_s[h, pl.ds(at, half), :] = low(units[rows, :])
+                at += half
+        mover.start(pack_s.at[h], out)
     mover.wait()
 
 
-def branch_back(place_ids, small, kept, own, pieces):
+def branch_back(place_ids, small, kept, units, own, pieces):
     length, width = small[2].shape
-    share, rank = width // 4, small[6].shape[2]
+    share, rank, unit_rows = width // 4, small[7].shape[1], units[0].shape[0]
     bf, f32, v = jnp.bfloat16, jnp.float32, pltpu.VMEM
     return kernel_call(
         functools.partial(branch_kernel, [p[1:] for p in pieces]),
         "branch_back",
-        [place_ids, *small, kept, own, *[p[0] for p in pieces]],
-        "s" + "v" * len(small) + "a" * (2 + len(pieces)),
+        [place_ids, *small, kept, *units, own, *[p[0] for p in pieces]],
+        "s" + "v" * len(small) + "a" * (2 + len(units) + len(pieces)),
         [
             shaped((length, width), f32),
             shaped((length, width)),
             shaped((length, width)),
             shaped((8, width), f32),
-            shaped((4, 4, rank, share)),
+            shaped((unit_rows + 8 * rank, share)),
+            shaped((unit_rows + 8 * rank, share)),
+            shaped((4, length, share)),
+            shaped((4, length, share)),
         ],
         [
+            v((unit_rows, share), f32),
+            v((unit_rows, share), f32),
+            v((2, unit_rows + 8 * rank, share), bf),
+            v((2, length, width), bf),
             v((width, width), bf),
             v((2, length, width), bf),
             v((length, width), f32),
@@ -894,18 +971,17 @@
     def take(n):
         return [refs.pop(0) for _ in range(n)]
 
-    place_ref, filtered, gates, tail, taps, prev, grad_hidden, tokens, normed, lows, select, gain_one, entry, column = take(14)
+    place_ref, filtered, gates, tail, taps, prev, grad_hidden, tokens, normed, lows, select, gain_one, entry, column, low_down, grad_down = take(16)
     kept, in_own = take(2)
     pieces = take(len(plan))
-    grad_out, wide_out = take(2)
-    in_s, kept_s, near_s, far_s, gp_s, w_s, gi_s, lo_s, wide_s, entry_s, sems = refs
+    grad_out, keep_out, give_out = take(3)
+    in_s, kept_s, near_s, far_s, gp_s, w_s, gi_s, lo_s, wide_s, entry_s, down_s, block_s, pack_s, sems = refs
     length, width = filtered.shape
     share, rank = width // 4, select.shape[1]
     mover = Mover(sems)
     first = [mover.start(kept.at[0], kept_s.at[0]), mover.start(kept.at[2], kept_s.at[1])]
     loads = []
-    located = [(ref, r, piece_index(place_ref, kind, flip), Pack(width, share, rank, PACK_COUNT[kind]), flip) for ref, (r, kind, flip) in zip(pieces, plan)]
-    start_in(mover, loads, in_own, located, in_s, width, share)
+    start_in(mover, loads, in_own, pieces, plan, place_ref, in_s, width, share)
     mover.wait(first)
     for r in range(4):
         lanes = pl.ds(r * share, share)
@@ -941,11 +1017,25 @@
         entry_s[:, cols] = low(product(turned_back, normed[:, cols]))
 
     each_tile(width, width // 3, entry_tile)
+    turned_down = low_down[0].T
+
+    def down_tile(at, n):
+        cols = pl.ds(at, n)
+        down_s[:, cols] = low(product(turned_down, grad_down[0, :, cols]))
+
+    each_tile(width, width // 3, down_tile)
+    half = 5 * rank // 2
     for r in range(4):
-        at = pl.multiple_of(jnp.bitwise_xor(place_ref[0], r) * share, 128)
-        mover.start(entry_s.at[:, pl.ds(at, share)], wide_out.at[r, 0])
+        lanes = pl.ds(pl.multiple_of(jnp.bitwise_xor(place_ref[0], r) * share, 128), share)
+        block_s[pl.ds(0, rank), :] = entry_s[:, lanes]
         for i in range(3):
-            mover.start(wide_s.at[:, pl.ds(i * width + r * share, share)], wide_out.at[r, 1 + i])
+            block_s[pl.ds((1 + i) * rank, rank), :] = wide_s[:, pl.ds(i * width + r * share, share)]
+        block_s[pl.ds(4 * rank, rank), :] = down_s[:, lanes]
+        for h in range(2):
+            rows = pl.ds(pl.multiple_of(jnp.bitwise_xor(place_ref[1], h) * half, 16), half)
+            pack_s[h, pl.ds(r * half, half), :] = block_s[rows, :]
+    mover.start(pack_s.at[0], keep_out)
+    mover.start(pack_s.at[1], give_out)
     mover.wait(loads)
 
     def back(at, n):
@@ -978,7 +1068,7 @@
         "input_back",
         [place_ids, *small, kept, own, *[p[0] for p in pieces]],
         "s" + "v" * len(small) + "a" * (2 + len(pieces)),
-        [shaped((4, length, share)), shaped((4, 4, rank, share))],
+        [shaped((4, length, share)), shaped((10 * rank, share)), shaped((10 * rank, share))],
         [
             v((width, 3 * width), bf),
             v((2, length, width), bf),
@@ -990,6 +1080,9 @@
             v((length, rank), bf),
             v((rank, 3 * width), bf),
             v((rank, width), bf),
+            v((rank, width), bf),
+            v((5 * rank, share), bf),
+            v((2, 10 * rank, share), bf),
         ],
         64,
         6 * length * width * width,
@@ -997,12 +1090,90 @@
     )
 
 
+def results_kernel(place_ref, own, came, low_down, exits, kept_out, sent_out, out_s, sems):
+    share, rank = own.shape[2], low_down.shape[2]
+    mover = Mover(sems)
+    for i, out in ((0, kept_out), (1, sent_out)):
+        lanes = pl.ds(pl.multiple_of(jnp.bitwise_xor(place_ref[0], 2 * i) * share, 128), share)
+        for t in range(2):
+            total = wide_value(own[2 * t + i]) + wide_value(came[2 * (1 - t) + i])
+            out_s[2 * i + t] = low(total + product(low_down[t], exits[pl.ds(rank, rank), lanes]))
+            mover.start(out_s.at[2 * i + t], out.at[jnp.bitwise_xor(place_ref[3], t)])
+    mover.wait()
+
+
+def results_of(place_ids, own, came, low_down, exits):
+    count, length, share = own.shape
+    return kernel_call(
+        results_kernel,
+        "results",
+        [place_ids, own, came, low_down, exits],
+        "svvvv",
+        [shaped((2, length, share))] * 2,
+        [pltpu.VMEM((count, length, share), jnp.bfloat16)],
+        8,
+        8 * length * share * low_down.shape[2],
+        8_000_000,
+    )
+
+
+def finish_kernel(place_ref, one_own, one_other, two_own, two_other, *refs):
+    in_entry, in_exit, out_entry, out_exit, gate_entry, gate_exit, up_entry, up_exit, down_entry, down_exit = refs[:10]
+    one_s, two_s, sems = refs[10:]
+    rank = in_entry.shape[1]
+    mover = Mover(sems)
+    for h, one, two in ((0, one_own, two_own), (1, one_other, two_other)):
+        at = jnp.bitwise_xor(place_ref[1], h)
+        mover.start(one, one_s.at[at])
+        mover.start(two, two_s.at[at])
+    mover.wait()
+    first, second = pl.ds(0, rank), pl.ds(rank, rank)
+    gate_entry[...] = wide_value(one_s[0, first, :]).T
+    up_entry[...] = wide_value(one_s[0, second, :]).T
+    out_exit[...] = wide_value(one_s[1, first, :])
+    out_entry[...] = wide_value(one_s[1, second, :]).T
+    half = gate_exit.shape[0] // 2
+    for h in range(2):
+        rows = pl.ds(h * half, half)
+        for i, out in enumerate((gate_exit, up_exit, down_entry)):
+            out[rows, :] = wide_value(one_s[h, pl.ds(2 * rank, half), pl.ds(i * rank, rank)])
+    cut = rank // 2
+    in_entry[...] = wide_value(two_s[0, first, :]).T
+    in_exit[0] = wide_value(two_s[0, second, :])
+    in_exit[1, pl.ds(0, cut), :] = wide_value(two_s[0, pl.ds(2 * rank, cut), :])
+    in_exit[1, pl.ds(cut, cut), :] = wide_value(two_s[1, pl.ds(0, cut), :])
+    in_exit[2] = wide_value(two_s[1, pl.ds(cut, rank), :])
+    down_exit[...] = wide_value(two_s[1, pl.ds(cut + rank, rank), :])
+
+
+def finish(place_ids, one_own, one_other, two_own, two_other, units, rank):
+    share, f32, bf = one_own.shape[1], jnp.float32, jnp.bfloat16
+    entry, exits, unit = (share, rank), (rank, share), (units, rank)
+    shapes = [entry, (3, rank, share), entry, exits, entry, unit, entry, unit, unit, exits]
+    return kernel_call(
+        finish_kernel,
+        "finish",
+        [place_ids, one_own, one_other, two_own, two_other],
+        "saaaa",
+        [shaped(v, f32) for v in shapes],
+        [pltpu.VMEM((2, *one_own.shape), bf), pltpu.VMEM((2, *two_own.shape), bf)],
+        4,
+        0,
+        8_000_000,
+        pltpu.VMEM,
+    )
+
+
 def swap(value, axis, bit):
     return lax.ppermute(value, axis, [(i, i ^ bit) for i in range(lax.axis_size(axis))])
 
 
 def after(value, *others):
     return lax.optimization_barrier((value, others))[0]
+
+
+def together(*values):
+    return lax.optimization_barrier(values)
 
 
 def place(relative, me):
@@ -1019,9 +1190,24 @@
     return low(wide_value(value) + wide_value(swap(value, "seq", bit)))
 
 
-def seq_total(value, bits=None):
-    for bit in bits or [2**k for k in range(1, 16) if 2**k < lax.axis_size("seq")]:
+def seq_bits():
+    return [2**k for k in range(1, 16) if 2**k < lax.axis_size("seq")]
+
+
+def seq_total(value):
+    for bit in seq_bits():
         value = seq_step(value, bit)
+    return value
+
+
+def seq_total_parts(value):
+    s = lax.axis_index("seq")
+    for bit in seq_bits():
+        keep = s // bit % 2
+        other = swap(part_of(value, 0, 1 - keep, 2), "seq", bit)
+        value = low(wide_value(part_of(value, 0, keep, 2)) + wide_value(other))
+    for bit in seq_bits()[::-1]:
+        value = jnp.concatenate(place([value, swap(value, "seq", bit)], s // bit % 2), 0)
     return value
 
 
@@ -1072,7 +1258,7 @@
     m = lax.axis_index("mp")
     s = lax.axis_index("seq")
     x, y, core, quarter = m % 2, m // 2, s % 2, s % 4
-    place_ids = jnp.stack([m, core, quarter]).astype(jnp.int32)
+    place_ids = jnp.stack([m, core, quarter, x]).astype(jnp.int32)
     halo = 16
 
     def block_for(stack, r):
@@ -1082,31 +1268,45 @@
     own_taps = jnp.pad(conv_weight, ((0, TAP_ROWS - 3), (0, 0)))
     entries = (in_entry, out_entry, gate_entry, up_entry)
     sides = (in_exit.swapaxes(0, 1), out_exit, down_exit)
-    quarter_pack, half_pack, *own_blocks = pack_first(
-        place_ids, inputs, in_slabs, out_weight, entries, sides, own_taps
-    )
-    from_g = swap(quarter_pack, "mp", 3)
-    from_y = swap(quarter_pack, "mp", 2)
-    from_x = swap(half_pack, "mp", 1)
-    blocks = [own_blocks[0]] + [swap(own_blocks[r], "mp", r) for r in (1, 2, 3)]
-    head = from_behind(jnp.stack([b[length - halo :] for b in blocks]), "seq", 1)
-    over_g, over_y = swap(from_g, "seq", 2), swap(from_y, "seq", 2)
-    pieces = []
-    for r, got, over in ((3, from_g, over_g), (2, from_y, over_y)):
-        pieces += [(got, r, "quarter", 0), (swap(got, "seq", 1), r, "quarter", 1)]
-        pieces += [(over, r, "quarter", 2), (swap(over, "seq", 1), r, "quarter", 3)]
-    pieces += [(from_x, 1, "half", 0), (swap(from_x, "seq", 1), 1, "half", 1)]
-
+    in_quarter = pack_in(place_ids, in_slabs)
+    far_pack, beside, below, own_block_rows, ct_rows, ct_far = pack_first(
+        after(place_ids, in_quarter), inputs, cotangent, in_slabs, out_weight, entries, sides, own_taps
+    )
     near = [gate_weight.T, gate_exit.T, up_weight.T, up_exit.T, down_weight, down_entry]
-    first_rows = units // 8 // 16 * 16 + 16
-    cuts = ((0, first_rows), (first_rows, units // 4 - first_rows))
-    ct_own, ct_other, ct_row, *packed = pack_second(after(place_ids, quarter_pack), cotangent, near, cuts)
-
-    came_row = swap(after(ct_row, from_y), "mp", 2)
-    came_own, came_other = came_row[0], came_row[1]
-    mine_pieces = [ct_own, swap(ct_other, "mp", 1), came_own, swap(came_other, "mp", 1)]
-    other_pieces = [ct_other, swap(ct_own, "mp", 1), came_other, swap(came_own, "mp", 1)]
-    far_first = [swap(after(p, from_y), "mp", 2) for p in packed]
+    count = units // 4 // 16
+    rows = (count * 3 // 10 * 16, count * 3 // 10 * 16)
+    cuts = ((0, rows[0]), (rows[0], rows[1]), (rows[0] + rows[1], units // 4 - rows[0] - rows[1]))
+
+    def spread(got, over, r, base):
+        return [
+            (got, r, "quarter", 0, base),
+            (swap(got, "seq", 1), r, "quarter", 1, base),
+            (over, r, "quarter", 2, base),
+            (swap(over, "seq", 1), r, "quarter", 3, base),
+        ]
+
+    in_x, in_y = swap(in_quarter, "mp", 1), swap(in_quarter, "mp", 2)
+    far_pack = swap(after(far_pack, in_x, in_y), "mp", 3)
+    over_x, over_y = swap(in_x, "seq", 2), swap(in_y, "seq", 2)
+    packed = pack_second(after(place_ids, in_x, in_y), near, cuts)
+    beside, below = after((beside, below), in_x, in_y)
+    beside, below = swap(beside, "mp", 1), swap(below, "mp", 2)
+    in_pieces = spread(in_x, over_x, 1, 0) + spread(in_y, over_y, 2, 0)
+    far_count = far_pack.shape[0] - length
+    far_weights = far_pack[:far_count]
+    over_far = swap(after(far_weights, [p[0] for p in in_pieces]), "seq", 2)
+    row_blocks = [own_block_rows, beside, below, far_pack]
+    ends = [length, length, length, far_pack.shape[0]]
+    head = from_behind(jnp.stack([b[e - halo : e] for b, e in zip(row_blocks, ends)]), "seq", 1)
+    far_pieces = spread(far_weights, over_far, 3, 3 * width // 4)
+    in_pieces += [p[:4] + (0,) for p in far_pieces]
+    rest_pieces = list(far_pieces)
+    for got, r in ((beside, 1), (below, 2)):
+        rest_pieces += [(got, r, "half", 0, length), (swap(got, "seq", 1), r, "half", 1, length)]
+    ct_rows, ct_far, *packed = after((ct_rows, ct_far, *packed), [p[0] for p in rest_pieces])
+    ct_x, ct_y, ct_g = swap(ct_rows, "mp", 1), swap(ct_far, "mp", 2), swap(ct_far, "mp", 3)
+    packed = [packed[0], *after(tuple(packed[1:]), ct_x)]
+    far_first = [swap(p, "mp", 2) for p in packed]
 
     starts = jnp.stack([doc_starts[m], doc_starts[m ^ 1]])[:, None, :]
     ids = jnp.stack([adapter_ids[m], adapter_ids[m ^ 1]])
@@ -1127,105 +1327,93 @@
         place_ids,
         (select_ext[0], prev, gain_one, gain_two),
         (head, in_slabs, out_weight, *entries, *sides, own_taps),
-        blocks,
-        pieces,
+        row_blocks,
+        in_pieces,
+        rest_pieces,
     )
     normed_next = swap(normed_two, "mp", 1)
-    grad_mine, back_low_mine = ready(place_ids, select[0], exit_full, mine_pieces)
-    grad_other, lows_other = ready(place_ids, select[1], exit_full, other_pieces, normed_next, entry_full)
-    mine = (normed_two, lows, grad_mine, back_low_mine), 2
-    other = (normed_next, lows_other, grad_other, lows_other), 1
+    grad_down, back_lows = ready(place_ids, select, exit_full, (ct_rows, ct_y, ct_x, ct_g))
+    lows_next = lows_of(select[1], normed_next, entry_full)
+    mine = (normed_two, lows, grad_down, back_lows), 2, 0
+    other = (normed_next, lows_next, grad_down, back_lows), 0, 1
     at_quarter = jnp.full((1,), quarter, jnp.int32)
 
-    def spread(first, then, last):
+    def spread_far(first, then, last):
         over = swap(after(first, then), "seq", 2)
         return [first, over, swap(after(first, last), "seq", 1), swap(after(over, last), "seq", 1)]
 
     near_mine = feed(*mine, near)
     near_next = feed(*other, near, add_grads=near_mine[2])
-    far_zero = spread(far_first[0], near_mine[2], near_next[2])
+    far_zero = spread_far(far_first[0], near_mine[2], near_next[2])
     next_zero = feed(*other, far_zero, at_quarter, add_tokens=near_next[:2])
     mine_zero = feed(*mine, far_zero, at_quarter, add_tokens=near_mine[:2], add_grads=next_zero[2], settle=True)
-    far_one = spread(far_first[1], near_next[2], next_zero[2])
-    down_next, back_next, grads_one = feed(*other, far_one, at_quarter, add_tokens=next_zero[:2])
+    far_one = spread_far(far_first[1], near_mine[2], next_zero[2])
+    next_one = feed(*other, far_one, at_quarter, add_tokens=next_zero[:2])
+    far_two = spread_far(far_first[2], near_next[2], mine_zero[2])
+    down_next, back_next, next_grads = feed(*other, far_two, at_quarter, add_tokens=next_one[:2])
     got_back = swap(back_next, "mp", 1)
-    down_mine, back_mine, grads_one = feed(
-        *mine, far_one, at_quarter, add_tokens=mine_zero[:2], add_grads=grads_one, settle=True
-    )
-    far_grads = jnp.concatenate([mine_zero[2], grads_one], 1).reshape(units, 3 * rank)
-    unit_chip = chip_half(jnp.stack([near_next[2], far_grads]), 1, core)
-
-    grad_hidden, grad_filtered, grad_gates, top_rows, wide_one = branch_back(
+    mine_one = feed(*mine, far_one, at_quarter, add_tokens=mine_zero[:2], add_grads=next_one[2], settle=True)
+    down_mine, back_mine, mine_grads = feed(
+        *mine, far_two, at_quarter, add_tokens=mine_one[:2], add_grads=next_grads, settle=True
+    )
+
+    grad_hidden, grad_filtered, grad_gates, edge, one_keep, one_give, sent, own_parts = branch_back(
         place_ids,
-        (got_back, after(back_mine, unit_chip), hidden, grad_mine, normed_two, gated, lows, select[0], gain_two, entry_full, exit_full),
+        (got_back, back_mine, hidden, grad_down, normed_two, gated, lows, select[0], gain_two, entry_full, exit_full, taps, prev, down_mine, down_next),
         kept,
+        (near_next[2], mine_zero[2], mine_one[2], mine_grads),
         out_weight,
-        pieces,
-    )
-    unit_came = after(swap(unit_chip[1], "mp", 2), top_rows)
-    unit_own = low(wide_value(unit_chip[0]) + wide_value(unit_came))
-
-    down_mine, down_next = after((down_mine, down_next), grad_hidden)
-    inner = jnp.stack([down_mine[:, width:], down_next[:, width:]])
+        rest_pieces,
+    )
+    came_edge = from_behind(edge, "seq", -1)
+    came = swap(sent, "mp", 1)
+    inner = after(jnp.stack([down_mine[:, width:], down_next[:, width:]]), got_back)
     inner_got = swap(inner, "mp", 1)
     low_down = low(wide_value(inner) + wide_value(inner_got[::-1])) * select
 
-    def quarter_stack(value):
-        return jnp.stack([value[:, i * share : (i + 1) * share] for i in range(4)])
-
-    stack_mine = quarter_stack(hidden + wide_value(down_mine[:, :width]))
-    stack_next = quarter_stack(down_next[:, :width])
-    sent = [block_for(stack_mine, 1), block_for(stack_mine, 3), block_for(stack_next, 1), block_for(stack_next, 3)]
-    came = swap(after(jnp.stack([low(v) for v in sent]), back_mine), "mp", 1)
-
-    near_row = taps[1] * prev_one[:2, None] * top_rows[:2]
-    far_row = taps[0] * prev_two[:2, None] * top_rows[:2]
-    edge = jnp.concatenate([far_row[:1], near_row[:1] + far_row[1:], jnp.zeros((6, width), jnp.float32)], 0)
-    came_edge = from_behind(edge, "seq", -1)
-    down_exit_grad = low(contract(low_down[0], grad_mine, 0, 0))
-    exit_parts = quarter_stack(down_exit_grad)
-    wide_one = jnp.concatenate([wide_one, jnp.stack([block_for(exit_parts, r) for r in range(4)])[:, None]], 1)
-    chip_one = chip_half(wide_one.reshape(4, 5 * rank, share), 1, core)
-    grad_blocks, wide_two = input_back(
+    def chip_sum(keep, give):
+        return low(wide_value(keep) + wide_value(swap(give, "seq", 1)))
+
+    one = chip_sum(one_keep, one_give)
+    head_rows, unit_rows = 2 * rank, units // 2
+    cut = head_rows + unit_rows
+    one_x = swap(one[2 * cut : 2 * cut + head_rows], "mp", 1)
+    one_y = swap(one[cut : 2 * cut], "mp", 2)
+    one_g = swap(one[2 * cut + head_rows :], "mp", 3)
+    grad_blocks, two_keep, two_give = input_back(
         place_ids,
-        (grad_filtered, grad_gates, after(came_edge, unit_own, chip_one), taps, prev, grad_hidden, tokens, normed, lows, select[0], gain_one, entry_full, column_full),
+        (grad_filtered, grad_gates, came_edge, taps, prev, grad_hidden, tokens, normed, lows, select[0], gain_one, entry_full, column_full, low_down, grad_down),
         kept,
         in_slabs,
-        pieces,
-    )
-    grad_rows = [grad_blocks[0]] + [swap(grad_blocks[r], "mp", r) for r in (1, 2, 3)]
+        in_pieces,
+    )
+    one_own = wide_value(one[:cut]) + wide_value(one_y)
+    one_own = one_own.at[:head_rows].add(wide_value(one_x) + wide_value(one_g))
+    one_own = low(one_own)
+    two = chip_sum(two_keep, two_give).reshape(4, 5 * rank // 2, share)
+    two_own = own_block(two)
+    grad_rows = [grad_blocks[0]] + [swap(after(grad_blocks[r], two_own), "mp", r) for r in (1, 2, 3)]
     grad_inputs = wide_value(jnp.stack(place(grad_rows, m)))
-    chip_two = chip_half(wide_two.reshape(4, 4 * rank, share), 1, core)
-    wide_own = jnp.concatenate([own_block(chip_one), own_block(chip_two)], 0)
-    unit_own, wide_own = seq_total(unit_own), seq_total(wide_own)
-    unit_grads = both_halves(unit_own, core)
-    cut = 5 * rank // 2
-    wide_one = both_halves(wide_own[:cut], core).reshape(5, rank, share)
-    wide_two = both_halves(wide_own[cut:], core).reshape(4, rank, share)
-
-    came = wide_value(after(came, grad_blocks))
-    exit_stack = quarter_stack(exit_full[rank:])
-    results = []
-    for i, r in ((0, 0), (1, 2)):
-        for t, stack in ((0, stack_mine), (1, stack_next)):
-            tail = product(low_down[t], block_for(exit_stack, r))
-            results.append(low(wide_value(block_for(stack, r)) + came[2 * (1 - t) + i] + tail))
-    kept_rows = jnp.stack(place(results[:2], x))
-    sent_rows = jnp.stack(place(results[2:], x))
+    one_own, two_own = seq_total_parts(one_own), seq_total(two_own)
+    grads = finish(place_ids, one_own, swap(one_own, "seq", 1), two_own, swap(two_own, "seq", 1), units, rank)
+
+    kept_rows, sent_rows = results_of(place_ids, own_parts, came, low_down, exit_full)
     output = jnp.concatenate(place([kept_rows, swap(sent_rows, "mp", 2)], y), 0)
+    in_entry_grad, in_exit_grad, out_entry_grad, out_exit_grad, gate_entry_grad, gate_exit_grad = grads[:6]
+    up_entry_grad, up_exit_grad, down_entry_grad, down_exit_grad = grads[6:]
     return (
         output,
         grad_inputs,
-        wide_two[0].T,
-        wide_two[1:].swapaxes(0, 1),
-        wide_one[3].T,
-        wide_one[2],
-        wide_one[0].T,
-        unit_grads[:, :rank].T,
-        wide_one[1].T,
-        unit_grads[:, rank : 2 * rank].T,
-        unit_grads[:, 2 * rank :],
-        wide_one[4],
+        in_entry_grad,
+        in_exit_grad.swapaxes(0, 1),
+        out_entry_grad,
+        out_exit_grad,
+        gate_entry_grad,
+        gate_exit_grad.T,
+        up_entry_grad,
+        up_exit_grad.T,
+        down_entry_grad,
+        down_exit_grad,
     )
 
 

time: 623 us -> 539 us (0.87)
  waiting for transfers between devices: 251 us -> 178 us
  other arithmetic: 24.6 us -> 12.3 us
  Pallas kernels: 252 us -> 263 us
  local copies, waits for them, and re-layouts: 29.7 us -> 22.3 us
    ppermute x51 -> x55, waiting for transfers between devices: 251 us -> 178 us  [swap(): lax.ppermute(value, axis, [(i, i ^ bit) for i in range(lax.axis_size(axis...]
    pallas_call x13 -> x17, Pallas kernels: 252 us -> 262 us  [kernel_call(): pl.pallas_call(body, out_shape=tuple(outs), in_specs=[pl.BlockSpec(memory...]
    ppermute x51 -> x55, starting transfers between devices: 52.2 us -> 50.7 us  [swap(): lax.ppermute(value, axis, [(i, i ^ bit) for i in range(lax.axis_size(axis...]
  transfers between devices with their start and end apart: 53 -> 57, of which waited for: 21 -> 23; matrix products, arithmetic and copies ran while one was open for 6% -> 4% of each run, Pallas kernels for 33% -> 41%
where the time goes in v3:
time: 539 us; the launch traced here: 532 us
  Pallas kernels  263 us (49%)
  waiting for transfers between devices  178 us (33%)
  starting transfers between devices  54.3 us (10%)
  local copies, waits for them, and re-layouts  22.3 us (4%)
  other arithmetic  12.3 us (2%)
    pallas_call x17, Pallas kernels, kernel_call(): pl.pallas_call(body, out_shape=tuple(outs), in_specs=[pl.BlockSpec(memory...  262 us
    ppermute x55, waiting for transfers between devices, swap(): lax.ppermute(value, axis, [(i, i ^ bit) for i in range(lax.axis_size(axis...  178 us
    ppermute x55, starting transfers between devices, swap(): lax.ppermute(value, axis, [(i, i ^ bit) for i in range(lax.axis_size(axis...  50.7 us
  transfers between devices with their start and end apart: 57, of which 23 were waited for; matrix products, arithmetic and copies ran while one was open for 4% of the time, Pallas kernels for 41%

profile of v3, /device:TPU:0, one launch (start us, length us, event | category | flops | bytes accessed | tf_op | source)
XLA Modules:
  0.0 531.9 jit_solution(15652348968561523118)
XLA Ops:
  9.4 7.3 %pack_first.1 = (bf16[2416,384]{1,0:T(8,128)(2,1)}, bf16[2000,384]{1,0:T(8,128)(2,1)}, bf16[2000,384]{1,0:T(8,128)(2,1)}, bf16[512,384]{1,0:T(8,128)(2,1)}, bf16...) custom-call(s32[4]{0:T(128)} %pad_add_fusion.2.place_ref.refs_0_, bf16[4,512,384]{2,1,0:T(8,128)(2,1)} %inputs.1, ...), custom_call_target="tpu_custom_call" | custom-call | bytes 16000000 | tf_op jit(solution)/shard_map/pack_first/pallas_call | solution.py:341
  16.7 10.4 %collective-permute-done.1.refs_24_.refs_22_ = bf16[1152,384]{1,0:T(8,128)(2,1)S(1)} collective-permute-done((bf16[1152,384]{1,0:T(8,128)(2,1)}, bf16[1152,384]{1,0:T(8,128)(2,1)S(1)}, u32[]{:S(2)}, u32[]{:S(2)}) %collective-permute-start.1) | collective-permute-done | bytes 884768 | tf_op jit(solution)/shard_map/ppermute | solution.py:1168
  32.6 20.2 %collective-permute-done.10.refs_26_.refs_24_ = bf16[1152,384]{1,0:T(8,128)(2,1)} collective-permute-done((bf16[1152,384]{1,0:T(8,128)(2,1)S(1)}, bf16[1152,384]{1,0:T(8,128)(2,1)}, u32[]{:S(2)}, u32[]{:S(2)}) %collective-permute-start.10) | collective-permute-done | bytes 884768 | tf_op jit(solution)/shard_map/ppermute | solution.py:1168
  52.7 16.4 %collective-permute-done.7.refs_22_.refs_20_ = bf16[1152,384]{1,0:T(8,128)(2,1)} collective-permute-done((bf16[1152,384]{1,0:T(8,128)(2,1)S(1)}, bf16[1152,384]{1,0:T(8,128)(2,1)}, u32[]{:S(2)}, u32[]{:S(2)}) %collective-permute-start.7) | collective-permute-done | bytes 884768 | tf_op jit(solution)/shard_map/ppermute | solution.py:1168
  76.5 29.9 %collective-permute-done.2.refs_17_.refs_36_.refs_26_ = bf16[2000,384]{1,0:T(8,128)(2,1)} collective-permute-done((bf16[2000,384]{1,0:T(8,128)(2,1)}, bf16[2000,384]{1,0:T(8,128)(2,1)}, u32[]{:S(2)}, u32[]{:S(2)}) %collective-permute-start.2) | collective-permute-done | bytes 1536032 | tf_op jit(solution)/shard_map/ppermute | solution.py:1168
  116.3 5.3 pack_second.1
  127.0 30.8 %mixer.1 = (bf16[4,512,1536]{2,1,0:T(8,128)(2,1)}, bf16[512,1536]{1,0:T(8,128)(2,1)}, bf16[512,1536]{1,0:T(8,128)(2,1)}, bf16[512,1536]{1,0:T(8,128)(2,1)}, f32[...) custom-call(s32[4]{0:T(128)} %pad_add_fusion.2.place_ref.refs_0_, ...), custom_call_target="tpu_custom_call" | custom-call | flops 9663676416 | bytes 50000000 | tf_op jit(solution)/shard_map/mixer/pallas_call | solution.py:341
  162.4 4.9 ready.1
  167.4 33.2 %feed_near.2 = (bf16[512,1664]{1,0:T(8,128)(2,1)}, bf16[512,1792]{1,0:T(8,128)(2,1)}, f32[1728,384]{1,0:T(8,128)}) custom-call(bf16[512,1536]{1,0:T(8,128)(2,1)} %get-tuple-element.128.refs_0_.refs_1_.refs_5_, bf16[4,512,128]{2,1,0:T(8,128)(2,1)} %get-tuple-element.144.refs_1_.refs_2_.refs_7_.refs_9_, ...), custom_call_target="tpu_custom_call" | custom-call | flops 19025362944 | bytes 30000000 | tf_op jit(solution)/shard_map/feed_near/pallas_call | solution.py:341
  204.1 33.2 %feed_near.3 = (bf16[512,1664]{1,0:T(8,128)(2,1)}, bf16[512,1792]{1,0:T(8,128)(2,1)}, f32[1728,384]{1,0:T(8,128)}) custom-call(bf16[512,1536]{1,0:T(8,128)(2,1)} %copy-done.1, bf16[2,512,128]{2,1,0:T(8,128)(2,1)} %copy-done.2, bf16[2,512,1536]{2,1,0:T(8,128)(2,1)} %get-tuple-element.139.refs_2_.refs_3_.refs_4_.refs_15_, ...), custom_call_target="tpu_custom_call" | custom-call | flops 19025362944 | bytes 30000000 | tf_op jit(solution)/shard_map/feed_near/pallas_call | solution.py:341
  238.4 14.3 %collective-permute-done.21.refs_5_ = bf16[3,176,1664]{2,1,0:T(8,128)(2,1)} collective-permute-done((bf16[3,176,1664]{2,1,0:T(8,128)(2,1)}, bf16[3,176,1664]{2,1,0:T(8,128)(2,1)}, u32[]{:S(2)}, u32[]{:S(2)}) %collective-permute-start.21) | collective-permute-done | bytes 1757216 | tf_op jit(solution)/shard_map/ppermute | solution.py:1168
  255.7 12.9 %feed_far.6 = (bf16[512,1664]{1,0:T(8,128)(2,1)}, bf16[512,1792]{1,0:T(8,128)(2,1)}, f32[512,384]{1,0:T(8,128)}) custom-call(s32[1]{0:T(128)} %bitcast.2.refs_0_, bf16[512,1536]{1,0:T(8,128)(2,1)} %copy-done.1, bf16[2,512,128]{2,1,0:T(8,128)(2,1)} %copy-done.2, bf16[2,512,1536]{2,1,0:T(8,128)(2,1)} %get-tuple-element.139.refs_2_.refs_3_.refs_4_.refs_15_, ...), custom_call_target="tpu_custom_call" | custom-call | flops 5637144576 | bytes 30000000 | tf_op jit(solution)/shard_map/feed_far/pallas_call | solution.py:341
  269.6 13.3 %feed_far.7 = (bf16[512,1664]{1,0:T(8,128)(2,1)}, bf16[512,1792]{1,0:T(8,128)(2,1)}, f32[4,128,384]{2,1,0:T(8,128)}) custom-call(s32[1]{0:T(128)} %bitcast.2.refs_0_, bf16[512,1536]{1,0:T(8,128)(2,1)} %get-tuple-element.128.refs_0_.refs_1_.refs_5_, bf16[4,512,128]{2,1,0:T(8,128)(2,1)} %get-tuple-element.144.refs_1_.refs_2_.refs_7_.refs_9_, ...), custom_call_target="tpu_custom_call" | custom-call | flops 5637144576 | bytes 30000000 | tf_op jit(solution)/shard_map/feed_far/pallas_call | solution.py:341
  283.0 22.8 %collective-permute-done.22.refs_6_ = bf16[3,176,1664]{2,1,0:T(8,128)(2,1)S(1)} collective-permute-done((bf16[3,176,1664]{2,1,0:T(8,128)(2,1)}, bf16[3,176,1664]{2,1,0:T(8,128)(2,1)S(1)}, u32[]{:S(2)}, u32[]{:S(2)}) %collective-permute-start.22) | collective-permute-done | bytes 1757216 | tf_op jit(solution)/shard_map/ppermute | solution.py:1168
  305.9 13.5 %feed_far.8 = (bf16[512,1664]{1,0:T(8,128)(2,1)}, bf16[512,1792]{1,0:T(8,128)(2,1)}, f32[512,384]{1,0:T(8,128)}) custom-call(s32[1]{0:T(128)} %bitcast.2.refs_0_, bf16[512,1536]{1,0:T(8,128)(2,1)} %copy-done.1, bf16[2,512,128]{2,1,0:T(8,128)(2,1)} %copy-done.2, bf16[2,512,1536]{2,1,0:T(8,128)(2,1)} %get-tuple-element.139.refs_2_.refs_3_.refs_4_.refs_15_, ...), custom_call_target="tpu_custom_call" | custom-call | flops 5637144576 | bytes 30000000 | tf_op jit(solution)/shard_map/feed_far/pallas_call | solution.py:341
  320.6 17.4 %feed_far.9 = (bf16[512,1664]{1,0:T(8,128)(2,1)}, bf16[512,1792]{1,0:T(8,128)(2,1)}, f32[704,384]{1,0:T(8,128)}) custom-call(s32[1]{0:T(128)} %bitcast.2.refs_0_, bf16[512,1536]{1,0:T(8,128)(2,1)} %copy-done.1, bf16[2,512,128]{2,1,0:T(8,128)(2,1)} %copy-done.2, bf16[2,512,1536]{2,1,0:T(8,128)(2,1)} %get-tuple-element.139.refs_2_.refs_3_.refs_4_.refs_15_, ...), custom_call_target="tpu_custom_call" | custom-call | flops 7751073792 | bytes 30000000 | tf_op jit(solution)/shard_map/feed_far/pallas_call | solution.py:341
  339.5 12.9 %feed_far.10 = (bf16[512,1664]{1,0:T(8,128)(2,1)}, bf16[512,1792]{1,0:T(8,128)(2,1)}, f32[4,128,384]{2,1,0:T(8,128)}) custom-call(s32[1]{0:T(128)} %bitcast.2.refs_0_, bf16[512,1536]{1,0:T(8,128)(2,1)} %get-tuple-element.128.refs_0_.refs_1_.refs_5_, bf16[4,512,128]{2,1,0:T(8,128)(2,1)} %get-tuple-element.144.refs_1_.refs_2_.refs_7_.refs_9_, ...), custom_call_target="tpu_custom_call" | custom-call | flops 5637144576 | bytes 30000000 | tf_op jit(solution)/shard_map/feed_far/pallas_call | solution.py:341
  352.4 17.3 %feed_far.11 = (bf16[512,1664]{1,0:T(8,128)(2,1)}, bf16[512,1792]{1,0:T(8,128)(2,1)}, f32[4,176,384]{2,1,0:T(8,128)}) custom-call(s32[1]{0:T(128)} %bitcast.2.refs_0_, bf16[512,1536]{1,0:T(8,128)(2,1)} %get-tuple-element.128.refs_0_.refs_1_.refs_5_, bf16[4,512,128]{2,1,0:T(8,128)(2,1)} %get-tuple-element.144.refs_1_.refs_2_.refs_7_.refs_9_, ...), custom_call_target="tpu_custom_call" | custom-call | flops 7751073792 | bytes 30000000 | tf_op jit(solution)/shard_map/feed_far/pallas_call | solution.py:341
  369.7 10.4 %collective-permute-done.33.refs_1_ = bf16[512,1792]{1,0:T(8,128)(2,1)S(1)} collective-permute-done((bf16[512,1792]{1,0:T(8,128)(2,1)}, bf16[512,1792]{1,0:T(8,128)(2,1)S(1)}, u32[]{:S(2)}, u32[]{:S(2)}) %collective-permute-start.33) | collective-permute-done | bytes 1835040 | tf_op jit(solution)/shard_map/ppermute | solution.py:1168
  381.4 21.8 %branch_back.1 = (f32[512,1536]{1,0:T(8,128)}, bf16[512,1536]{1,0:T(8,128)(2,1)}, bf16[512,1536]{1,0:T(8,128)(2,1)}, f32[8,1536]{1,0:T(8,128)}, bf16[2752,384]{1...) custom-call(s32[4]{0:T(128)} %pad_add_fusion.2.place_ref.refs_0_, ...), custom_call_target="tpu_custom_call" | custom-call | flops 3221225472 | bytes 40000000 | tf_op jit(solution)/shard_map/branch_back/pallas_call | solution.py:341
  408.8 5.7 %collective-permute-done.35 = bf16[2,512,128]{2,1,0:T(8,128)(2,1)S(1)} collective-permute-done((bf16[2,512,128]{2,1,0:T(8,128)(2,1)S(1)}, bf16[2,512,128]{2,1,0:T(8,128)(2,1)S(1)}, u32[]{:S(2)}, u32[]{:S(2)}) %collective-permute-start.35) | collective-permute-done | bytes 262176 | tf_op jit(solution)/shard_map/ppermute | solution.py:1168
  419.3 27.5 %input_back.1 = (bf16[4,512,384]{2,1,0:T(8,128)(2,1)}, bf16[1280,384]{1,0:T(8,128)(2,1)}, bf16[1280,384]{1,0:T(8,128)(2,1)}) custom-call(s32[4]{0:T(128)} %pad_add_fusion.2.place_ref.refs_0_, bf16[512,1536]{1,0:T(8,128)(2,1)} %get-tuple-element.189.refs_1_, bf16[512,1536]{1,0:T(8,128)(2,1)} %get-tuple-element.190.refs_2_, f32[8,1536]{1,0:T(8,128)} %copy-done.21, ...), custom_call_target="tpu_custom_call" | custom-call | flops 7247757312 | bytes 40000000 | tf_op jit(solution)/shard_map/input_back/pallas_call | solution.py:341
  449.7 5.0 collective-permute-done.47
  454.7 4.3 collective-permute-done.48
  464.3 6.6 %collective-permute-done.49 = bf16[560,384]{1,0:T(8,128)(2,1)S(1)} collective-permute-done((bf16[560,384]{1,0:T(8,128)(2,1)S(1)}, bf16[560,384]{1,0:T(8,128)(2,1)S(1)}, u32[]{:S(2)}, u32[]{:S(2)}) %collective-permute-start.49) | collective-permute-done | bytes 430112 | tf_op jit(solution)/shard_map/ppermute | solution.py:1168
  473.7 8.9 %collective-permute-done.50 = bf16[280,384]{1,0:T(8,128)(2,1)S(1)} collective-permute-done((bf16[280,384]{1,0:T(8,128)(2,1)S(1)}, bf16[280,384]{1,0:T(8,128)(2,1)S(1)}, u32[]{:S(2)}, u32[]{:S(2)}) %collective-permute-start.50) | collective-permute-done | bytes 215072 | tf_op jit(solution)/shard_map/ppermute | solution.py:1168
  482.9 3.2 collective-permute-start.54
  488.4 6.2 %collective-permute-done.51 = bf16[280,384]{1,0:T(8,128)(2,1)S(1)} collective-permute-done((bf16[280,384]{1,0:T(8,128)(2,1)S(1)}, bf16[280,384]{1,0:T(8,128)(2,1)S(1)}, u32[]{:S(2)}, u32[]{:S(2)}) %collective-permute-start.51) | collective-permute-done | bytes 215072 | tf_op jit(solution)/shard_map/ppermute | solution.py:1168
  497.7 3.7 results.1
  508.1 3.4 collective-permute-done.52
  517.1 6.3 %collective-permute-done.36 = bf16[2,512,384]{2,1,0:T(8,128)(2,1)S(1)} collective-permute-done((bf16[2,512,384]{2,1,0:T(8,128)(2,1)}, bf16[2,512,384]{2,1,0:T(8,128)(2,1)S(1)}, u32[]{:S(2)}, u32[]{:S(2)}) %collective-permute-start.36) | collective-permute-done | bytes 786464 | tf_op jit(solution)/shard_map/ppermute | solution.py:1168
  527.0 4.5 finish.1
  (221 shorter events, 96.3 us)
Async XLA Ops:
  4.2 22.9 %collective-permute-start.1 = (bf16[1152,384]{1,0:T(8,128)(2,1)}, bf16[1152,384]{1,0:T(8,128)(2,1)S(1)}, u32[]{:S(2)}, u32[]{:S(2)}) collective-permute-start(bf16[1152,384]{1,0:T(8,128)(2,1)} %pack_in.1), channel_id=1, source_target_pairs={{0,2},{1,3},{2,0},{3,1},{4,6},{5,7},{6,4},{7,5},{8,10},{9,11},{10,... | collective-permute-start | bytes 2654216 | tf_op jit(solution)/shard_map/ppermute | solution.py:1168
  7.3 21.3 %collective-permute-start = (bf16[1152,384]{1,0:T(8,128)(2,1)}, bf16[1152,384]{1,0:T(8,128)(2,1)S(1)}, u32[]{:S(2)}, u32[]{:S(2)}) collective-permute-start(bf16[1152,384]{1,0:T(8,128)(2,1)} %pack_in.1), channel_id=1, source_target_pairs={{0,1},{1,0},{2,3},{3,2},{4,5},{5,4},{6,7},{7,6},{8,9},{9,8},{10,11... | collective-permute-start | bytes 2654216 | tf_op jit(solution)/shard_map/ppermute | solution.py:1168
  28.6 42.2 %collective-permute-start.4 = (bf16[2416,384]{1,0:T(8,128)(2,1)}, bf16[2416,384]{1,0:T(8,128)(2,1)}, u32[]{:S(2)}, u32[]{:S(2)}) collective-permute-start(bf16[2416,384]{1,0:T(8,128)(2,1)} %get-tuple-element.126), channel_id=1, source_target_pairs={{0,3},{1,2},{2,1},{3,0},{4,7},{5,6},{6,5},{7,4},{8,11},{9,10},{10,... | collective-permute-start | bytes 5566472 | tf_op jit(solution)/shard_map/ppermute | solution.py:1168
  30.0 22.7 %collective-permute-start.10 = (bf16[1152,384]{1,0:T(8,128)(2,1)S(1)}, bf16[1152,384]{1,0:T(8,128)(2,1)}, u32[]{:S(2)}, u32[]{:S(2)}) collective-permute-start(bf16[1152,384]{1,0:T(8,128)(2,1)S(1)} %collective-permute-done.1.refs_24_.refs_22_), channel_id=1, source_target_pairs={{0,8},{4,12},{8,0},{12,4},{16,24},{20,28},{24,16},{28,20},{1,9},{5... | collective-permute-start | bytes 2654216 | tf_op jit(solution)/shard_map/ppermute | solution.py:1168
  31.6 37.6 %collective-permute-start.7 = (bf16[1152,384]{1,0:T(8,128)(2,1)S(1)}, bf16[1152,384]{1,0:T(8,128)(2,1)}, u32[]{:S(2)}, u32[]{:S(2)}) collective-permute-start(bf16[1152,384]{1,0:T(8,128)(2,1)S(1)} %collective-permute-done.refs_20_.refs_18_), channel_id=1, source_target_pairs={{0,8},{4,12},{8,0},{12,4},{16,24},{20,28},{24,16},{28,20},{1,9},{5... | collective-permute-start | bytes 2654216 | tf_op jit(solution)/shard_map/ppermute | solution.py:1168
  32.1 37.1 %collective-permute-start.9 = (bf16[1152,384]{1,0:T(8,128)(2,1)S(1)}, bf16[1152,384]{1,0:T(8,128)(2,1)S(1)}, u32[]{:S(2)}, u32[]{:S(2)}) collective-permute-start(bf16[1152,384]{1,0:T(8,128)(2,1)S(1)} %collective-permute-done.1.refs_24_.refs_22_), channel_id=1, source_target_pairs={{0,4},{4,0},{8,12},{12,8},{16,20},{20,16},{24,28},{28,24},{1,5},{5... | collective-permute-start | bytes 2654216 | tf_op jit(solution)/shard_map/ppermute | solution.py:1168
  32.1 41.5 %collective-permute-start.6 = (bf16[1152,384]{1,0:T(8,128)(2,1)S(1)}, bf16[1152,384]{1,0:T(8,128)(2,1)}, u32[]{:S(2)}, u32[]{:S(2)}) collective-permute-start(bf16[1152,384]{1,0:T(8,128)(2,1)S(1)} %collective-permute-done.refs_20_.refs_18_), channel_id=1, source_target_pairs={{0,4},{4,0},{8,12},{12,8},{16,20},{20,16},{24,28},{28,24},{1,5},{5... | collective-permute-start | bytes 2654216 | tf_op jit(solution)/shard_map/ppermute | solution.py:1168
  52.7 20.8 %collective-permute-start.11 = (bf16[1152,384]{1,0:T(8,128)(2,1)}, bf16[1152,384]{1,0:T(8,128)(2,1)}, u32[]{:S(2)}, u32[]{:S(2)}) collective-permute-start(bf16[1152,384]{1,0:T(8,128)(2,1)} %collective-permute-done.10.refs_26_.refs_24_), channel_id=1, source_target_pairs={{0,4},{4,0},{8,12},{12,8},{16,20},{20,16},{24,28},{28,24},{1,5},{5... | collective-permute-start | bytes 2654216 | tf_op jit(solution)/shard_map/ppermute | solution.py:1168
  70.1 36.3 %collective-permute-start.2 = (bf16[2000,384]{1,0:T(8,128)(2,1)}, bf16[2000,384]{1,0:T(8,128)(2,1)}, u32[]{:S(2)}, u32[]{:S(2)}) collective-permute-start(bf16[2000,384]{1,0:T(8,128)(2,1)} %get-tuple-element.123), channel_id=1, source_target_pairs={{0,1},{1,0},{2,3},{3,2},{4,5},{5,4},{6,7},{7,6},{8,9},{9,8},{10,11... | collective-permute-start | bytes 4608008 | tf_op jit(solution)/shard_map/ppermute | solution.py:1168
  70.8 35.9 %collective-permute-start.3 = (bf16[2000,384]{1,0:T(8,128)(2,1)}, bf16[2000,384]{1,0:T(8,128)(2,1)}, u32[]{:S(2)}, u32[]{:S(2)}) collective-permute-start(bf16[2000,384]{1,0:T(8,128)(2,1)} %get-tuple-element.124), channel_id=1, source_target_pairs={{0,2},{1,3},{2,0},{3,1},{4,6},{5,7},{6,4},{7,5},{8,10},{9,11},{10,... | collective-permute-start | bytes 4608008 | tf_op jit(solution)/shard_map/ppermute | solution.py:1168
  73.6 33.9 %collective-permute-start.13 = (bf16[1904,384]{1,0:T(8,128)(2,1)S(1)}, bf16[1904,384]{1,0:T(8,128)(2,1)S(1)}, u32[]{:S(2)}, u32[]{:S(2)}) collective-permute-start(bf16[1904,384]{1,0:T(8,128)(2,1)S(1)} %slice.137.refs_28_.refs_32_.refs_22_.refs_26_), channel_id=1, source_target_pairs={{0,8},{4,12},{8,0},{12,4},{16,24},{20,28},{24,16},{28,20},{1,9},{5... | collective-permute-start | bytes 4386824 | tf_op jit(solution)/shard_map/ppermute | solution.py:1168
  121.7 38.7 %collective-permute-start.20 = (bf16[2,512,384]{2,1,0:T(8,128)(2,1)}, bf16[2,512,384]{2,1,0:T(8,128)(2,1)S(1)}, u32[]{:S(2)}, u32[]{:S(2)}) collective-permute-start(bf16[2,512,384]{2,1,0:T(8,128)(2,1)} %get-tuple-element.138), channel_id=1, source_target_pairs={{0,3},{1,2},{2,1},{3,0},{4,7},{5,6},{6,5},{7,4},{8,11},{9,10},{10,... | collective-permute-start | bytes 2359304 | tf_op jit(solution)/shard_map/ppermute | solution.py:1168
  123.7 37.8 %collective-permute-start.18 = (bf16[2,512,384]{2,1,0:T(8,128)(2,1)}, bf16[2,512,384]{2,1,0:T(8,128)(2,1)S(1)}, u32[]{:S(2)}, u32[]{:S(2)}) collective-permute-start(bf16[2,512,384]{2,1,0:T(8,128)(2,1)} %get-tuple-element.138), channel_id=1, source_target_pairs={{0,2},{1,3},{2,0},{3,1},{4,6},{5,7},{6,4},{7,5},{8,10},{9,11},{10,... | collective-permute-start | bytes 2359304 | tf_op jit(solution)/shard_map/ppermute | solution.py:1168
  124.7 34.8 %collective-permute-start.19 = (bf16[2,512,384]{2,1,0:T(8,128)(2,1)S(1)}, bf16[2,512,384]{2,1,0:T(8,128)(2,1)S(1)}, u32[]{:S(2)}, u32[]{:S(2)}) collective-permute-start(bf16[2,512,384]{2,1,0:T(8,128)(2,1)S(1)} %copy-done.15), channel_id=1, source_target_pairs={{0,1},{1,0},{2,3},{3,2},{4,5},{5,4},{6,7},{7,6},{8,9},{9,8},{10,11... | collective-permute-start | bytes 2359304 | tf_op jit(solution)/shard_map/ppermute | solution.py:1168
  125.3 75.3 %collective-permute-start.23 = (bf16[3,128,1664]{2,1,0:T(8,128)(2,1)}, bf16[3,128,1664]{2,1,0:T(8,128)(2,1)}, u32[]{:S(2)}, u32[]{:S(2)}) collective-permute-start(bf16[3,128,1664]{2,1,0:T(8,128)(2,1)} %get-tuple-element.148), channel_id=1, source_target_pairs={{0,2},{1,3},{2,0},{3,1},{4,6},{5,7},{6,4},{7,5},{8,10},{9,11},{10,... | collective-permute-start | bytes 3833864 | tf_op jit(solution)/shard_map/ppermute | solution.py:1168
  157.9 44.4 %collective-permute-start.17 = (bf16[512,1536]{1,0:T(8,128)(2,1)}, bf16[512,1536]{1,0:T(8,128)(2,1)S(1)}, u32[]{:S(2)}, u32[]{:S(2)}) collective-permute-start(bf16[512,1536]{1,0:T(8,128)(2,1)} %get-tuple-element.128.refs_0_.refs_1_.refs_5_), channel_id=1, source_target_pairs={{0,1},{1,0},{2,3},{3,2},{4,5},{5,4},{6,7},{7,6},{8,9},{9,8},{10,11... | collective-permute-start | bytes 4718600 | tf_op jit(solution)/shard_map/ppermute | solution.py:1168
  159.5 78.4 %collective-permute-start.29 = (bf16[3,128,1664]{2,1,0:T(8,128)(2,1)}, bf16[3,128,1664]{2,1,0:T(8,128)(2,1)}, u32[]{:S(2)}, u32[]{:S(2)}) collective-permute-start(bf16[3,128,1664]{2,1,0:T(8,128)(2,1)} %get-tuple-element.160), channel_id=1, source_target_pairs={{0,2},{1,3},{2,0},{3,1},{4,6},{5,7},{6,4},{7,5},{8,10},{9,11},{10,... | collective-permute-start | bytes 3833864 | tf_op jit(solution)/shard_map/ppermute | solution.py:1168
  160.4 92.2 %collective-permute-start.21 = (bf16[3,176,1664]{2,1,0:T(8,128)(2,1)}, bf16[3,176,1664]{2,1,0:T(8,128)(2,1)}, u32[]{:S(2)}, u32[]{:S(2)}) collective-permute-start(bf16[3,176,1664]{2,1,0:T(8,128)(2,1)} %get-tuple-element.143), channel_id=1, source_target_pairs={{0,2},{1,3},{2,0},{3,1},{4,6},{5,7},{6,4},{7,5},{8,10},{9,11},{10,... | collective-permute-start | bytes 5271560 | tf_op jit(solution)/shard_map/ppermute | solution.py:1168
  200.6 36.8 %collective-permute-start.24 = (bf16[3,128,1664]{2,1,0:T(8,128)(2,1)}, bf16[3,128,1664]{2,1,0:T(8,128)(2,1)}, u32[]{:S(2)}, u32[]{:S(2)}) collective-permute-start(bf16[3,128,1664]{2,1,0:T(8,128)(2,1)} %collective-permute-done.23.refs_5_), channel_id=1, source_target_pairs={{0,8},{4,12},{8,0},{12,4},{16,24},{20,28},{24,16},{28,20},{1,9},{5... | collective-permute-start | bytes 3833864 | tf_op jit(solution)/shard_map/ppermute | solution.py:1168
  237.9 31.1 %collective-permute-start.30 = (bf16[3,128,1664]{2,1,0:T(8,128)(2,1)}, bf16[3,128,1664]{2,1,0:T(8,128)(2,1)S(1)}, u32[]{:S(2)}, u32[]{:S(2)}) collective-permute-start(bf16[3,128,1664]{2,1,0:T(8,128)(2,1)} %collective-permute-done.29.refs_5_), channel_id=1, source_target_pairs={{0,8},{4,12},{8,0},{12,4},{16,24},{20,28},{24,16},{28,20},{1,9},{5... | collective-permute-start | bytes 3833864 | tf_op jit(solution)/shard_map/ppermute | solution.py:1168
  252.7 53.2 %collective-permute-start.22 = (bf16[3,176,1664]{2,1,0:T(8,128)(2,1)}, bf16[3,176,1664]{2,1,0:T(8,128)(2,1)S(1)}, u32[]{:S(2)}, u32[]{:S(2)}) collective-permute-start(bf16[3,176,1664]{2,1,0:T(8,128)(2,1)} %collective-permute-done.21.refs_5_), channel_id=1, source_target_pairs={{0,8},{4,12},{8,0},{12,4},{16,24},{20,28},{24,16},{28,20},{1,9},{5... | collective-permute-start | bytes 5271560 | tf_op jit(solution)/shard_map/ppermute | solution.py:1168
  269.1 36.8 %collective-permute-start.31 = (bf16[3,128,1664]{2,1,0:T(8,128)(2,1)}, bf16[3,128,1664]{2,1,0:T(8,128)(2,1)}, u32[]{:S(2)}, u32[]{:S(2)}) collective-permute-start(bf16[3,128,1664]{2,1,0:T(8,128)(2,1)} %collective-permute-done.29.refs_5_), channel_id=1, source_target_pairs={{0,4},{4,0},{8,12},{12,8},{16,20},{20,16},{24,28},{28,24},{1,5},{5... | collective-permute-start | bytes 3833864 | tf_op jit(solution)/shard_map/ppermute | solution.py:1168
  269.1 36.8 %collective-permute-start.32 = (bf16[3,128,1664]{2,1,0:T(8,128)(2,1)S(1)}, bf16[3,128,1664]{2,1,0:T(8,128)(2,1)}, u32[]{:S(2)}, u32[]{:S(2)}) collective-permute-start(bf16[3,128,1664]{2,1,0:T(8,128)(2,1)S(1)} %collective-permute-done.30.refs_6_), channel_id=1, source_target_pairs={{0,4},{4,0},{8,12},{12,8},{16,20},{20,16},{24,28},{28,24},{1,5},{5... | collective-permute-start | bytes 3833864 | tf_op jit(solution)/shard_map/ppermute | solution.py:1168
  282.9 36.5 %collective-permute-start.27 = (bf16[3,176,1664]{2,1,0:T(8,128)(2,1)}, bf16[3,176,1664]{2,1,0:T(8,128)(2,1)S(1)}, u32[]{:S(2)}, u32[]{:S(2)}) collective-permute-start(bf16[3,176,1664]{2,1,0:T(8,128)(2,1)} %collective-permute-done.21.refs_5_), channel_id=1, source_target_pairs={{0,4},{4,0},{8,12},{12,8},{16,20},{20,16},{24,28},{28,24},{1,5},{5... | collective-permute-start | bytes 5271560 | tf_op jit(solution)/shard_map/ppermute | solution.py:1168
  338.1 42.0 %collective-permute-start.33 = (bf16[512,1792]{1,0:T(8,128)(2,1)}, bf16[512,1792]{1,0:T(8,128)(2,1)S(1)}, u32[]{:S(2)}, u32[]{:S(2)}) collective-permute-start(bf16[512,1792]{1,0:T(8,128)(2,1)} %get-tuple-element.168), channel_id=1, source_target_pairs={{0,1},{1,0},{2,3},{3,2},{4,5},{5,4},{6,7},{7,6},{8,9},{9,8},{10,11... | collective-permute-start | bytes 5505032 | tf_op jit(solution)/shard_map/ppermute | solution.py:1168
  408.1 89.4 %collective-permute-start.34 = (bf16[4,512,384]{2,1,0:T(8,128)(2,1)}, bf16[4,512,384]{2,1,0:T(8,128)(2,1)}, u32[]{:S(2)}, u32[]{:S(2)}) collective-permute-start(bf16[4,512,384]{2,1,0:T(8,128)(2,1)} %get-tuple-element.185), channel_id=1, source_target_pairs={{0,1},{1,0},{2,3},{3,2},{4,5},{5,4},{6,7},{7,6},{8,9},{9,8},{10,11... | collective-permute-start | bytes 4718600 | tf_op jit(solution)/shard_map/ppermute | solution.py:1168
  417.6 31.9 %collective-permute-start.46 = (bf16[1120,384]{1,0:T(8,128)(2,1)S(1)}, bf16[1120,384]{1,0:T(8,128)(2,1)S(1)}, u32[]{:S(2)}, u32[]{:S(2)}) collective-permute-start(bf16[1120,384]{1,0:T(8,128)(2,1)S(1)} %slice.146), channel_id=1, source_target_pairs={{0,2},{1,3},{2,0},{3,1},{4,6},{5,7},{6,4},{7,5},{8,10},{9,11},{10,... | collective-permute-start | bytes 2580488 | tf_op jit(solution)/shard_map/ppermute | solution.py:1168
  460.7 22.0 %collective-permute-start.39 = (bf16[320,384]{1,0:T(8,128)(2,1)S(1)}, bf16[320,384]{1,0:T(8,128)(2,1)S(1)}, u32[]{:S(2)}, u32[]{:S(2)}) collective-permute-start(bf16[320,384]{1,0:T(8,128)(2,1)S(1)} %get-tuple-element.226), channel_id=1, source_target_pairs={{0,3},{1,2},{2,1},{3,0},{4,7},{5,6},{6,5},{7,4},{8,11},{9,10},{10,... | collective-permute-start | bytes 737288 | tf_op jit(solution)/shard_map/ppermute | solution.py:1168
  462.7 20.0 %collective-permute-start.41 = (bf16[320,384]{1,0:T(8,128)(2,1)S(1)}, bf16[320,384]{1,0:T(8,128)(2,1)S(1)}, u32[]{:S(2)}, u32[]{:S(2)}) collective-permute-start(bf16[320,384]{1,0:T(8,128)(2,1)S(1)} %get-tuple-element.227), channel_id=1, source_target_pairs={{0,2},{1,3},{2,0},{3,1},{4,6},{5,7},{6,4},{7,5},{8,10},{9,11},{10,... | collective-permute-start | bytes 737288 | tf_op jit(solution)/shard_map/ppermute | solution.py:1168
  463.7 19.1 %collective-permute-start.40 = (bf16[320,384]{1,0:T(8,128)(2,1)S(1)}, bf16[320,384]{1,0:T(8,128)(2,1)S(1)}, u32[]{:S(2)}, u32[]{:S(2)}) collective-permute-start(bf16[320,384]{1,0:T(8,128)(2,1)S(1)} %get-tuple-element.228), channel_id=1, source_target_pairs={{0,1},{1,0},{2,3},{3,2},{4,5},{5,4},{6,7},{7,6},{8,9},{9,8},{10,11... | collective-permute-start | bytes 737288 | tf_op jit(solution)/shard_map/ppermute | solution.py:1168
  482.9 18.5 %collective-permute-start.54 = (bf16[320,384]{1,0:T(8,128)(2,1)S(1)}, bf16[320,384]{1,0:T(8,128)(2,1)}, u32[]{:S(2)}, u32[]{:S(2)}) collective-permute-start(bf16[320,384]{1,0:T(8,128)(2,1)S(1)} %add_convert_fusion.6), channel_id=1, source_target_pairs={{0,8},{4,12},{8,0},{12,4},{16,24},{20,28},{24,16},{28,20},{1,9},{5... | collective-permute-start | bytes 737288 | tf_op jit(solution)/shard_map/ppermute | solution.py:1168
  501.4 22.0 %collective-permute-start.36 = (bf16[2,512,384]{2,1,0:T(8,128)(2,1)}, bf16[2,512,384]{2,1,0:T(8,128)(2,1)S(1)}, u32[]{:S(2)}, u32[]{:S(2)}) collective-permute-start(bf16[2,512,384]{2,1,0:T(8,128)(2,1)} %get-tuple-element.188), channel_id=1, source_target_pairs={{0,2},{1,3},{2,0},{3,1},{4,6},{5,7},{6,4},{7,5},{8,10},{9,11},{10,... | collective-permute-start | bytes 2359304 | tf_op jit(solution)/shard_map/ppermute | solution.py:1168
  (58 other events, 777.4 us)

commit v4 on v3

--- a/solution.py
+++ b/solution.py
@@ -1200,11 +1200,13 @@
     return value
 
 
-def seq_total_parts(value):
+def seq_total_parts(value, *firsts):
     s = lax.axis_index("seq")
-    for bit in seq_bits():
+    for bit, first in zip(seq_bits(), firsts + (None,) * len(seq_bits())):
         keep = s // bit % 2
         other = swap(part_of(value, 0, 1 - keep, 2), "seq", bit)
+        if first is not None:
+            other = after(other, first)
         value = low(wide_value(part_of(value, 0, keep, 2)) + wide_value(other))
     for bit in seq_bits()[::-1]:
         value = jnp.concatenate(place([value, swap(value, "seq", bit)], s // bit % 2), 0)
@@ -1274,7 +1276,7 @@
     )
     near = [gate_weight.T, gate_exit.T, up_weight.T, up_exit.T, down_weight, down_entry]
     count = units // 4 // 16
-    rows = (count * 3 // 10 * 16, count * 3 // 10 * 16)
+    rows = (-(-count * 10 // 27) * 16, count * 9 // 27 * 16)
     cuts = ((0, rows[0]), (rows[0], rows[1]), (rows[0] + rows[1], units // 4 - rows[0] - rows[1]))
 
     def spread(got, over, r, base):
@@ -1294,7 +1296,7 @@
     in_pieces = spread(in_x, over_x, 1, 0) + spread(in_y, over_y, 2, 0)
     far_count = far_pack.shape[0] - length
     far_weights = far_pack[:far_count]
-    over_far = swap(after(far_weights, [p[0] for p in in_pieces]), "seq", 2)
+    over_far = swap(after(far_weights, [p[0] for p in in_pieces], packed), "seq", 2)
     row_blocks = [own_block_rows, beside, below, far_pack]
     ends = [length, length, length, far_pack.shape[0]]
     head = from_behind(jnp.stack([b[e - halo : e] for b, e in zip(row_blocks, ends)]), "seq", 1)
@@ -1349,7 +1351,7 @@
     mine_zero = feed(*mine, far_zero, at_quarter, add_tokens=near_mine[:2], add_grads=next_zero[2], settle=True)
     far_one = spread_far(far_first[1], near_mine[2], next_zero[2])
     next_one = feed(*other, far_one, at_quarter, add_tokens=next_zero[:2])
-    far_two = spread_far(far_first[2], near_next[2], mine_zero[2])
+    far_two = spread_far(far_first[2], next_zero[2], next_one[2])
     down_next, back_next, next_grads = feed(*other, far_two, at_quarter, add_tokens=next_one[:2])
     got_back = swap(back_next, "mp", 1)
     mine_one = feed(*mine, far_one, at_quarter, add_tokens=mine_zero[:2], add_grads=next_one[2], settle=True)
@@ -1387,17 +1389,19 @@
         in_slabs,
         in_pieces,
     )
+    one_x, one_y, one_g, came = after((one_x, one_y, one_g, came), grad_blocks)
     one_own = wide_value(one[:cut]) + wide_value(one_y)
     one_own = one_own.at[:head_rows].add(wide_value(one_x) + wide_value(one_g))
     one_own = low(one_own)
+    kept_rows, sent_rows = results_of(place_ids, after(own_parts, one_own), came, low_down, exit_full)
+    two_keep, two_give = after((two_keep, two_give), sent_rows)
     two = chip_sum(two_keep, two_give).reshape(4, 5 * rank // 2, share)
     two_own = own_block(two)
     grad_rows = [grad_blocks[0]] + [swap(after(grad_blocks[r], two_own), "mp", r) for r in (1, 2, 3)]
     grad_inputs = wide_value(jnp.stack(place(grad_rows, m)))
-    one_own, two_own = seq_total_parts(one_own), seq_total(two_own)
+    one_own, two_own = seq_total_parts(one_own, two, two_own), seq_total(two_own)
     grads = finish(place_ids, one_own, swap(one_own, "seq", 1), two_own, swap(two_own, "seq", 1), units, rank)
 
-    kept_rows, sent_rows = results_of(place_ids, own_parts, came, low_down, exit_full)
     output = jnp.concatenate(place([kept_rows, swap(sent_rows, "mp", 2)], y), 0)
     in_entry_grad, in_exit_grad, out_entry_grad, out_exit_grad, gate_entry_grad, gate_exit_grad = grads[:6]
     up_entry_grad, up_exit_grad, down_entry_grad, down_exit_grad = grads[6:]

time: 539 us -> 535 us (level)
  waiting for transfers between devices: 178 us -> 169 us
    ppermute x55, waiting for transfers between devices: 178 us -> 169 us  [swap(): lax.ppermute(value, axis, [(i, i ^ bit) for i in range(lax.axis_size(axis...]
    unnamed x66 -> x70, local copies, waits for them, and re-layouts: 10.5 us -> 11.2 us
  transfers between devices with their start and end apart: 57 -> 57, of which waited for: 23 -> 25; matrix products, arithmetic and copies ran while one was open for 4% -> 4% of each run, Pallas kernels for 41% -> 42%
where the time goes in v4:
time: 535 us; the launch traced here: 527 us
  Pallas kernels  267 us (50%)
  waiting for transfers between devices  169 us (32%)
  starting transfers between devices  54.5 us (10%)
  local copies, waits for them, and re-layouts  23.6 us (4%)
  other arithmetic  11.4 us (2%)
    pallas_call x17, Pallas kernels, kernel_call(): pl.pallas_call(body, out_shape=tuple(outs), in_specs=[pl.BlockSpec(memory...  266 us
    ppermute x55, waiting for transfers between devices, swap(): lax.ppermute(value, axis, [(i, i ^ bit) for i in range(lax.axis_size(axis...  169 us
    ppermute x55, starting transfers between devices, swap(): lax.ppermute(value, axis, [(i, i ^ bit) for i in range(lax.axis_size(axis...  50.9 us
    unnamed x70, local copies, waits for them, and re-layouts  11.2 us
  transfers between devices with their start and end apart: 57, of which 25 were waited for; matrix products, arithmetic and copies ran while one was open for 4% of the time, Pallas kernels for 42%

profile of v4, /device:TPU:0, one launch (start us, length us, event | category | flops | bytes accessed | tf_op | source)
XLA Modules:
  0.0 527.5 jit_solution(7497636872729017909)
XLA Ops:
  9.4 7.3 %pack_first.1 = (bf16[2416,384]{1,0:T(8,128)(2,1)}, bf16[2000,384]{1,0:T(8,128)(2,1)}, bf16[2000,384]{1,0:T(8,128)(2,1)}, bf16[512,384]{1,0:T(8,128)(2,1)}, bf16...) custom-call(s32[4]{0:T(128)} %pad_add_fusion.2.place_ref.refs_0_, bf16[4,512,384]{2,1,0:T(8,128)(2,1)} %inputs.1, ...), custom_call_target="tpu_custom_call" | custom-call | bytes 16000000 | tf_op jit(solution)/shard_map/pack_first/pallas_call | solution.py:341
  16.7 10.4 %collective-permute-done.1.refs_24_.refs_22_ = bf16[1152,384]{1,0:T(8,128)(2,1)S(1)} collective-permute-done((bf16[1152,384]{1,0:T(8,128)(2,1)}, bf16[1152,384]{1,0:T(8,128)(2,1)S(1)}, u32[]{:S(2)}, u32[]{:S(2)}) %collective-permute-start.1) | collective-permute-done | bytes 884768 | tf_op jit(solution)/shard_map/ppermute | solution.py:1168
  32.6 20.2 %collective-permute-done.10.refs_26_.refs_24_ = bf16[1152,384]{1,0:T(8,128)(2,1)} collective-permute-done((bf16[1152,384]{1,0:T(8,128)(2,1)S(1)}, bf16[1152,384]{1,0:T(8,128)(2,1)}, u32[]{:S(2)}, u32[]{:S(2)}) %collective-permute-start.10) | collective-permute-done | bytes 884768 | tf_op jit(solution)/shard_map/ppermute | solution.py:1168
  52.7 16.4 %collective-permute-done.7.refs_22_.refs_20_ = bf16[1152,384]{1,0:T(8,128)(2,1)} collective-permute-done((bf16[1152,384]{1,0:T(8,128)(2,1)S(1)}, bf16[1152,384]{1,0:T(8,128)(2,1)}, u32[]{:S(2)}, u32[]{:S(2)}) %collective-permute-start.7) | collective-permute-done | bytes 884768 | tf_op jit(solution)/shard_map/ppermute | solution.py:1168
  72.0 5.2 pack_second.1
  81.7 24.7 %collective-permute-done.2.refs_17_.refs_36_.refs_26_ = bf16[2000,384]{1,0:T(8,128)(2,1)} collective-permute-done((bf16[2000,384]{1,0:T(8,128)(2,1)}, bf16[2000,384]{1,0:T(8,128)(2,1)}, u32[]{:S(2)}, u32[]{:S(2)}) %collective-permute-start.2) | collective-permute-done | bytes 1536032 | tf_op jit(solution)/shard_map/ppermute | solution.py:1168
  107.2 5.5 %collective-permute-done.13.refs_30_.refs_34_.refs_24_.refs_28_ = bf16[1904,384]{1,0:T(8,128)(2,1)S(1)} collective-permute-done((bf16[1904,384]{1,0:T(8,128)(2,1)S(1)}, bf16[1904,384]{1,0:T(8,128)(2,1)S(1)}, u32[]{:S(2)}, u32[]{:S(2)}) %collective-permute-start.13) | collective-permute-done | bytes 1462304 | tf_op jit(solution)/shard_map/ppermute | solution.py:1168
  126.4 30.8 %mixer.1 = (bf16[4,512,1536]{2,1,0:T(8,128)(2,1)}, bf16[512,1536]{1,0:T(8,128)(2,1)}, bf16[512,1536]{1,0:T(8,128)(2,1)}, bf16[512,1536]{1,0:T(8,128)(2,1)}, f32[...) custom-call(s32[4]{0:T(128)} %pad_add_fusion.2.place_ref.refs_0_, ...), custom_call_target="tpu_custom_call" | custom-call | flops 9663676416 | bytes 50000000 | tf_op jit(solution)/shard_map/mixer/pallas_call | solution.py:341
  161.3 4.9 ready.1
  166.2 33.2 %feed_near.2 = (bf16[512,1664]{1,0:T(8,128)(2,1)}, bf16[512,1792]{1,0:T(8,128)(2,1)}, f32[1728,384]{1,0:T(8,128)}) custom-call(bf16[512,1536]{1,0:T(8,128)(2,1)} %get-tuple-element.140.refs_0_.refs_1_.refs_5_, bf16[4,512,128]{2,1,0:T(8,128)(2,1)} %get-tuple-element.153.refs_1_.refs_2_.refs_7_.refs_9_, ...), custom_call_target="tpu_custom_call" | custom-call | flops 19025362944 | bytes 30000000 | tf_op jit(solution)/shard_map/feed_near/pallas_call | solution.py:341
  202.9 33.2 %feed_near.3 = (bf16[512,1664]{1,0:T(8,128)(2,1)}, bf16[512,1792]{1,0:T(8,128)(2,1)}, f32[1728,384]{1,0:T(8,128)}) custom-call(bf16[512,1536]{1,0:T(8,128)(2,1)} %copy-done.1, bf16[2,512,128]{2,1,0:T(8,128)(2,1)} %copy-done.2, bf16[2,512,1536]{2,1,0:T(8,128)(2,1)} %get-tuple-element.147.refs_2_.refs_3_.refs_4_.refs_15_, ...), custom_call_target="tpu_custom_call" | custom-call | flops 19025362944 | bytes 30000000 | tf_op jit(solution)/shard_map/feed_near/pallas_call | solution.py:341
  243.2 16.3 %feed_far.6 = (bf16[512,1664]{1,0:T(8,128)(2,1)}, bf16[512,1792]{1,0:T(8,128)(2,1)}, f32[640,384]{1,0:T(8,128)}) custom-call(s32[1]{0:T(128)} %bitcast.2.refs_0_, bf16[512,1536]{1,0:T(8,128)(2,1)} %copy-done.1, bf16[2,512,128]{2,1,0:T(8,128)(2,1)} %copy-done.2, bf16[2,512,1536]{2,1,0:T(8,128)(2,1)} %get-tuple-element.147.refs_2_.refs_3_.refs_4_.refs_15_, ...), custom_call_target="tpu_custom_call" | custom-call | flops 7046430720 | bytes 30000000 | tf_op jit(solution)/shard_map/feed_far/pallas_call | solution.py:341
  259.5 13.3 %collective-permute-done.28.refs_6_ = bf16[3,144,1664]{2,1,0:T(8,128)(2,1)} collective-permute-done((bf16[3,144,1664]{2,1,0:T(8,128)(2,1)}, bf16[3,144,1664]{2,1,0:T(8,128)(2,1)}, u32[]{:S(2)}, u32[]{:S(2)}) %collective-permute-start.28) | collective-permute-done | bytes 1437728 | tf_op jit(solution)/shard_map/ppermute | solution.py:1168
  279.4 16.5 %feed_far.7 = (bf16[512,1664]{1,0:T(8,128)(2,1)}, bf16[512,1792]{1,0:T(8,128)(2,1)}, f32[576,384]{1,0:T(8,128)}) custom-call(s32[1]{0:T(128)} %bitcast.2.refs_0_, bf16[512,1536]{1,0:T(8,128)(2,1)} %copy-done.1, bf16[2,512,128]{2,1,0:T(8,128)(2,1)} %copy-done.2, bf16[2,512,1536]{2,1,0:T(8,128)(2,1)} %get-tuple-element.147.refs_2_.refs_3_.refs_4_.refs_15_, ...), custom_call_target="tpu_custom_call" | custom-call | flops 6341787648 | bytes 30000000 | tf_op jit(solution)/shard_map/feed_far/pallas_call | solution.py:341
  295.9 7.6 %collective-permute-done.26.refs_6_ = bf16[3,128,1664]{2,1,0:T(8,128)(2,1)S(1)} collective-permute-done((bf16[3,128,1664]{2,1,0:T(8,128)(2,1)}, bf16[3,128,1664]{2,1,0:T(8,128)(2,1)S(1)}, u32[]{:S(2)}, u32[]{:S(2)}) %collective-permute-start.26) | collective-permute-done | bytes 1277984 | tf_op jit(solution)/shard_map/ppermute | solution.py:1168
  304.0 4.5 collective-permute-done.31.refs_7_
  310.0 12.9 %feed_far.8 = (bf16[512,1664]{1,0:T(8,128)(2,1)}, bf16[512,1792]{1,0:T(8,128)(2,1)}, f32[512,384]{1,0:T(8,128)}) custom-call(s32[1]{0:T(128)} %bitcast.2.refs_0_, bf16[512,1536]{1,0:T(8,128)(2,1)} %copy-done.1, bf16[2,512,128]{2,1,0:T(8,128)(2,1)} %copy-done.2, bf16[2,512,1536]{2,1,0:T(8,128)(2,1)} %get-tuple-element.147.refs_2_.refs_3_.refs_4_.refs_15_, ...), custom_call_target="tpu_custom_call" | custom-call | flops 5637144576 | bytes 30000000 | tf_op jit(solution)/shard_map/feed_far/pallas_call | solution.py:341
  324.4 16.4 %feed_far.9 = (bf16[512,1664]{1,0:T(8,128)(2,1)}, bf16[512,1792]{1,0:T(8,128)(2,1)}, f32[4,160,384]{2,1,0:T(8,128)}) custom-call(s32[1]{0:T(128)} %bitcast.2.refs_0_, bf16[512,1536]{1,0:T(8,128)(2,1)} %get-tuple-element.140.refs_0_.refs_1_.refs_5_, bf16[4,512,128]{2,1,0:T(8,128)(2,1)} %get-tuple-element.153.refs_1_.refs_2_.refs_7_.refs_9_, ...), custom_call_target="tpu_custom_call" | custom-call | flops 7046430720 | bytes 30000000 | tf_op jit(solution)/shard_map/feed_far/pallas_call | solution.py:341
  340.8 16.2 %feed_far.10 = (bf16[512,1664]{1,0:T(8,128)(2,1)}, bf16[512,1792]{1,0:T(8,128)(2,1)}, f32[4,144,384]{2,1,0:T(8,128)}) custom-call(s32[1]{0:T(128)} %bitcast.2.refs_0_, bf16[512,1536]{1,0:T(8,128)(2,1)} %get-tuple-element.140.refs_0_.refs_1_.refs_5_, bf16[4,512,128]{2,1,0:T(8,128)(2,1)} %get-tuple-element.153.refs_1_.refs_2_.refs_7_.refs_9_, ...), custom_call_target="tpu_custom_call" | custom-call | flops 6341787648 | bytes 30000000 | tf_op jit(solution)/shard_map/feed_far/pallas_call | solution.py:341
  357.0 12.9 %feed_far.11 = (bf16[512,1664]{1,0:T(8,128)(2,1)}, bf16[512,1792]{1,0:T(8,128)(2,1)}, f32[4,128,384]{2,1,0:T(8,128)}) custom-call(s32[1]{0:T(128)} %bitcast.2.refs_0_, bf16[512,1536]{1,0:T(8,128)(2,1)} %get-tuple-element.140.refs_0_.refs_1_.refs_5_, bf16[4,512,128]{2,1,0:T(8,128)(2,1)} %get-tuple-element.153.refs_1_.refs_2_.refs_7_.refs_9_, ...), custom_call_target="tpu_custom_call" | custom-call | flops 5637144576 | bytes 30000000 | tf_op jit(solution)/shard_map/feed_far/pallas_call | solution.py:341
  371.2 21.9 %branch_back.1 = (f32[512,1536]{1,0:T(8,128)}, bf16[512,1536]{1,0:T(8,128)(2,1)}, bf16[512,1536]{1,0:T(8,128)(2,1)}, f32[8,1536]{1,0:T(8,128)}, bf16[2752,384]{1...) custom-call(s32[4]{0:T(128)} %pad_add_fusion.2.place_ref.refs_0_, ...), custom_call_target="tpu_custom_call" | custom-call | flops 3221225472 | bytes 40000000 | tf_op jit(solution)/shard_map/branch_back/pallas_call | solution.py:341
  398.5 5.7 %collective-permute-done.40 = bf16[2,512,128]{2,1,0:T(8,128)(2,1)S(1)} collective-permute-done((bf16[2,512,128]{2,1,0:T(8,128)(2,1)S(1)}, bf16[2,512,128]{2,1,0:T(8,128)(2,1)S(1)}, u32[]{:S(2)}, u32[]{:S(2)}) %collective-permute-start.40) | collective-permute-done | bytes 262176 | tf_op jit(solution)/shard_map/ppermute | solution.py:1168
  410.9 27.5 %input_back.1 = (bf16[4,512,384]{2,1,0:T(8,128)(2,1)}, bf16[1280,384]{1,0:T(8,128)(2,1)}, bf16[1280,384]{1,0:T(8,128)(2,1)}) custom-call(s32[4]{0:T(128)} %pad_add_fusion.2.place_ref.refs_0_, bf16[512,1536]{1,0:T(8,128)(2,1)} %get-tuple-element.196.refs_1_, bf16[512,1536]{1,0:T(8,128)(2,1)} %get-tuple-element.197.refs_2_, ...), custom_call_target="tpu_custom_call" | custom-call | flops 7247757312 | bytes 40000000 | tf_op jit(solution)/shard_map/input_back/pallas_call | solution.py:341
  438.5 3.7 collective-permute-done.37
  442.3 3.7 collective-permute-done.35
  446.4 3.8 results.1
  453.3 10.3 %collective-permute-done.49 = bf16[560,384]{1,0:T(8,128)(2,1)S(1)} collective-permute-done((bf16[560,384]{1,0:T(8,128)(2,1)}, bf16[560,384]{1,0:T(8,128)(2,1)S(1)}, u32[]{:S(2)}, u32[]{:S(2)}) %collective-permute-start.49) | collective-permute-done | bytes 430112 | tf_op jit(solution)/shard_map/ppermute | solution.py:1168
  473.8 9.3 %collective-permute-done.45 = bf16[320,384]{1,0:T(8,128)(2,1)S(1)} collective-permute-done((bf16[320,384]{1,0:T(8,128)(2,1)S(1)}, bf16[320,384]{1,0:T(8,128)(2,1)S(1)}, u32[]{:S(2)}, u32[]{:S(2)}) %collective-permute-start.45) | collective-permute-done | bytes 245792 | tf_op jit(solution)/shard_map/ppermute | solution.py:1168
  486.4 9.0 %collective-permute-done.51 = bf16[280,384]{1,0:T(8,128)(2,1)S(1)} collective-permute-done((bf16[280,384]{1,0:T(8,128)(2,1)S(1)}, bf16[280,384]{1,0:T(8,128)(2,1)S(1)}, u32[]{:S(2)}, u32[]{:S(2)}) %collective-permute-start.51) | collective-permute-done | bytes 215072 | tf_op jit(solution)/shard_map/ppermute | solution.py:1168
  504.3 6.5 %collective-permute-done.52 = bf16[560,384]{1,0:T(8,128)(2,1)S(1)} collective-permute-done((bf16[560,384]{1,0:T(8,128)(2,1)S(1)}, bf16[560,384]{1,0:T(8,128)(2,1)S(1)}, u32[]{:S(2)}, u32[]{:S(2)}) %collective-permute-start.52) | collective-permute-done | bytes 430112 | tf_op jit(solution)/shard_map/ppermute | solution.py:1168
  512.7 5.7 %collective-permute-done.47 = bf16[512,384]{1,0:T(8,128)(2,1)S(1)} collective-permute-done((bf16[512,384]{1,0:T(8,128)(2,1)S(1)}, bf16[512,384]{1,0:T(8,128)(2,1)S(1)}, u32[]{:S(2)}, u32[]{:S(2)}) %collective-permute-start.47) | collective-permute-done | bytes 393248 | tf_op jit(solution)/shard_map/ppermute | solution.py:1168
  522.6 4.5 finish.1
  (225 shorter events, 105.4 us)
Async XLA Ops:
  4.2 22.9 %collective-permute-start.1 = (bf16[1152,384]{1,0:T(8,128)(2,1)}, bf16[1152,384]{1,0:T(8,128)(2,1)S(1)}, u32[]{:S(2)}, u32[]{:S(2)}) collective-permute-start(bf16[1152,384]{1,0:T(8,128)(2,1)} %pack_in.1), channel_id=1, source_target_pairs={{0,2},{1,3},{2,0},{3,1},{4,6},{5,7},{6,4},{7,5},{8,10},{9,11},{10,... | collective-permute-start | bytes 2654216 | tf_op jit(solution)/shard_map/ppermute | solution.py:1168
  7.3 21.3 %collective-permute-start = (bf16[1152,384]{1,0:T(8,128)(2,1)}, bf16[1152,384]{1,0:T(8,128)(2,1)S(1)}, u32[]{:S(2)}, u32[]{:S(2)}) collective-permute-start(bf16[1152,384]{1,0:T(8,128)(2,1)} %pack_in.1), channel_id=1, source_target_pairs={{0,1},{1,0},{2,3},{3,2},{4,5},{5,4},{6,7},{7,6},{8,9},{9,8},{10,11... | collective-permute-start | bytes 2654216 | tf_op jit(solution)/shard_map/ppermute | solution.py:1168
  28.6 42.2 %collective-permute-start.4 = (bf16[2416,384]{1,0:T(8,128)(2,1)}, bf16[2416,384]{1,0:T(8,128)(2,1)}, u32[]{:S(2)}, u32[]{:S(2)}) collective-permute-start(bf16[2416,384]{1,0:T(8,128)(2,1)} %get-tuple-element.134), channel_id=1, source_target_pairs={{0,3},{1,2},{2,1},{3,0},{4,7},{5,6},{6,5},{7,4},{8,11},{9,10},{10,... | collective-permute-start | bytes 5566472 | tf_op jit(solution)/shard_map/ppermute | solution.py:1168
  30.0 22.7 %collective-permute-start.10 = (bf16[1152,384]{1,0:T(8,128)(2,1)S(1)}, bf16[1152,384]{1,0:T(8,128)(2,1)}, u32[]{:S(2)}, u32[]{:S(2)}) collective-permute-start(bf16[1152,384]{1,0:T(8,128)(2,1)S(1)} %collective-permute-done.1.refs_24_.refs_22_), channel_id=1, source_target_pairs={{0,8},{4,12},{8,0},{12,4},{16,24},{20,28},{24,16},{28,20},{1,9},{5... | collective-permute-start | bytes 2654216 | tf_op jit(solution)/shard_map/ppermute | solution.py:1168
  31.6 37.6 %collective-permute-start.7 = (bf16[1152,384]{1,0:T(8,128)(2,1)S(1)}, bf16[1152,384]{1,0:T(8,128)(2,1)}, u32[]{:S(2)}, u32[]{:S(2)}) collective-permute-start(bf16[1152,384]{1,0:T(8,128)(2,1)S(1)} %collective-permute-done.refs_20_.refs_18_), channel_id=1, source_target_pairs={{0,8},{4,12},{8,0},{12,4},{16,24},{20,28},{24,16},{28,20},{1,9},{5... | collective-permute-start | bytes 2654216 | tf_op jit(solution)/shard_map/ppermute | solution.py:1168
  32.0 37.1 %collective-permute-start.9 = (bf16[1152,384]{1,0:T(8,128)(2,1)S(1)}, bf16[1152,384]{1,0:T(8,128)(2,1)S(1)}, u32[]{:S(2)}, u32[]{:S(2)}) collective-permute-start(bf16[1152,384]{1,0:T(8,128)(2,1)S(1)} %collective-permute-done.1.refs_24_.refs_22_), channel_id=1, source_target_pairs={{0,4},{4,0},{8,12},{12,8},{16,20},{20,16},{24,28},{28,24},{1,5},{5... | collective-permute-start | bytes 2654216 | tf_op jit(solution)/shard_map/ppermute | solution.py:1168
  32.0 46.7 %collective-permute-start.6 = (bf16[1152,384]{1,0:T(8,128)(2,1)S(1)}, bf16[1152,384]{1,0:T(8,128)(2,1)}, u32[]{:S(2)}, u32[]{:S(2)}) collective-permute-start(bf16[1152,384]{1,0:T(8,128)(2,1)S(1)} %collective-permute-done.refs_20_.refs_18_), channel_id=1, source_target_pairs={{0,4},{4,0},{8,12},{12,8},{16,20},{20,16},{24,28},{28,24},{1,5},{5... | collective-permute-start | bytes 2654216 | tf_op jit(solution)/shard_map/ppermute | solution.py:1168
  52.7 26.1 %collective-permute-start.11 = (bf16[1152,384]{1,0:T(8,128)(2,1)}, bf16[1152,384]{1,0:T(8,128)(2,1)}, u32[]{:S(2)}, u32[]{:S(2)}) collective-permute-start(bf16[1152,384]{1,0:T(8,128)(2,1)} %collective-permute-done.10.refs_26_.refs_24_), channel_id=1, source_target_pairs={{0,4},{4,0},{8,12},{12,8},{16,20},{20,16},{24,28},{28,24},{1,5},{5... | collective-permute-start | bytes 2654216 | tf_op jit(solution)/shard_map/ppermute | solution.py:1168
  70.1 36.3 %collective-permute-start.2 = (bf16[2000,384]{1,0:T(8,128)(2,1)}, bf16[2000,384]{1,0:T(8,128)(2,1)}, u32[]{:S(2)}, u32[]{:S(2)}) collective-permute-start(bf16[2000,384]{1,0:T(8,128)(2,1)} %get-tuple-element.131), channel_id=1, source_target_pairs={{0,1},{1,0},{2,3},{3,2},{4,5},{5,4},{6,7},{7,6},{8,9},{9,8},{10,11... | collective-permute-start | bytes 4608008 | tf_op jit(solution)/shard_map/ppermute | solution.py:1168
  70.8 35.9 %collective-permute-start.3 = (bf16[2000,384]{1,0:T(8,128)(2,1)}, bf16[2000,384]{1,0:T(8,128)(2,1)}, u32[]{:S(2)}, u32[]{:S(2)}) collective-permute-start(bf16[2000,384]{1,0:T(8,128)(2,1)} %get-tuple-element.132), channel_id=1, source_target_pairs={{0,2},{1,3},{2,0},{3,1},{4,6},{5,7},{6,4},{7,5},{8,10},{9,11},{10,... | collective-permute-start | bytes 4608008 | tf_op jit(solution)/shard_map/ppermute | solution.py:1168
  78.8 33.9 %collective-permute-start.13 = (bf16[1904,384]{1,0:T(8,128)(2,1)S(1)}, bf16[1904,384]{1,0:T(8,128)(2,1)S(1)}, u32[]{:S(2)}, u32[]{:S(2)}) collective-permute-start(bf16[1904,384]{1,0:T(8,128)(2,1)S(1)} %slice.137.refs_28_.refs_32_.refs_22_.refs_26_), channel_id=1, source_target_pairs={{0,8},{4,12},{8,0},{12,4},{16,24},{20,28},{24,16},{28,20},{1,9},{5... | collective-permute-start | bytes 4386824 | tf_op jit(solution)/shard_map/ppermute | solution.py:1168
  121.5 38.8 %collective-permute-start.20 = (bf16[2,512,384]{2,1,0:T(8,128)(2,1)}, bf16[2,512,384]{2,1,0:T(8,128)(2,1)S(1)}, u32[]{:S(2)}, u32[]{:S(2)}) collective-permute-start(bf16[2,512,384]{2,1,0:T(8,128)(2,1)} %get-tuple-element.146), channel_id=1, source_target_pairs={{0,3},{1,2},{2,1},{3,0},{4,7},{5,6},{6,5},{7,4},{8,11},{9,10},{10,... | collective-permute-start | bytes 2359304 | tf_op jit(solution)/shard_map/ppermute | solution.py:1168
  123.2 37.2 %collective-permute-start.18 = (bf16[2,512,384]{2,1,0:T(8,128)(2,1)}, bf16[2,512,384]{2,1,0:T(8,128)(2,1)}, u32[]{:S(2)}, u32[]{:S(2)}) collective-permute-start(bf16[2,512,384]{2,1,0:T(8,128)(2,1)} %get-tuple-element.146), channel_id=1, source_target_pairs={{0,2},{1,3},{2,0},{3,1},{4,6},{5,7},{6,4},{7,5},{8,10},{9,11},{10,... | collective-permute-start | bytes 2359304 | tf_op jit(solution)/shard_map/ppermute | solution.py:1168
  124.6 34.5 %collective-permute-start.19 = (bf16[2,512,384]{2,1,0:T(8,128)(2,1)}, bf16[2,512,384]{2,1,0:T(8,128)(2,1)}, u32[]{:S(2)}, u32[]{:S(2)}) collective-permute-start(bf16[2,512,384]{2,1,0:T(8,128)(2,1)} %get-tuple-element.145.rows_mine), channel_id=1, source_target_pairs={{0,1},{1,0},{2,3},{3,2},{4,5},{5,4},{6,7},{7,6},{8,9},{9,8},{10,11... | collective-permute-start | bytes 2359304 | tf_op jit(solution)/shard_map/ppermute | solution.py:1168
  125.1 76.2 %collective-permute-start.22 = (bf16[3,160,1664]{2,1,0:T(8,128)(2,1)}, bf16[3,160,1664]{2,1,0:T(8,128)(2,1)}, u32[]{:S(2)}, u32[]{:S(2)}) collective-permute-start(bf16[3,160,1664]{2,1,0:T(8,128)(2,1)} %get-tuple-element.152), channel_id=1, source_target_pairs={{0,2},{1,3},{2,0},{3,1},{4,6},{5,7},{6,4},{7,5},{8,10},{9,11},{10,... | collective-permute-start | bytes 4792328 | tf_op jit(solution)/shard_map/ppermute | solution.py:1168
  157.2 42.3 %collective-permute-start.17 = (bf16[512,1536]{1,0:T(8,128)(2,1)}, bf16[512,1536]{1,0:T(8,128)(2,1)S(1)}, u32[]{:S(2)}, u32[]{:S(2)}) collective-permute-start(bf16[512,1536]{1,0:T(8,128)(2,1)} %get-tuple-element.140.refs_0_.refs_1_.refs_5_), channel_id=1, source_target_pairs={{0,1},{1,0},{2,3},{3,2},{4,5},{5,4},{6,7},{7,6},{8,9},{9,8},{10,11... | collective-permute-start | bytes 4718600 | tf_op jit(solution)/shard_map/ppermute | solution.py:1168
  159.0 79.5 %collective-permute-start.27 = (bf16[3,144,1664]{2,1,0:T(8,128)(2,1)}, bf16[3,144,1664]{2,1,0:T(8,128)(2,1)}, u32[]{:S(2)}, u32[]{:S(2)}) collective-permute-start(bf16[3,144,1664]{2,1,0:T(8,128)(2,1)} %get-tuple-element.163), channel_id=1, source_target_pairs={{0,2},{1,3},{2,0},{3,1},{4,6},{5,7},{6,4},{7,5},{8,10},{9,11},{10,... | collective-permute-start | bytes 4313096 | tf_op jit(solution)/shard_map/ppermute | solution.py:1168
  201.3 37.2 %collective-permute-start.23 = (bf16[3,160,1664]{2,1,0:T(8,128)(2,1)}, bf16[3,160,1664]{2,1,0:T(8,128)(2,1)S(1)}, u32[]{:S(2)}, u32[]{:S(2)}) collective-permute-start(bf16[3,160,1664]{2,1,0:T(8,128)(2,1)} %collective-permute-done.22.refs_5_), channel_id=1, source_target_pairs={{0,8},{4,12},{8,0},{12,4},{16,24},{20,28},{24,16},{28,20},{1,9},{5... | collective-permute-start | bytes 4792328 | tf_op jit(solution)/shard_map/ppermute | solution.py:1168
  238.6 34.2 %collective-permute-start.28 = (bf16[3,144,1664]{2,1,0:T(8,128)(2,1)}, bf16[3,144,1664]{2,1,0:T(8,128)(2,1)}, u32[]{:S(2)}, u32[]{:S(2)}) collective-permute-start(bf16[3,144,1664]{2,1,0:T(8,128)(2,1)} %collective-permute-done.27.refs_5_), channel_id=1, source_target_pairs={{0,8},{4,12},{8,0},{12,4},{16,24},{20,28},{24,16},{28,20},{1,9},{5... | collective-permute-start | bytes 4313096 | tf_op jit(solution)/shard_map/ppermute | solution.py:1168
  240.2 33.1 %collective-permute-start.21 = (bf16[3,128,1664]{2,1,0:T(8,128)(2,1)S(1)}, bf16[3,128,1664]{2,1,0:T(8,128)(2,1)}, u32[]{:S(2)}, u32[]{:S(2)}) collective-permute-start(bf16[3,128,1664]{2,1,0:T(8,128)(2,1)S(1)} %copy-done.31), channel_id=1, source_target_pairs={{0,2},{1,3},{2,0},{3,1},{4,6},{5,7},{6,4},{7,5},{8,10},{9,11},{10,... | collective-permute-start | bytes 3833864 | tf_op jit(solution)/shard_map/ppermute | solution.py:1168
  273.3 30.2 %collective-permute-start.26 = (bf16[3,128,1664]{2,1,0:T(8,128)(2,1)}, bf16[3,128,1664]{2,1,0:T(8,128)(2,1)S(1)}, u32[]{:S(2)}, u32[]{:S(2)}) collective-permute-start(bf16[3,128,1664]{2,1,0:T(8,128)(2,1)} %collective-permute-done.21.refs_5_), channel_id=1, source_target_pairs={{0,8},{4,12},{8,0},{12,4},{16,24},{20,28},{24,16},{28,20},{1,9},{5... | collective-permute-start | bytes 3833864 | tf_op jit(solution)/shard_map/ppermute | solution.py:1168
  322.9 47.1 %collective-permute-start.33 = (bf16[512,1792]{1,0:T(8,128)(2,1)}, bf16[512,1792]{1,0:T(8,128)(2,1)S(1)}, u32[]{:S(2)}, u32[]{:S(2)}) collective-permute-start(bf16[512,1792]{1,0:T(8,128)(2,1)} %get-tuple-element.174), channel_id=1, source_target_pairs={{0,1},{1,0},{2,3},{3,2},{4,5},{5,4},{6,7},{7,6},{8,9},{9,8},{10,11... | collective-permute-start | bytes 5505032 | tf_op jit(solution)/shard_map/ppermute | solution.py:1168
  397.0 41.5 %collective-permute-start.38 = (bf16[4,512,384]{2,1,0:T(8,128)(2,1)}, bf16[4,512,384]{2,1,0:T(8,128)(2,1)S(1)}, u32[]{:S(2)}, u32[]{:S(2)}) collective-permute-start(bf16[4,512,384]{2,1,0:T(8,128)(2,1)} %get-tuple-element.195), channel_id=1, source_target_pairs={{0,1},{1,0},{2,3},{3,2},{4,5},{5,4},{6,7},{7,6},{8,9},{9,8},{10,11... | collective-permute-start | bytes 4718600 | tf_op jit(solution)/shard_map/ppermute | solution.py:1168
  407.3 38.7 %collective-permute-start.36 = (bf16[1120,384]{1,0:T(8,128)(2,1)S(1)}, bf16[1120,384]{1,0:T(8,128)(2,1)S(1)}, u32[]{:S(2)}, u32[]{:S(2)}) collective-permute-start(bf16[1120,384]{1,0:T(8,128)(2,1)S(1)} %slice.143), channel_id=1, source_target_pairs={{0,2},{1,3},{2,0},{3,1},{4,6},{5,7},{6,4},{7,5},{8,10},{9,11},{10,... | collective-permute-start | bytes 2580488 | tf_op jit(solution)/shard_map/ppermute | solution.py:1168
  408.1 34.2 %collective-permute-start.37 = (bf16[256,384]{1,0:T(8,128)(2,1)S(1)}, bf16[256,384]{1,0:T(8,128)(2,1)S(1)}, u32[]{:S(2)}, u32[]{:S(2)}) collective-permute-start(bf16[256,384]{1,0:T(8,128)(2,1)S(1)} %get-tuple-element.230), channel_id=1, source_target_pairs={{0,3},{1,2},{2,1},{3,0},{4,7},{5,6},{6,5},{7,4},{8,11},{9,10},{10,... | collective-permute-start | bytes 589832 | tf_op jit(solution)/shard_map/ppermute | solution.py:1168
  409.5 36.5 %collective-permute-start.35 = (bf16[256,384]{1,0:T(8,128)(2,1)S(1)}, bf16[256,384]{1,0:T(8,128)(2,1)S(1)}, u32[]{:S(2)}, u32[]{:S(2)}) collective-permute-start(bf16[256,384]{1,0:T(8,128)(2,1)S(1)} %get-tuple-element.231), channel_id=1, source_target_pairs={{0,1},{1,0},{2,3},{3,2},{4,5},{5,4},{6,7},{7,6},{8,9},{9,8},{10,11... | collective-permute-start | bytes 589832 | tf_op jit(solution)/shard_map/ppermute | solution.py:1168
  452.7 43.3 %collective-permute-start.41 = (bf16[2,512,384]{2,1,0:T(8,128)(2,1)}, bf16[2,512,384]{2,1,0:T(8,128)(2,1)}, u32[]{:S(2)}, u32[]{:S(2)}) collective-permute-start(bf16[2,512,384]{2,1,0:T(8,128)(2,1)} %get-tuple-element.211), channel_id=1, source_target_pairs={{0,2},{1,3},{2,0},{3,1},{4,6},{5,7},{6,4},{7,5},{8,10},{9,11},{10,... | collective-permute-start | bytes 2359304 | tf_op jit(solution)/shard_map/ppermute | solution.py:1168
  464.7 18.4 %collective-permute-start.45 = (bf16[320,384]{1,0:T(8,128)(2,1)S(1)}, bf16[320,384]{1,0:T(8,128)(2,1)S(1)}, u32[]{:S(2)}, u32[]{:S(2)}) collective-permute-start(bf16[320,384]{1,0:T(8,128)(2,1)S(1)} %get-tuple-element.243), channel_id=1, source_target_pairs={{0,2},{1,3},{2,0},{3,1},{4,6},{5,7},{6,4},{7,5},{8,10},{9,11},{10,... | collective-permute-start | bytes 737288 | tf_op jit(solution)/shard_map/ppermute | solution.py:1168
  466.0 17.1 %collective-permute-start.44 = (bf16[320,384]{1,0:T(8,128)(2,1)S(1)}, bf16[320,384]{1,0:T(8,128)(2,1)S(1)}, u32[]{:S(2)}, u32[]{:S(2)}) collective-permute-start(bf16[320,384]{1,0:T(8,128)(2,1)S(1)} %get-tuple-element.244), channel_id=1, source_target_pairs={{0,1},{1,0},{2,3},{3,2},{4,5},{5,4},{6,7},{7,6},{8,9},{9,8},{10,11... | collective-permute-start | bytes 737288 | tf_op jit(solution)/shard_map/ppermute | solution.py:1168
  484.7 17.5 %collective-permute-start.54 = (bf16[320,384]{1,0:T(8,128)(2,1)S(1)}, bf16[320,384]{1,0:T(8,128)(2,1)S(1)}, u32[]{:S(2)}, u32[]{:S(2)}) collective-permute-start(bf16[320,384]{1,0:T(8,128)(2,1)S(1)} %add_convert_fusion.6), channel_id=1, source_target_pairs={{0,8},{4,12},{8,0},{12,4},{16,24},{20,28},{24,16},{28,20},{1,9},{5... | collective-permute-start | bytes 737288 | tf_op jit(solution)/shard_map/ppermute | solution.py:1168
  499.2 19.1 %collective-permute-start.47 = (bf16[512,384]{1,0:T(8,128)(2,1)S(1)}, bf16[512,384]{1,0:T(8,128)(2,1)S(1)}, u32[]{:S(2)}, u32[]{:S(2)}) collective-permute-start(bf16[512,384]{1,0:T(8,128)(2,1)S(1)} %get-tuple-element.217), channel_id=1, source_target_pairs={{0,2},{1,3},{2,0},{3,1},{4,6},{5,7},{6,4},{7,5},{8,10},{9,11},{10,... | collective-permute-start | bytes 1179656 | tf_op jit(solution)/shard_map/ppermute | solution.py:1168
  499.9 18.4 %collective-permute-start.48 = (bf16[512,384]{1,0:T(8,128)(2,1)S(1)}, bf16[512,384]{1,0:T(8,128)(2,1)S(1)}, u32[]{:S(2)}, u32[]{:S(2)}) collective-permute-start(bf16[512,384]{1,0:T(8,128)(2,1)S(1)} %get-tuple-element.218), channel_id=1, source_target_pairs={{0,3},{1,2},{2,1},{3,0},{4,7},{5,6},{6,5},{7,4},{8,11},{9,10},{10,... | collective-permute-start | bytes 1179656 | tf_op jit(solution)/shard_map/ppermute | solution.py:1168
  (60 other events, 680.2 us)

commit v5 on v4

--- a/solution.py
+++ b/solution.py
@@ -1351,7 +1351,7 @@
     mine_zero = feed(*mine, far_zero, at_quarter, add_tokens=near_mine[:2], add_grads=next_zero[2], settle=True)
     far_one = spread_far(far_first[1], near_mine[2], next_zero[2])
     next_one = feed(*other, far_one, at_quarter, add_tokens=next_zero[:2])
-    far_two = spread_far(far_first[2], next_zero[2], next_one[2])
+    far_two = spread_far(far_first[2], near_next[2], next_one[2])
     down_next, back_next, next_grads = feed(*other, far_two, at_quarter, add_tokens=next_one[:2])
     got_back = swap(back_next, "mp", 1)
     mine_one = feed(*mine, far_one, at_quarter, add_tokens=mine_zero[:2], add_grads=next_one[2], settle=True)

time: 535 us -> 535 us (level)
  no operation moved by 1% of the time
where the time goes in v5:
time: 535 us; the launch traced here: 527 us
  Pallas kernels  267 us (50%)
  waiting for transfers between devices  169 us (32%)
  starting transfers between devices  54.5 us (10%)
  local copies, waits for them, and re-layouts  23.6 us (4%)
  other arithmetic  11.4 us (2%)
    pallas_call x17, Pallas kernels, kernel_call(): pl.pallas_call(body, out_shape=tuple(outs), in_specs=[pl.BlockSpec(memory...  266 us
    ppermute x55, waiting for transfers between devices, swap(): lax.ppermute(value, axis, [(i, i ^ bit) for i in range(lax.axis_size(axis...  169 us
    ppermute x55, starting transfers between devices, swap(): lax.ppermute(value, axis, [(i, i ^ bit) for i in range(lax.axis_size(axis...  50.9 us
    unnamed x70, local copies, waits for them, and re-layouts  11.2 us
  transfers between devices with their start and end apart: 57, of which 25 were waited for; matrix products, arithmetic and copies ran while one was open for 4% of the time, Pallas kernels for 42%

profile of v5, /device:TPU:0, one launch (start us, length us, event | category | flops | bytes accessed | tf_op | source)
XLA Modules:
  0.0 527.5 jit_solution(4147062796528745696)
XLA Ops:
  9.4 7.3 %pack_first.1 = (bf16[2416,384]{1,0:T(8,128)(2,1)}, bf16[2000,384]{1,0:T(8,128)(2,1)}, bf16[2000,384]{1,0:T(8,128)(2,1)}, bf16[512,384]{1,0:T(8,128)(2,1)}, bf16...) custom-call(s32[4]{0:T(128)} %pad_add_fusion.2.place_ref.refs_0_, bf16[4,512,384]{2,1,0:T(8,128)(2,1)} %inputs.1, ...), custom_call_target="tpu_custom_call" | custom-call | bytes 16000000 | tf_op jit(solution)/shard_map/pack_first/pallas_call | solution.py:341
  16.7 10.4 %collective-permute-done.1.refs_24_.refs_22_ = bf16[1152,384]{1,0:T(8,128)(2,1)S(1)} collective-permute-done((bf16[1152,384]{1,0:T(8,128)(2,1)}, bf16[1152,384]{1,0:T(8,128)(2,1)S(1)}, u32[]{:S(2)}, u32[]{:S(2)}) %collective-permute-start.1) | collective-permute-done | bytes 884768 | tf_op jit(solution)/shard_map/ppermute | solution.py:1168
  32.6 20.2 %collective-permute-done.10.refs_26_.refs_24_ = bf16[1152,384]{1,0:T(8,128)(2,1)} collective-permute-done((bf16[1152,384]{1,0:T(8,128)(2,1)S(1)}, bf16[1152,384]{1,0:T(8,128)(2,1)}, u32[]{:S(2)}, u32[]{:S(2)}) %collective-permute-start.10) | collective-permute-done | bytes 884768 | tf_op jit(solution)/shard_map/ppermute | solution.py:1168
  52.7 16.4 %collective-permute-done.7.refs_22_.refs_20_ = bf16[1152,384]{1,0:T(8,128)(2,1)} collective-permute-done((bf16[1152,384]{1,0:T(8,128)(2,1)S(1)}, bf16[1152,384]{1,0:T(8,128)(2,1)}, u32[]{:S(2)}, u32[]{:S(2)}) %collective-permute-start.7) | collective-permute-done | bytes 884768 | tf_op jit(solution)/shard_map/ppermute | solution.py:1168
  72.0 5.2 pack_second.1
  81.7 24.7 %collective-permute-done.2.refs_17_.refs_36_.refs_26_ = bf16[2000,384]{1,0:T(8,128)(2,1)} collective-permute-done((bf16[2000,384]{1,0:T(8,128)(2,1)}, bf16[2000,384]{1,0:T(8,128)(2,1)}, u32[]{:S(2)}, u32[]{:S(2)}) %collective-permute-start.2) | collective-permute-done | bytes 1536032 | tf_op jit(solution)/shard_map/ppermute | solution.py:1168
  107.2 5.5 %collective-permute-done.13.refs_30_.refs_34_.refs_24_.refs_28_ = bf16[1904,384]{1,0:T(8,128)(2,1)S(1)} collective-permute-done((bf16[1904,384]{1,0:T(8,128)(2,1)S(1)}, bf16[1904,384]{1,0:T(8,128)(2,1)S(1)}, u32[]{:S(2)}, u32[]{:S(2)}) %collective-permute-start.13) | collective-permute-done | bytes 1462304 | tf_op jit(solution)/shard_map/ppermute | solution.py:1168
  126.4 30.8 %mixer.1 = (bf16[4,512,1536]{2,1,0:T(8,128)(2,1)}, bf16[512,1536]{1,0:T(8,128)(2,1)}, bf16[512,1536]{1,0:T(8,128)(2,1)}, bf16[512,1536]{1,0:T(8,128)(2,1)}, f32[...) custom-call(s32[4]{0:T(128)} %pad_add_fusion.2.place_ref.refs_0_, ...), custom_call_target="tpu_custom_call" | custom-call | flops 9663676416 | bytes 50000000 | tf_op jit(solution)/shard_map/mixer/pallas_call | solution.py:341
  161.3 4.9 ready.1
  166.2 33.2 %feed_near.2 = (bf16[512,1664]{1,0:T(8,128)(2,1)}, bf16[512,1792]{1,0:T(8,128)(2,1)}, f32[1728,384]{1,0:T(8,128)}) custom-call(bf16[512,1536]{1,0:T(8,128)(2,1)} %get-tuple-element.140.refs_0_.refs_1_.refs_5_, bf16[4,512,128]{2,1,0:T(8,128)(2,1)} %get-tuple-element.152.refs_1_.refs_2_.refs_7_.refs_9_, ...), custom_call_target="tpu_custom_call" | custom-call | flops 19025362944 | bytes 30000000 | tf_op jit(solution)/shard_map/feed_near/pallas_call | solution.py:341
  202.9 33.2 %feed_near.3 = (bf16[512,1664]{1,0:T(8,128)(2,1)}, bf16[512,1792]{1,0:T(8,128)(2,1)}, f32[1728,384]{1,0:T(8,128)}) custom-call(bf16[512,1536]{1,0:T(8,128)(2,1)} %copy-done.1, bf16[2,512,128]{2,1,0:T(8,128)(2,1)} %copy-done.2, bf16[2,512,1536]{2,1,0:T(8,128)(2,1)} %get-tuple-element.147.refs_2_.refs_3_.refs_4_.refs_15_, ...), custom_call_target="tpu_custom_call" | custom-call | flops 19025362944 | bytes 30000000 | tf_op jit(solution)/shard_map/feed_near/pallas_call | solution.py:341
  243.2 16.3 %feed_far.6 = (bf16[512,1664]{1,0:T(8,128)(2,1)}, bf16[512,1792]{1,0:T(8,128)(2,1)}, f32[640,384]{1,0:T(8,128)}) custom-call(s32[1]{0:T(128)} %bitcast.2.refs_0_, bf16[512,1536]{1,0:T(8,128)(2,1)} %copy-done.1, bf16[2,512,128]{2,1,0:T(8,128)(2,1)} %copy-done.2, bf16[2,512,1536]{2,1,0:T(8,128)(2,1)} %get-tuple-element.147.refs_2_.refs_3_.refs_4_.refs_15_, ...), custom_call_target="tpu_custom_call" | custom-call | flops 7046430720 | bytes 30000000 | tf_op jit(solution)/shard_map/feed_far/pallas_call | solution.py:341
  259.5 13.3 %collective-permute-done.24.refs_6_ = bf16[3,144,1664]{2,1,0:T(8,128)(2,1)} collective-permute-done((bf16[3,144,1664]{2,1,0:T(8,128)(2,1)}, bf16[3,144,1664]{2,1,0:T(8,128)(2,1)}, u32[]{:S(2)}, u32[]{:S(2)}) %collective-permute-start.24) | collective-permute-done | bytes 1437728 | tf_op jit(solution)/shard_map/ppermute | solution.py:1168
  279.4 16.5 %feed_far.7 = (bf16[512,1664]{1,0:T(8,128)(2,1)}, bf16[512,1792]{1,0:T(8,128)(2,1)}, f32[576,384]{1,0:T(8,128)}) custom-call(s32[1]{0:T(128)} %bitcast.2.refs_0_, bf16[512,1536]{1,0:T(8,128)(2,1)} %copy-done.1, bf16[2,512,128]{2,1,0:T(8,128)(2,1)} %copy-done.2, bf16[2,512,1536]{2,1,0:T(8,128)(2,1)} %get-tuple-element.147.refs_2_.refs_3_.refs_4_.refs_15_, ...), custom_call_target="tpu_custom_call" | custom-call | flops 6341787648 | bytes 30000000 | tf_op jit(solution)/shard_map/feed_far/pallas_call | solution.py:341
  295.9 7.6 %collective-permute-done.22.refs_6_ = bf16[3,128,1664]{2,1,0:T(8,128)(2,1)S(1)} collective-permute-done((bf16[3,128,1664]{2,1,0:T(8,128)(2,1)}, bf16[3,128,1664]{2,1,0:T(8,128)(2,1)S(1)}, u32[]{:S(2)}, u32[]{:S(2)}) %collective-permute-start.22) | collective-permute-done | bytes 1277984 | tf_op jit(solution)/shard_map/ppermute | solution.py:1168
  304.0 4.5 collective-permute-done.31.refs_7_
  310.0 12.9 %feed_far.8 = (bf16[512,1664]{1,0:T(8,128)(2,1)}, bf16[512,1792]{1,0:T(8,128)(2,1)}, f32[512,384]{1,0:T(8,128)}) custom-call(s32[1]{0:T(128)} %bitcast.2.refs_0_, bf16[512,1536]{1,0:T(8,128)(2,1)} %copy-done.1, bf16[2,512,128]{2,1,0:T(8,128)(2,1)} %copy-done.2, bf16[2,512,1536]{2,1,0:T(8,128)(2,1)} %get-tuple-element.147.refs_2_.refs_3_.refs_4_.refs_15_, ...), custom_call_target="tpu_custom_call" | custom-call | flops 5637144576 | bytes 30000000 | tf_op jit(solution)/shard_map/feed_far/pallas_call | solution.py:341
  324.4 16.4 %feed_far.9 = (bf16[512,1664]{1,0:T(8,128)(2,1)}, bf16[512,1792]{1,0:T(8,128)(2,1)}, f32[4,160,384]{2,1,0:T(8,128)}) custom-call(s32[1]{0:T(128)} %bitcast.2.refs_0_, bf16[512,1536]{1,0:T(8,128)(2,1)} %get-tuple-element.140.refs_0_.refs_1_.refs_5_, bf16[4,512,128]{2,1,0:T(8,128)(2,1)} %get-tuple-element.152.refs_1_.refs_2_.refs_7_.refs_9_, ...), custom_call_target="tpu_custom_call" | custom-call | flops 7046430720 | bytes 30000000 | tf_op jit(solution)/shard_map/feed_far/pallas_call | solution.py:341
  340.8 16.2 %feed_far.10 = (bf16[512,1664]{1,0:T(8,128)(2,1)}, bf16[512,1792]{1,0:T(8,128)(2,1)}, f32[4,144,384]{2,1,0:T(8,128)}) custom-call(s32[1]{0:T(128)} %bitcast.2.refs_0_, bf16[512,1536]{1,0:T(8,128)(2,1)} %get-tuple-element.140.refs_0_.refs_1_.refs_5_, bf16[4,512,128]{2,1,0:T(8,128)(2,1)} %get-tuple-element.152.refs_1_.refs_2_.refs_7_.refs_9_, ...), custom_call_target="tpu_custom_call" | custom-call | flops 6341787648 | bytes 30000000 | tf_op jit(solution)/shard_map/feed_far/pallas_call | solution.py:341
  357.0 12.9 %feed_far.11 = (bf16[512,1664]{1,0:T(8,128)(2,1)}, bf16[512,1792]{1,0:T(8,128)(2,1)}, f32[4,128,384]{2,1,0:T(8,128)}) custom-call(s32[1]{0:T(128)} %bitcast.2.refs_0_, bf16[512,1536]{1,0:T(8,128)(2,1)} %get-tuple-element.140.refs_0_.refs_1_.refs_5_, bf16[4,512,128]{2,1,0:T(8,128)(2,1)} %get-tuple-element.152.refs_1_.refs_2_.refs_7_.refs_9_, ...), custom_call_target="tpu_custom_call" | custom-call | flops 5637144576 | bytes 30000000 | tf_op jit(solution)/shard_map/feed_far/pallas_call | solution.py:341
  371.2 21.9 %branch_back.1 = (f32[512,1536]{1,0:T(8,128)}, bf16[512,1536]{1,0:T(8,128)(2,1)}, bf16[512,1536]{1,0:T(8,128)(2,1)}, f32[8,1536]{1,0:T(8,128)}, bf16[2752,384]{1...) custom-call(s32[4]{0:T(128)} %pad_add_fusion.2.place_ref.refs_0_, ...), custom_call_target="tpu_custom_call" | custom-call | flops 3221225472 | bytes 40000000 | tf_op jit(solution)/shard_map/branch_back/pallas_call | solution.py:341
  398.5 5.7 %collective-permute-done.40 = bf16[2,512,128]{2,1,0:T(8,128)(2,1)S(1)} collective-permute-done((bf16[2,512,128]{2,1,0:T(8,128)(2,1)S(1)}, bf16[2,512,128]{2,1,0:T(8,128)(2,1)S(1)}, u32[]{:S(2)}, u32[]{:S(2)}) %collective-permute-start.40) | collective-permute-done | bytes 262176 | tf_op jit(solution)/shard_map/ppermute | solution.py:1168
  410.9 27.5 %input_back.1 = (bf16[4,512,384]{2,1,0:T(8,128)(2,1)}, bf16[1280,384]{1,0:T(8,128)(2,1)}, bf16[1280,384]{1,0:T(8,128)(2,1)}) custom-call(s32[4]{0:T(128)} %pad_add_fusion.2.place_ref.refs_0_, bf16[512,1536]{1,0:T(8,128)(2,1)} %get-tuple-element.196.refs_1_, bf16[512,1536]{1,0:T(8,128)(2,1)} %get-tuple-element.197.refs_2_, ...), custom_call_target="tpu_custom_call" | custom-call | flops 7247757312 | bytes 40000000 | tf_op jit(solution)/shard_map/input_back/pallas_call | solution.py:341
  438.5 3.7 collective-permute-done.37
  442.3 3.7 collective-permute-done.35
  446.4 3.8 results.1
  453.3 10.3 %collective-permute-done.49 = bf16[560,384]{1,0:T(8,128)(2,1)S(1)} collective-permute-done((bf16[560,384]{1,0:T(8,128)(2,1)}, bf16[560,384]{1,0:T(8,128)(2,1)S(1)}, u32[]{:S(2)}, u32[]{:S(2)}) %collective-permute-start.49) | collective-permute-done | bytes 430112 | tf_op jit(solution)/shard_map/ppermute | solution.py:1168
  473.8 9.3 %collective-permute-done.45 = bf16[320,384]{1,0:T(8,128)(2,1)S(1)} collective-permute-done((bf16[320,384]{1,0:T(8,128)(2,1)S(1)}, bf16[320,384]{1,0:T(8,128)(2,1)S(1)}, u32[]{:S(2)}, u32[]{:S(2)}) %collective-permute-start.45) | collective-permute-done | bytes 245792 | tf_op jit(solution)/shard_map/ppermute | solution.py:1168
  486.4 9.0 %collective-permute-done.51 = bf16[280,384]{1,0:T(8,128)(2,1)S(1)} collective-permute-done((bf16[280,384]{1,0:T(8,128)(2,1)S(1)}, bf16[280,384]{1,0:T(8,128)(2,1)S(1)}, u32[]{:S(2)}, u32[]{:S(2)}) %collective-permute-start.51) | collective-permute-done | bytes 215072 | tf_op jit(solution)/shard_map/ppermute | solution.py:1168
  504.3 6.5 %collective-permute-done.52 = bf16[560,384]{1,0:T(8,128)(2,1)S(1)} collective-permute-done((bf16[560,384]{1,0:T(8,128)(2,1)S(1)}, bf16[560,384]{1,0:T(8,128)(2,1)S(1)}, u32[]{:S(2)}, u32[]{:S(2)}) %collective-permute-start.52) | collective-permute-done | bytes 430112 | tf_op jit(solution)/shard_map/ppermute | solution.py:1168
  512.7 5.7 %collective-permute-done.47 = bf16[512,384]{1,0:T(8,128)(2,1)S(1)} collective-permute-done((bf16[512,384]{1,0:T(8,128)(2,1)S(1)}, bf16[512,384]{1,0:T(8,128)(2,1)S(1)}, u32[]{:S(2)}, u32[]{:S(2)}) %collective-permute-start.47) | collective-permute-done | bytes 393248 | tf_op jit(solution)/shard_map/ppermute | solution.py:1168
  522.6 4.5 finish.1
  (225 shorter events, 105.4 us)
Async XLA Ops:
  4.2 22.9 %collective-permute-start.1 = (bf16[1152,384]{1,0:T(8,128)(2,1)}, bf16[1152,384]{1,0:T(8,128)(2,1)S(1)}, u32[]{:S(2)}, u32[]{:S(2)}) collective-permute-start(bf16[1152,384]{1,0:T(8,128)(2,1)} %pack_in.1), channel_id=1, source_target_pairs={{0,2},{1,3},{2,0},{3,1},{4,6},{5,7},{6,4},{7,5},{8,10},{9,11},{10,... | collective-permute-start | bytes 2654216 | tf_op jit(solution)/shard_map/ppermute | solution.py:1168
  7.3 21.3 %collective-permute-start = (bf16[1152,384]{1,0:T(8,128)(2,1)}, bf16[1152,384]{1,0:T(8,128)(2,1)S(1)}, u32[]{:S(2)}, u32[]{:S(2)}) collective-permute-start(bf16[1152,384]{1,0:T(8,128)(2,1)} %pack_in.1), channel_id=1, source_target_pairs={{0,1},{1,0},{2,3},{3,2},{4,5},{5,4},{6,7},{7,6},{8,9},{9,8},{10,11... | collective-permute-start | bytes 2654216 | tf_op jit(solution)/shard_map/ppermute | solution.py:1168
  28.6 42.2 %collective-permute-start.4 = (bf16[2416,384]{1,0:T(8,128)(2,1)}, bf16[2416,384]{1,0:T(8,128)(2,1)}, u32[]{:S(2)}, u32[]{:S(2)}) collective-permute-start(bf16[2416,384]{1,0:T(8,128)(2,1)} %get-tuple-element.134), channel_id=1, source_target_pairs={{0,3},{1,2},{2,1},{3,0},{4,7},{5,6},{6,5},{7,4},{8,11},{9,10},{10,... | collective-permute-start | bytes 5566472 | tf_op jit(solution)/shard_map/ppermute | solution.py:1168
  30.0 22.7 %collective-permute-start.10 = (bf16[1152,384]{1,0:T(8,128)(2,1)S(1)}, bf16[1152,384]{1,0:T(8,128)(2,1)}, u32[]{:S(2)}, u32[]{:S(2)}) collective-permute-start(bf16[1152,384]{1,0:T(8,128)(2,1)S(1)} %collective-permute-done.1.refs_24_.refs_22_), channel_id=1, source_target_pairs={{0,8},{4,12},{8,0},{12,4},{16,24},{20,28},{24,16},{28,20},{1,9},{5... | collective-permute-start | bytes 2654216 | tf_op jit(solution)/shard_map/ppermute | solution.py:1168
  31.6 37.6 %collective-permute-start.7 = (bf16[1152,384]{1,0:T(8,128)(2,1)S(1)}, bf16[1152,384]{1,0:T(8,128)(2,1)}, u32[]{:S(2)}, u32[]{:S(2)}) collective-permute-start(bf16[1152,384]{1,0:T(8,128)(2,1)S(1)} %collective-permute-done.refs_20_.refs_18_), channel_id=1, source_target_pairs={{0,8},{4,12},{8,0},{12,4},{16,24},{20,28},{24,16},{28,20},{1,9},{5... | collective-permute-start | bytes 2654216 | tf_op jit(solution)/shard_map/ppermute | solution.py:1168
  32.0 37.1 %collective-permute-start.9 = (bf16[1152,384]{1,0:T(8,128)(2,1)S(1)}, bf16[1152,384]{1,0:T(8,128)(2,1)S(1)}, u32[]{:S(2)}, u32[]{:S(2)}) collective-permute-start(bf16[1152,384]{1,0:T(8,128)(2,1)S(1)} %collective-permute-done.1.refs_24_.refs_22_), channel_id=1, source_target_pairs={{0,4},{4,0},{8,12},{12,8},{16,20},{20,16},{24,28},{28,24},{1,5},{5... | collective-permute-start | bytes 2654216 | tf_op jit(solution)/shard_map/ppermute | solution.py:1168
  32.0 46.7 %collective-permute-start.6 = (bf16[1152,384]{1,0:T(8,128)(2,1)S(1)}, bf16[1152,384]{1,0:T(8,128)(2,1)}, u32[]{:S(2)}, u32[]{:S(2)}) collective-permute-start(bf16[1152,384]{1,0:T(8,128)(2,1)S(1)} %collective-permute-done.refs_20_.refs_18_), channel_id=1, source_target_pairs={{0,4},{4,0},{8,12},{12,8},{16,20},{20,16},{24,28},{28,24},{1,5},{5... | collective-permute-start | bytes 2654216 | tf_op jit(solution)/shard_map/ppermute | solution.py:1168
  52.7 26.1 %collective-permute-start.11 = (bf16[1152,384]{1,0:T(8,128)(2,1)}, bf16[1152,384]{1,0:T(8,128)(2,1)}, u32[]{:S(2)}, u32[]{:S(2)}) collective-permute-start(bf16[1152,384]{1,0:T(8,128)(2,1)} %collective-permute-done.10.refs_26_.refs_24_), channel_id=1, source_target_pairs={{0,4},{4,0},{8,12},{12,8},{16,20},{20,16},{24,28},{28,24},{1,5},{5... | collective-permute-start | bytes 2654216 | tf_op jit(solution)/shard_map/ppermute | solution.py:1168
  70.1 36.3 %collective-permute-start.2 = (bf16[2000,384]{1,0:T(8,128)(2,1)}, bf16[2000,384]{1,0:T(8,128)(2,1)}, u32[]{:S(2)}, u32[]{:S(2)}) collective-permute-start(bf16[2000,384]{1,0:T(8,128)(2,1)} %get-tuple-element.131), channel_id=1, source_target_pairs={{0,1},{1,0},{2,3},{3,2},{4,5},{5,4},{6,7},{7,6},{8,9},{9,8},{10,11... | collective-permute-start | bytes 4608008 | tf_op jit(solution)/shard_map/ppermute | solution.py:1168
  70.8 35.9 %collective-permute-start.3 = (bf16[2000,384]{1,0:T(8,128)(2,1)}, bf16[2000,384]{1,0:T(8,128)(2,1)}, u32[]{:S(2)}, u32[]{:S(2)}) collective-permute-start(bf16[2000,384]{1,0:T(8,128)(2,1)} %get-tuple-element.132), channel_id=1, source_target_pairs={{0,2},{1,3},{2,0},{3,1},{4,6},{5,7},{6,4},{7,5},{8,10},{9,11},{10,... | collective-permute-start | bytes 4608008 | tf_op jit(solution)/shard_map/ppermute | solution.py:1168
  78.8 33.9 %collective-permute-start.13 = (bf16[1904,384]{1,0:T(8,128)(2,1)S(1)}, bf16[1904,384]{1,0:T(8,128)(2,1)S(1)}, u32[]{:S(2)}, u32[]{:S(2)}) collective-permute-start(bf16[1904,384]{1,0:T(8,128)(2,1)S(1)} %slice.137.refs_28_.refs_32_.refs_22_.refs_26_), channel_id=1, source_target_pairs={{0,8},{4,12},{8,0},{12,4},{16,24},{20,28},{24,16},{28,20},{1,9},{5... | collective-permute-start | bytes 4386824 | tf_op jit(solution)/shard_map/ppermute | solution.py:1168
  121.5 38.8 %collective-permute-start.20 = (bf16[2,512,384]{2,1,0:T(8,128)(2,1)}, bf16[2,512,384]{2,1,0:T(8,128)(2,1)S(1)}, u32[]{:S(2)}, u32[]{:S(2)}) collective-permute-start(bf16[2,512,384]{2,1,0:T(8,128)(2,1)} %get-tuple-element.146), channel_id=1, source_target_pairs={{0,3},{1,2},{2,1},{3,0},{4,7},{5,6},{6,5},{7,4},{8,11},{9,10},{10,... | collective-permute-start | bytes 2359304 | tf_op jit(solution)/shard_map/ppermute | solution.py:1168
  123.2 37.2 %collective-permute-start.18 = (bf16[2,512,384]{2,1,0:T(8,128)(2,1)}, bf16[2,512,384]{2,1,0:T(8,128)(2,1)}, u32[]{:S(2)}, u32[]{:S(2)}) collective-permute-start(bf16[2,512,384]{2,1,0:T(8,128)(2,1)} %get-tuple-element.146), channel_id=1, source_target_pairs={{0,2},{1,3},{2,0},{3,1},{4,6},{5,7},{6,4},{7,5},{8,10},{9,11},{10,... | collective-permute-start | bytes 2359304 | tf_op jit(solution)/shard_map/ppermute | solution.py:1168
  124.6 34.5 %collective-permute-start.19 = (bf16[2,512,384]{2,1,0:T(8,128)(2,1)}, bf16[2,512,384]{2,1,0:T(8,128)(2,1)}, u32[]{:S(2)}, u32[]{:S(2)}) collective-permute-start(bf16[2,512,384]{2,1,0:T(8,128)(2,1)} %get-tuple-element.145.rows_mine), channel_id=1, source_target_pairs={{0,1},{1,0},{2,3},{3,2},{4,5},{5,4},{6,7},{7,6},{8,9},{9,8},{10,11... | collective-permute-start | bytes 2359304 | tf_op jit(solution)/shard_map/ppermute | solution.py:1168
  125.1 76.2 %collective-permute-start.25 = (bf16[3,160,1664]{2,1,0:T(8,128)(2,1)}, bf16[3,160,1664]{2,1,0:T(8,128)(2,1)}, u32[]{:S(2)}, u32[]{:S(2)}) collective-permute-start(bf16[3,160,1664]{2,1,0:T(8,128)(2,1)} %get-tuple-element.158), channel_id=1, source_target_pairs={{0,2},{1,3},{2,0},{3,1},{4,6},{5,7},{6,4},{7,5},{8,10},{9,11},{10,... | collective-permute-start | bytes 4792328 | tf_op jit(solution)/shard_map/ppermute | solution.py:1168
  157.2 42.3 %collective-permute-start.17 = (bf16[512,1536]{1,0:T(8,128)(2,1)}, bf16[512,1536]{1,0:T(8,128)(2,1)S(1)}, u32[]{:S(2)}, u32[]{:S(2)}) collective-permute-start(bf16[512,1536]{1,0:T(8,128)(2,1)} %get-tuple-element.140.refs_0_.refs_1_.refs_5_), channel_id=1, source_target_pairs={{0,1},{1,0},{2,3},{3,2},{4,5},{5,4},{6,7},{7,6},{8,9},{9,8},{10,11... | collective-permute-start | bytes 4718600 | tf_op jit(solution)/shard_map/ppermute | solution.py:1168
  159.0 79.5 %collective-permute-start.23 = (bf16[3,144,1664]{2,1,0:T(8,128)(2,1)}, bf16[3,144,1664]{2,1,0:T(8,128)(2,1)}, u32[]{:S(2)}, u32[]{:S(2)}) collective-permute-start(bf16[3,144,1664]{2,1,0:T(8,128)(2,1)} %get-tuple-element.156), channel_id=1, source_target_pairs={{0,2},{1,3},{2,0},{3,1},{4,6},{5,7},{6,4},{7,5},{8,10},{9,11},{10,... | collective-permute-start | bytes 4313096 | tf_op jit(solution)/shard_map/ppermute | solution.py:1168
  201.3 37.2 %collective-permute-start.26 = (bf16[3,160,1664]{2,1,0:T(8,128)(2,1)}, bf16[3,160,1664]{2,1,0:T(8,128)(2,1)S(1)}, u32[]{:S(2)}, u32[]{:S(2)}) collective-permute-start(bf16[3,160,1664]{2,1,0:T(8,128)(2,1)} %collective-permute-done.25.refs_5_), channel_id=1, source_target_pairs={{0,8},{4,12},{8,0},{12,4},{16,24},{20,28},{24,16},{28,20},{1,9},{5... | collective-permute-start | bytes 4792328 | tf_op jit(solution)/shard_map/ppermute | solution.py:1168
  238.6 34.2 %collective-permute-start.24 = (bf16[3,144,1664]{2,1,0:T(8,128)(2,1)}, bf16[3,144,1664]{2,1,0:T(8,128)(2,1)}, u32[]{:S(2)}, u32[]{:S(2)}) collective-permute-start(bf16[3,144,1664]{2,1,0:T(8,128)(2,1)} %collective-permute-done.23.refs_5_), channel_id=1, source_target_pairs={{0,8},{4,12},{8,0},{12,4},{16,24},{20,28},{24,16},{28,20},{1,9},{5... | collective-permute-start | bytes 4313096 | tf_op jit(solution)/shard_map/ppermute | solution.py:1168
  240.2 33.1 %collective-permute-start.21 = (bf16[3,128,1664]{2,1,0:T(8,128)(2,1)S(1)}, bf16[3,128,1664]{2,1,0:T(8,128)(2,1)}, u32[]{:S(2)}, u32[]{:S(2)}) collective-permute-start(bf16[3,128,1664]{2,1,0:T(8,128)(2,1)S(1)} %copy-done.31), channel_id=1, source_target_pairs={{0,2},{1,3},{2,0},{3,1},{4,6},{5,7},{6,4},{7,5},{8,10},{9,11},{10,... | collective-permute-start | bytes 3833864 | tf_op jit(solution)/shard_map/ppermute | solution.py:1168
  273.3 30.2 %collective-permute-start.22 = (bf16[3,128,1664]{2,1,0:T(8,128)(2,1)}, bf16[3,128,1664]{2,1,0:T(8,128)(2,1)S(1)}, u32[]{:S(2)}, u32[]{:S(2)}) collective-permute-start(bf16[3,128,1664]{2,1,0:T(8,128)(2,1)} %collective-permute-done.21.refs_5_), channel_id=1, source_target_pairs={{0,8},{4,12},{8,0},{12,4},{16,24},{20,28},{24,16},{28,20},{1,9},{5... | collective-permute-start | bytes 3833864 | tf_op jit(solution)/shard_map/ppermute | solution.py:1168
  322.9 47.1 %collective-permute-start.33 = (bf16[512,1792]{1,0:T(8,128)(2,1)}, bf16[512,1792]{1,0:T(8,128)(2,1)S(1)}, u32[]{:S(2)}, u32[]{:S(2)}) collective-permute-start(bf16[512,1792]{1,0:T(8,128)(2,1)} %get-tuple-element.174), channel_id=1, source_target_pairs={{0,1},{1,0},{2,3},{3,2},{4,5},{5,4},{6,7},{7,6},{8,9},{9,8},{10,11... | collective-permute-start | bytes 5505032 | tf_op jit(solution)/shard_map/ppermute | solution.py:1168
  397.0 41.5 %collective-permute-start.38 = (bf16[4,512,384]{2,1,0:T(8,128)(2,1)}, bf16[4,512,384]{2,1,0:T(8,128)(2,1)S(1)}, u32[]{:S(2)}, u32[]{:S(2)}) collective-permute-start(bf16[4,512,384]{2,1,0:T(8,128)(2,1)} %get-tuple-element.195), channel_id=1, source_target_pairs={{0,1},{1,0},{2,3},{3,2},{4,5},{5,4},{6,7},{7,6},{8,9},{9,8},{10,11... | collective-permute-start | bytes 4718600 | tf_op jit(solution)/shard_map/ppermute | solution.py:1168
  407.3 38.7 %collective-permute-start.36 = (bf16[1120,384]{1,0:T(8,128)(2,1)S(1)}, bf16[1120,384]{1,0:T(8,128)(2,1)S(1)}, u32[]{:S(2)}, u32[]{:S(2)}) collective-permute-start(bf16[1120,384]{1,0:T(8,128)(2,1)S(1)} %slice.143), channel_id=1, source_target_pairs={{0,2},{1,3},{2,0},{3,1},{4,6},{5,7},{6,4},{7,5},{8,10},{9,11},{10,... | collective-permute-start | bytes 2580488 | tf_op jit(solution)/shard_map/ppermute | solution.py:1168
  408.1 34.2 %collective-permute-start.37 = (bf16[256,384]{1,0:T(8,128)(2,1)S(1)}, bf16[256,384]{1,0:T(8,128)(2,1)S(1)}, u32[]{:S(2)}, u32[]{:S(2)}) collective-permute-start(bf16[256,384]{1,0:T(8,128)(2,1)S(1)} %get-tuple-element.230), channel_id=1, source_target_pairs={{0,3},{1,2},{2,1},{3,0},{4,7},{5,6},{6,5},{7,4},{8,11},{9,10},{10,... | collective-permute-start | bytes 589832 | tf_op jit(solution)/shard_map/ppermute | solution.py:1168
  409.5 36.5 %collective-permute-start.35 = (bf16[256,384]{1,0:T(8,128)(2,1)S(1)}, bf16[256,384]{1,0:T(8,128)(2,1)S(1)}, u32[]{:S(2)}, u32[]{:S(2)}) collective-permute-start(bf16[256,384]{1,0:T(8,128)(2,1)S(1)} %get-tuple-element.231), channel_id=1, source_target_pairs={{0,1},{1,0},{2,3},{3,2},{4,5},{5,4},{6,7},{7,6},{8,9},{9,8},{10,11... | collective-permute-start | bytes 589832 | tf_op jit(solution)/shard_map/ppermute | solution.py:1168
  452.7 43.3 %collective-permute-start.41 = (bf16[2,512,384]{2,1,0:T(8,128)(2,1)}, bf16[2,512,384]{2,1,0:T(8,128)(2,1)}, u32[]{:S(2)}, u32[]{:S(2)}) collective-permute-start(bf16[2,512,384]{2,1,0:T(8,128)(2,1)} %get-tuple-element.211), channel_id=1, source_target_pairs={{0,2},{1,3},{2,0},{3,1},{4,6},{5,7},{6,4},{7,5},{8,10},{9,11},{10,... | collective-permute-start | bytes 2359304 | tf_op jit(solution)/shard_map/ppermute | solution.py:1168
  464.7 18.4 %collective-permute-start.45 = (bf16[320,384]{1,0:T(8,128)(2,1)S(1)}, bf16[320,384]{1,0:T(8,128)(2,1)S(1)}, u32[]{:S(2)}, u32[]{:S(2)}) collective-permute-start(bf16[320,384]{1,0:T(8,128)(2,1)S(1)} %get-tuple-element.243), channel_id=1, source_target_pairs={{0,2},{1,3},{2,0},{3,1},{4,6},{5,7},{6,4},{7,5},{8,10},{9,11},{10,... | collective-permute-start | bytes 737288 | tf_op jit(solution)/shard_map/ppermute | solution.py:1168
  466.0 17.1 %collective-permute-start.44 = (bf16[320,384]{1,0:T(8,128)(2,1)S(1)}, bf16[320,384]{1,0:T(8,128)(2,1)S(1)}, u32[]{:S(2)}, u32[]{:S(2)}) collective-permute-start(bf16[320,384]{1,0:T(8,128)(2,1)S(1)} %get-tuple-element.244), channel_id=1, source_target_pairs={{0,1},{1,0},{2,3},{3,2},{4,5},{5,4},{6,7},{7,6},{8,9},{9,8},{10,11... | collective-permute-start | bytes 737288 | tf_op jit(solution)/shard_map/ppermute | solution.py:1168
  484.7 17.5 %collective-permute-start.54 = (bf16[320,384]{1,0:T(8,128)(2,1)S(1)}, bf16[320,384]{1,0:T(8,128)(2,1)S(1)}, u32[]{:S(2)}, u32[]{:S(2)}) collective-permute-start(bf16[320,384]{1,0:T(8,128)(2,1)S(1)} %add_convert_fusion.6), channel_id=1, source_target_pairs={{0,8},{4,12},{8,0},{12,4},{16,24},{20,28},{24,16},{28,20},{1,9},{5... | collective-permute-start | bytes 737288 | tf_op jit(solution)/shard_map/ppermute | solution.py:1168
  499.2 19.1 %collective-permute-start.47 = (bf16[512,384]{1,0:T(8,128)(2,1)S(1)}, bf16[512,384]{1,0:T(8,128)(2,1)S(1)}, u32[]{:S(2)}, u32[]{:S(2)}) collective-permute-start(bf16[512,384]{1,0:T(8,128)(2,1)S(1)} %get-tuple-element.217), channel_id=1, source_target_pairs={{0,2},{1,3},{2,0},{3,1},{4,6},{5,7},{6,4},{7,5},{8,10},{9,11},{10,... | collective-permute-start | bytes 1179656 | tf_op jit(solution)/shard_map/ppermute | solution.py:1168
  499.9 18.4 %collective-permute-start.48 = (bf16[512,384]{1,0:T(8,128)(2,1)S(1)}, bf16[512,384]{1,0:T(8,128)(2,1)S(1)}, u32[]{:S(2)}, u32[]{:S(2)}) collective-permute-start(bf16[512,384]{1,0:T(8,128)(2,1)S(1)} %get-tuple-element.218), channel_id=1, source_target_pairs={{0,3},{1,2},{2,1},{3,0},{4,7},{5,6},{6,5},{7,4},{8,11},{9,10},{10,... | collective-permute-start | bytes 1179656 | tf_op jit(solution)/shard_map/ppermute | solution.py:1168
  (60 other events, 680.2 us)
